TPU v7x, 32 devices: a whole 2x2x4 slice. The times are simulated.
32 devices in a mesh: dp: 4 (over x, core), seq: 8 (over z, y).
Axes of the slice: x: 2, y: 2, z: 4, core: 2. Of those that a mesh axis runs over, the one named last changes fastest.
Arguments:
- byte_ids: int32 [16, 4096], P('dp', 'seq'), may hold values from 0 to 255
- item_lengths: int32 [16], P('dp'), may hold values from 2048 to 4096, as said below
- block_counts: int32 [16], P('dp'), may hold values from 32 to 64, as said below
- byte_embed: bfloat16 [256, 512], replicated, may hold values from -6 to 6
- norm1_gain: float32 [512], replicated, may hold values from 0.25 to 1.75
- norm1_shift: float32 [512], replicated, may hold values from -4 to 4
- qkv_weight: bfloat16 [512, 1536], replicated, may hold values from -0.25 to 0.25
- out_weight: bfloat16 [512, 512], replicated, may hold values from -0.75 to 0.75
- norm2_gain: float32 [512], replicated, may hold values from 0.25 to 1.75
- norm2_shift: float32 [512], replicated, may hold values from -4 to 4
- up_weight: bfloat16 [512, 2048], replicated, may hold values from -0.25 to 0.25
- up_bias: float32 [2048], replicated, may hold values from -6 to 6
- down_weight: bfloat16 [2048, 512], replicated, may hold values from -0.125 to 0.125
- down_bias: float32 [512], replicated, may hold values from -4 to 4
- frontier_weight: float32 [512], replicated, may hold values from -0.25 to 0.25
- pooled_cot: float32 [16, 64, 512], P('dp'), may hold values from -6 to 6
Outputs:
- pooled: float32 [16, 64, 512], P('dp')
- embed_grad: float32 [256, 512], replicated
- norm1_gain_grad: float32 [512], replicated
- norm1_shift_grad: float32 [512], replicated
- qkv_grad: float32 [512, 1536], replicated
- out_grad: float32 [512, 512], replicated
- norm2_gain_grad: float32 [512], replicated
- norm2_shift_grad: float32 [512], replicated
- up_grad: float32 [512, 2048], replicated
- up_bias_grad: float32 [2048], replicated
- down_grad: float32 [2048, 512], replicated
- down_bias_grad: float32 [512], replicated
- frontier_grad: float32 [512], replicated
Inputs may be any that keep to these rules, and one draw needn't show every extreme that they name: `item_lengths`: slots at or after an item's length are padding. Among the 4 items of each index of dp, one fills all 4096 slots. `block_counts`: some item has 64 blocks.
All inputs are finite; a program needn't handle non-finite values.
Results may differ from a plain program's by a relative error of at most 0.012.
The roundings to bfloat16 on the way count: a program that leaves them out, or rounds other values in their place, can miss the bound.
Values may be sent and summed in bfloat16 or wider, within the bound.
No kernel may reach another device: no remote copies, remote signals or barrier semaphores. Data moves between devices by JAX's collectives and lax.ppermute only.
A program may use at most 192 MiB of HBM per device.

v0:
```python
import jax
import jax.numpy as jnp
from jax import lax
from jax.sharding import PartitionSpec as P

H = 8
HD = 64
WIN = 64
NB = 64


HIGH = lax.Precision.HIGHEST
eps = 1e-05
spread = 2.0


def padded(cells, sides, width):
    for axis, dim in sides:
        count = lax.axis_size(axis)
        ends = count - 1
        head = lax.slice_in_dim(cells, 0, width, axis=dim)
        tail = lax.slice_in_dim(cells, cells.shape[dim] - width, cells.shape[dim], axis=dim)
        cells = jnp.concatenate(
            [
                lax.ppermute(tail, axis, [(i, (i + 1) % count) for i in range(ends)]),
                cells,
                lax.ppermute(head, axis, [((i + 1) % count, i) for i in range(ends)]),
            ],
            axis=dim,
        )
    return cells


def carried_in(shard, axis, combine, identity, reverse):
    count, here = (lax.axis_size(axis), lax.axis_index(axis))
    everything = lax.all_gather(shard, axis)
    start = jnp.broadcast_to(jnp.asarray(identity, shard.dtype), shard.shape)

    def step(k, before):
        at = count - 1 - k if reverse else k
        reached = at > here if reverse else at < here
        new = combine(before, everything[at])
        return jnp.where(reached, new, before)

    return lax.fori_loop(0, count, step, start)


def from_behind(shard, axis, by):
    count = lax.axis_size(axis)
    pairs = [(i, i + by) for i in range(count) if 0 <= i + by < count]
    return lax.ppermute(shard, axis, pairs)


def layer_norm(inputs, norm_gain, norm_shift):
    center = jnp.mean(inputs, -1, keepdims=True)
    centered = inputs - center
    variance = jnp.mean(centered * centered, -1, keepdims=True)
    return centered * lax.rsqrt(variance + eps) * norm_gain + norm_shift


def exact_gelu(inputs):
    return jax.nn.gelu(inputs, approximate=False)


def add_terms(earlier, later):
    return earlier + later


def cross_rows(left_rows, right_rows):
    return lax.dot_general(
        left_rows, right_rows, (((0,), (0,)), ((), ())), preferred_element_type=jnp.float32
    )


def back_rows(grad_rows, weight):
    return lax.dot_general(
        grad_rows, weight, (((1,), (1,)), ((), ())), preferred_element_type=jnp.float32
    )


def local(
    byte_ids,
    item_lengths,
    block_counts,
    byte_embed,
    norm1_gain,
    norm1_shift,
    qkv_weight,
    out_weight,
    norm2_gain,
    norm2_shift,
    up_weight,
    up_bias,
    down_weight,
    down_bias,
    frontier_weight,
    pooled_cot,
):
    row_count, span = byte_ids.shape
    vocab_size, model_width = byte_embed.shape
    seq_count = lax.axis_size("seq")
    seq_place = lax.axis_index("seq")
    offset = seq_place * span
    seq_total = span * seq_count
    score_scale = HD ** (-0.5)
    ext_len = span + 2 * WIN
    tile_rows = min(128, span)
    tile_count = span // tile_rows
    window_len = tile_rows + 2 * WIN
    one_hot = (byte_ids.reshape(-1)[:, None] == jnp.arange(vocab_size)[None, :]).astype(
        jnp.bfloat16
    )
    embedded = jnp.dot(one_hot, byte_embed, preferred_element_type=jnp.float32)
    normed_one, norm_one_back = jax.vjp(layer_norm, embedded, norm1_gain, norm1_shift)
    normed_one_low = normed_one.astype(jnp.bfloat16)
    qkv_low = jnp.dot(normed_one_low, qkv_weight, preferred_element_type=jnp.float32).astype(
        jnp.bfloat16
    )
    queries = qkv_low[:, :model_width].reshape(row_count, span, H, HD)
    kv_local = qkv_low[:, model_width:].reshape(row_count, span, 2 * model_width)
    kv_ext = padded(kv_local, (("seq", 1),), WIN)
    keys_ext = kv_ext[:, :, :model_width].reshape(row_count, ext_len, H, HD)
    values_ext = kv_ext[:, :, model_width:].reshape(row_count, ext_len, H, HD)
    query_at = offset + jnp.arange(span)
    key_at = offset - WIN + jnp.arange(ext_len)
    allowed = (
        (jnp.abs(query_at[:, None] - key_at[None, :]) <= WIN)
        & (key_at >= 0)[None, :]
        & (key_at < seq_total)[None, :]
    )
    allowed_tiles = jnp.stack(
        [
            allowed[
                index * tile_rows : (index + 1) * tile_rows,
                index * tile_rows : index * tile_rows + window_len,
            ]
            for index in range(tile_count)
        ]
    )

    def windows_of(ext_rows):
        return jnp.stack(
            [
                ext_rows[index * tile_rows : index * tile_rows + window_len]
                for index in range(tile_count)
            ]
        )

    def score_block(query_tiles, key_tiles):
        raw_scores = (
            jnp.einsum(
                "tqhd,tkhd->thqk", query_tiles, key_tiles, preferred_element_type=jnp.float32
            )
            * score_scale
        )
        return jnp.where(allowed_tiles[:, None], raw_scores, -1e30)

    def attend_row(row_data):
        query_rows, key_rows, value_rows = row_data
        query_tiles = query_rows.reshape(tile_count, tile_rows, H, HD)
        key_tiles = windows_of(key_rows)
        value_tiles = windows_of(value_rows)
        scores = score_block(query_tiles, key_tiles)
        row_peak = jnp.max(scores, -1, keepdims=True)
        weights = jnp.exp(scores - row_peak)
        weight_sum = jnp.sum(weights, -1, keepdims=True)
        soft_probs = weights / weight_sum
        attended_rows = jnp.einsum(
            "thqk,tkhd->tqhd",
            soft_probs.astype(jnp.bfloat16),
            value_tiles,
            preferred_element_type=jnp.float32,
        )
        return (
            attended_rows.reshape(span, H, HD).astype(jnp.bfloat16),
            row_peak + jnp.log(weight_sum),
        )

    attended, log_total = lax.map(attend_row, (queries, keys_ext, values_ext))
    attended_flat = attended.reshape(row_count * span, model_width)
    middle = embedded + jnp.dot(attended_flat, out_weight, preferred_element_type=jnp.float32)
    normed_two, norm_two_back = jax.vjp(layer_norm, middle, norm2_gain, norm2_shift)
    normed_two_low = normed_two.astype(jnp.bfloat16)
    preact = jnp.dot(normed_two_low, up_weight, preferred_element_type=jnp.float32) + up_bias
    activated, gelu_back = jax.vjp(exact_gelu, preact)
    activated_low = activated.astype(jnp.bfloat16)
    hidden_flat = (
        middle + jnp.dot(activated_low, down_weight, preferred_element_type=jnp.float32) + down_bias
    )
    hidden = hidden_flat.reshape(row_count, span, model_width)
    frontier = jax.nn.sigmoid(jnp.dot(hidden_flat, frontier_weight, precision=HIGH)).reshape(
        row_count, span
    )
    in_item = (query_at[None, :] < item_lengths[:, None]).astype(jnp.float32)
    prob_rows = frontier * in_item
    local_cum = jnp.cumsum(prob_rows, 1)
    local_mass = local_cum[:, -1]
    mass_before = carried_in(local_mass, "seq", add_terms, jnp.zeros_like(local_mass), False)
    item_total = lax.psum(local_mass, "seq")
    counts_real = block_counts.astype(jnp.float32)
    cumulative = local_cum + mass_before[:, None]
    position = counts_real[:, None] * cumulative / item_total[:, None]
    centers = jnp.arange(NB).astype(jnp.float32) + 0.5
    in_block = (jnp.arange(NB)[None, :] < block_counts[:, None]).astype(jnp.float32)
    distance = position[:, :, None] - centers[None, None, :]
    assign = jnp.exp(-spread * distance * distance) * in_item[:, :, None] * in_block[:, None, :]
    numer_term = jnp.einsum("rck,rcd->rkd", assign, hidden, precision=HIGH)
    denom_term = jnp.sum(assign, 1)
    numer_whole, denom_whole = lax.psum((numer_term, denom_term), "seq")
    inverse_whole = 1.0 / (denom_whole + 1.0)
    pooled = numer_whole * inverse_whole[:, :, None]
    d_numer = pooled_cot * inverse_whole[:, :, None]
    d_denom = -jnp.sum(pooled_cot * pooled, -1) * inverse_whole
    d_assign = jnp.einsum("rkd,rcd->rck", d_numer, hidden, precision=HIGH) + d_denom[:, None, :]
    d_hidden_pool = jnp.einsum("rck,rkd->rcd", assign, d_numer, precision=HIGH)
    d_position = jnp.sum(d_assign * assign * (-2.0 * spread) * distance, -1)
    d_cumulative = d_position * counts_real[:, None] / item_total[:, None]
    total_term = -jnp.sum(d_position * position, 1) / item_total
    local_suffix = jnp.flip(jnp.cumsum(jnp.flip(d_cumulative, 1), 1), 1)
    local_push = local_suffix[:, 0]
    push_after = carried_in(local_push, "seq", add_terms, jnp.zeros_like(local_push), True)
    d_item_total = lax.psum(total_term, "seq")
    d_prob = local_suffix + push_after[:, None] + d_item_total[:, None]
    d_logit = (d_prob * in_item * frontier * (1.0 - frontier)).reshape(-1)
    d_hidden = (
        d_hidden_pool.reshape(row_count * span, model_width)
        + d_logit[:, None] * frontier_weight[None, :]
    )
    d_frontier = jnp.dot(d_logit, hidden_flat, precision=HIGH)
    d_hidden_low = d_hidden.astype(jnp.bfloat16)
    d_down = cross_rows(activated_low, d_hidden_low)
    d_down_bias = jnp.sum(d_hidden_low.astype(jnp.float32), 0)
    d_activated = back_rows(d_hidden_low, down_weight)
    d_preact_low = gelu_back(d_activated)[0].astype(jnp.bfloat16)
    d_up_bias = jnp.sum(d_preact_low.astype(jnp.float32), 0)
    d_up = cross_rows(normed_two_low, d_preact_low)
    d_normed_two = back_rows(d_preact_low, up_weight)
    d_middle_norm, d_gain_two, d_shift_two = norm_two_back(d_normed_two)
    d_middle = d_hidden + d_middle_norm
    d_middle_low = d_middle.astype(jnp.bfloat16)
    d_out = cross_rows(attended_flat, d_middle_low)
    d_attended = (
        back_rows(d_middle_low, out_weight).astype(jnp.bfloat16).reshape(row_count, span, H, HD)
    )

    def attend_back(row_data):
        query_rows, key_rows, value_rows, row_log, grad_rows = row_data
        query_tiles = query_rows.reshape(tile_count, tile_rows, H, HD)
        grad_tiles = grad_rows.reshape(tile_count, tile_rows, H, HD)
        key_tiles = windows_of(key_rows)
        value_tiles = windows_of(value_rows)
        soft_probs = jnp.exp(score_block(query_tiles, key_tiles) - row_log)
        d_probs = jnp.einsum(
            "tqhd,tkhd->thqk", grad_tiles, value_tiles, preferred_element_type=jnp.float32
        )
        d_values = jnp.einsum(
            "thqk,tqhd->tkhd",
            soft_probs.astype(jnp.bfloat16),
            grad_tiles,
            preferred_element_type=jnp.float32,
        )
        inner = jnp.sum(soft_probs * d_probs, -1, keepdims=True)
        d_scores = (soft_probs * (d_probs - inner)).astype(jnp.bfloat16)
        d_queries = (
            jnp.einsum("thqk,tkhd->tqhd", d_scores, key_tiles, preferred_element_type=jnp.float32)
            * score_scale
        )
        d_keys = (
            jnp.einsum("thqk,tqhd->tkhd", d_scores, query_tiles, preferred_element_type=jnp.float32)
            * score_scale
        )
        kv_tiles = jnp.concatenate(
            (
                d_keys.reshape(tile_count, window_len, model_width),
                d_values.reshape(tile_count, window_len, model_width),
            ),
            -1,
        )
        d_kv_rows = jnp.zeros((ext_len, 2 * model_width), jnp.float32)
        for index in range(tile_count):
            d_kv_rows = d_kv_rows.at[index * tile_rows : index * tile_rows + window_len].add(
                kv_tiles[index]
            )
        return (d_queries.reshape(span, H, HD), d_kv_rows)

    d_queries, d_kv_ext = lax.map(
        attend_back, (queries, keys_ext, values_ext, log_total, d_attended)
    )
    left_rim = d_kv_ext[:, :WIN]
    right_rim = d_kv_ext[:, span + WIN :]
    from_above = from_behind(left_rim.astype(jnp.bfloat16), "seq", -1).astype(left_rim.dtype)
    from_below = from_behind(right_rim.astype(jnp.bfloat16), "seq", 1).astype(right_rim.dtype)
    d_kv = (
        d_kv_ext[:, WIN : span + WIN]
        + jnp.pad(from_above, ((0, 0), (span - WIN, 0), (0, 0)))
        + jnp.pad(from_below, ((0, 0), (0, span - WIN), (0, 0)))
    )
    d_qkv_low = jnp.concatenate(
        (
            d_queries.reshape(row_count * span, model_width),
            d_kv.reshape(row_count * span, 2 * model_width),
        ),
        -1,
    ).astype(jnp.bfloat16)
    d_qkv = cross_rows(normed_one_low, d_qkv_low)
    d_normed_one = back_rows(d_qkv_low, qkv_weight)
    d_input_norm, d_gain_one, d_shift_one = norm_one_back(d_normed_one)
    d_input = d_middle + d_input_norm
    d_embed = lax.dot_general(
        one_hot.astype(jnp.float32),
        d_input,
        (((0,), (0,)), ((), ())),
        precision=HIGH,
        preferred_element_type=jnp.float32,
    )
    (
        d_embed,
        d_gain_one,
        d_shift_one,
        d_qkv,
        d_out,
        d_gain_two,
        d_shift_two,
        d_up,
        d_up_bias,
        d_down,
        d_down_bias,
        d_frontier,
    ) = lax.psum(
        (
            d_embed,
            d_gain_one,
            d_shift_one,
            d_qkv,
            d_out,
            d_gain_two,
            d_shift_two,
            d_up,
            d_up_bias,
            d_down,
            d_down_bias,
            d_frontier,
        ),
        ("dp", "seq"),
    )
    return (
        pooled,
        d_embed,
        d_gain_one,
        d_shift_one,
        d_qkv,
        d_out,
        d_gain_two,
        d_shift_two,
        d_up,
        d_up_bias,
        d_down,
        d_down_bias,
        d_frontier,
    )


def solution(mesh):
    placed = (
        P("dp", "seq"),
        P("dp"),
        P("dp"),
        P(),
        P(),
        P(),
        P(),
        P(),
        P(),
        P(),
        P(),
        P(),
        P(),
        P(),
        P(),
        P("dp", None, None),
    )
    return jax.shard_map(
        local,
        mesh=mesh,
        in_specs=placed,
        out_specs=(P("dp", None, None), P(), P(), P(), P(), P(), P(), P(), P(), P(), P(), P(), P()),
        check_vma=False,
    )
```

profile of v0, /device:TPU:0, one launch (start us, length us, event | category | flops | bytes accessed | tf_op | source)
XLA Modules:
  0.0 810.0 jit_solution(1152127588859389440)
XLA Ops:
  12.1 3.8 convolution_convert_fusion
  21.0 4.9 collective-permute-start
  27.3 3.0 slice.301
  31.5 6.4 reshape.606
  37.8 5.5 copy.43
  48.6 4.7 pad_maximum_fusion.5
  53.4 2.9 fusion.129
  56.2 4.4 copy.40
  60.6 4.4 copy.42
  65.0 51.4 %while.61 = (s32[]{:T(128)}, bf16[4,512,8,64]{1,3,2,0:T(8,128)(2,1)}, f32[4,4,8,128,1]{3,2,1,4,0:T(8,128)}, bf16[4,640,8,64]{1,3,2,0:T(8,128)(2,1)}, pred[4,128,...) while((s32[]{:T(128)}, ...), condition=%wide.region_5.6_spmd, body=%wide.region_2.5_spmd.sunk | while | flops 284422144 | bytes 28837120 | solution.py:179
  65.0 2.8 constant_dynamic-slice_fusion.23
  73.9 2.5 fusion.181
  77.9 2.8 constant_dynamic-slice_fusion.23
  86.7 2.5 fusion.181
  90.8 2.8 constant_dynamic-slice_fusion.23
  103.6 2.8 constant_dynamic-slice_fusion.23
  116.4 3.4 copy.44
  122.9 43.8 %multiply_convert_fusion.1 = (bf16[2048,2048]{1,0:T(8,128)(2,1)S(1)}, f32[2048,2048]{1,0:T(8,128)}, f32[2048,2048]{1,0:T(8,128)}) fusion(f32[2048]{0:T(1024)S(1)} %copy-done.70, bf16[512,2048]{1,0:T(8,128)(2,1)S(1)} %copy-done, f32[2048,512]{1,0:T(8,128)S(1)} %get-tuple-element.615, f32[512]{0:T(512)S(1)} %copy-done.72, f32[512]{0:T(512)S(1)} %copy-done.63, ...), kind=kOutput, calls=%fused_computation.112 | convolution fusion | flops 4577034240 | bytes 48263168 | tf_op jit(solution)/shard_map/dot_general | solution.py:184
  166.8 4.5 add_add_fusion.3
  173.4 3.6 fusion.133
  179.0 21.9 %all-reduce.8 = (f32[4]{0:T(128)S(1)}, f32[32]{0:T(128)S(1)}) all-reduce(f32[4]{0:T(128)S(1)} %bitcast.214, f32[32]{0:T(128)S(1)} %bitcast_dynamic-update-slice_fusion.2), channel_id=1, replica_groups=mesh['dp'=4,'seq'=8] {'seq'}, use_global_device_ids=true, to_apply=%region_12.13 | all-reduce | flops 36 | bytes 288 | tf_op jit(solution)/shard_map/psum | solution.py:199
  201.5 5.8 fusion.96
  207.7 17.3 %psum.114 = f32[4,64]{1,0:T(4,128)S(1)} all-reduce(f32[4,64]{1,0:T(4,128)S(1)} %fusion.95), channel_id=1, replica_groups=mesh['dp'=4,'seq'=8] {'seq'}, use_global_device_ids=true, to_apply=%region_15.16 | all-reduce | flops 256 | bytes 2048 | tf_op jit(solution)/shard_map/psum | solution.py:209
  224.9 52.1 %all-reduce.12.cloned.1.call-done = f32[4,64,512]{2,1,0:T(8,128)} async-done(((f32[4,64,512]{2,1,0:T(8,128)}), f32[4,64,512]{2,1,0:T(8,128)}) %all-reduce.12.cloned.1.call-update) | async-done | bytes 524304 | tf_op jit(solution)/shard_map/psum | solution.py:209
  279.0 6.5 fusion.84
  288.2 19.9 %all-reduce.7 = (f32[4]{0:T(128)S(1)}, f32[32]{0:T(128)S(1)}) all-reduce(f32[4]{0:T(128)S(1)} %negate_divide_fusion, f32[32]{0:T(128)S(1)} %bitcast_dynamic-update-slice_fusion.1), channel_id=1, replica_groups=mesh['dp'=4,'seq'=8] {'seq'}, use_global_device_ids=true, to_apply=%region_23.24 | all-reduce | flops 36 | bytes 288 | tf_op jit(solution)/shard_map/psum | solution.py:222
  308.6 4.6 convert_reduce_fusion.1
  317.1 22.5 %convert_reduce_fusion = (f32[2048]{0:T(1024)}, bf16[2048,2048]{1,0:T(8,128)(2,1)}) fusion(f32[2048,2048]{1,0:T(8,128)} %get-tuple-element.569, bf16[2048,512]{1,0:T(8,128)(2,1)} %fusion.76, bf16[2048,512]{1,0:T(8,128)(2,1)} %param.44, f32[2048,2048]{1,0:T(8,128)} %get-tuple-element.616, f32[2048]{0:T(1024)S(1)} %copy-done.70), kind=kOutput, calls=%fused_computation.110 | convolution fusion | flops 4366268416 | bytes 46153728 | tf_op jit(solution)/shard_map/dot_general | solution.py:76
  339.6 11.3 %multiply_reduce_fusion.1 = (f32[512]{0:T(512)}, f32[2048]{0:T(1024)S(1)}, f32[512]{0:T(512)}, f32[2048,512]{1,0:T(8,128)S(1)}) fusion(f32[2048,512]{1,0:T(8,128)} %copy-done.9, f32[2048]{0:T(1024)S(1)} %fusion.115, f32[2048]{0:T(1024)S(1)} %broadcast_multiply_fusion.1, f32[512]{0:T(512)S(1)} %copy-done.63, bf16[2048,2048]{1,0:T(8,128)(2,1)} %get-tuple-element.620, ...), kind=kOutput, calls=%fused_computation.135 | convolution fusion | flops 4303352832 | bytes 18905088 | tf_op jit(solution)/shard_map/dot_general | solution.py:76
  350.9 7.0 fusion.123
  365.0 3.7 reshape.603
  368.7 5.5 copy.49
  374.2 115.9 %while.62 = (s32[]{:T(128)}, bf16[4,512,8,64]{1,3,2,0:T(8,128)(2,1)}, f32[4,640,1024]{2,1,0:T(8,128)}, bf16[4,640,8,64]{1,3,2,0:T(8,128)(2,1)}, pred[4,128,256]{...) while((s32[]{:T(128)}, ...), condition=%wide.region_28.29_spmd, body=%wide.region_26.28_spmd.sunk | while | flops 694415360 | bytes 134727088 | solution.py:286
  374.2 2.6 constant_dynamic-slice_fusion.26
  378.4 2.7 fusion.188
  382.0 4.3 multiply_reduce_fusion.10
  393.9 3.5 copy.129
  397.4 3.6 constant_dynamic-update-slice_fusion.8
  407.3 2.7 fusion.188
  410.9 4.3 multiply_reduce_fusion.10
  422.9 3.5 copy.129
  426.3 3.6 constant_dynamic-update-slice_fusion.8
  436.3 2.7 fusion.188
  439.9 4.3 multiply_reduce_fusion.10
  451.8 3.5 copy.129
  455.3 3.5 constant_dynamic-update-slice_fusion.8
  465.2 2.7 fusion.188
  468.8 4.3 multiply_reduce_fusion.10
  480.7 3.5 copy.129
  484.2 3.6 constant_dynamic-update-slice_fusion.8
  490.1 5.0 convert.17
  496.4 5.4 collective-permute-start.3
  501.8 9.9 %fusion.134 = f32[2048,512]{1,0:T(8,128)} fusion(bf16[2048,2048]{1,0:T(8,128)(2,1)} %copy-done.77, bf16[2048,512]{1,0:T(8,128)(2,1)S(1)} %copy-done.31), kind=kOutput, calls=%fused_computation.250 | convolution fusion | flops 4294967296 | bytes 14680064 | tf_op jit(solution)/shard_map/dot_general | solution.py:70
  511.7 5.6 copy.56
  517.3 6.6 reshape.604
  523.9 4.4 fusion.85
  528.4 4.2 add_convert_fusion.1
  534.4 4.9 multiply_reduce_fusion.2
  539.3 5.4 fusion.74
  547.0 3.9 fusion.71
  551.5 4.3 fusion.135
  555.9 39.2 %all-reduce.5 = (f32[512]{0:T(512)}, f32[512]{0:T(512)}, f32[512]{0:T(512)}, f32[512]{0:T(512)}, f32[2048]{0:T(1024)}, /*index=5*/f32[512]{0:T(512)}, f32[512]{0:T(512)}) all-reduce(f32[512]{0:T(512)S(1)} %get-tuple-element.494, f32[512]{0:T(512)S(1)} %get-tuple-element.497, ...), channel_id=1, replica_groups=mesh['dp'=4,'seq'=8] {'dp','seq'}, use_global_device_ids=true, to_apply=%region_33.34 | all-reduce | flops 5120 | bytes 40960 | tf_op jit(solution)/shard_map/psum | solution.py:329
  595.1 195.3 %all-reduce.14.cloned.1.call-done = (f32[256,512]{1,0:T(8,128)}, f32[512,1536]{1,0:T(8,128)}, f32[512,512]{1,0:T(8,128)}, f32[512,2048]{1,0:T(8,128)}, f32[2048,512]{1,0:T(8,128)}) async-done(((f32[256,512]{1,0:T(8,128)}, f32[512,1536]{1,0:T(8,128)}, f32[512,512]{1,0:T(8,128)}, f32[512,2048]{1,0:T(8,128)}, f32[2048,512]{1,0:T(8,128)}), (f32[256,512]{1,0:T(8,128)}, f32[512,1536]{1,0:T(8,128)}, ...) | async-done | bytes 13107216 | tf_op jit(solution)/shard_map/psum | solution.py:329
  792.3 3.9 copy.181
  (429 shorter events, 147.2 us)
Async XLA Ops:
  7.2 115.7 %copy-start = (bf16[512,2048]{1,0:T(8,128)(2,1)S(1)}, bf16[512,2048]{1,0:T(8,128)(2,1)}, u32[]{:S(2)}) copy-start(bf16[512,2048]{1,0:T(8,128)(2,1)} %param.42) | copy-start | bytes 6291460
  7.2 269.8 %all-reduce.12.cloned.1.call-start = ((), (), s32[]{:S(2)}) async-start(), calls=%async_computation | async-start | bytes 1048576 | tf_op jit(solution)/shard_map/psum | solution.py:209
  10.0 5.9 copy-start.5
  10.1 5.8 copy-start.45
  21.0 27.6 %collective-permute-start = (bf16[4,64,1024]{2,1,0:T(8,128)(2,1)}, bf16[4,64,1024]{2,1,0:T(8,128)(2,1)S(1)}, u32[]{:S(2)}, u32[]{:S(2)}) collective-permute-start(bf16[4,64,1024]{2,1,0:T(8,128)(2,1)} %get-tuple-element.604), channel_id=1, source_target_pairs={{0,1},{1,2},{2,3},{3,4},{4,5},{5,6},{6,7},{8,9},{9,10},{10,11},{11... | collective-permute-start | bytes 1572872 | tf_op jit(solution)/shard_map/ppermute | solution.py:25
  25.9 22.7 %collective-permute-start.1 = (bf16[4,64,1024]{2,1,0:T(8,128)(2,1)}, bf16[4,64,1024]{2,1,0:T(8,128)(2,1)S(1)}, u32[]{:S(2)}, u32[]{:S(2)}) collective-permute-start(bf16[4,64,1024]{2,1,0:T(8,128)(2,1)} %get-tuple-element.605), channel_id=1, source_target_pairs={{1,0},{2,1},{3,2},{4,3},{5,4},{6,5},{7,6},{9,8},{10,9},{11,10},{12... | collective-permute-start | bytes 1572872 | tf_op jit(solution)/shard_map/ppermute | solution.py:27
  27.3 19.0 %copy-start.48 = (s32[512]{0:T(512)}, s32[512]{0:T(512)S(1)}, u32[]{:S(2)}) copy-start(s32[512]{0:T(512)S(1)} %iota_add_fusion.1) | copy-start | bytes 6148
  37.8 5.5 copy-start.66
  37.8 6.0 copy-start.75
  37.8 8.4 %copy-start.57 = (s32[4]{0:T(128)S(1)}, s32[4]{0:T(128)}, u32[]{:S(2)}) copy-start(s32[4]{0:T(128)} %param.33) | copy-start | bytes 52
  121.9 44.8 %copy-start.9 = (f32[2048,512]{1,0:T(8,128)}, f32[2048,512]{1,0:T(8,128)S(1)}, u32[]{:S(2)}) copy-start(f32[2048,512]{1,0:T(8,128)S(1)} %get-tuple-element.615) | copy-start | bytes 12582916
  122.8 43.9 %copy-start.41 = (f32[2048]{0:T(1024)}, f32[2048]{0:T(1024)S(1)}, u32[]{:S(2)}) copy-start(f32[2048]{0:T(1024)S(1)} %multiply_reduce_fusion.5) | copy-start | bytes 24580
  122.9 43.9 %copy-start.67 = (bf16[2048,512]{1,0:T(8,128)(2,1)S(1)}, bf16[2048,512]{1,0:T(8,128)(2,1)}, u32[]{:S(2)}) copy-start(bf16[2048,512]{1,0:T(8,128)(2,1)} %param.44) | copy-start | bytes 6291460
  122.9 43.9 %copy-start.71 = (f32[512]{0:T(512)S(1)}, f32[512]{0:T(512)}, u32[]{:S(2)}) copy-start(f32[512]{0:T(512)} %param.45) | copy-start | bytes 6148
  166.8 4.6 copy-start.77
  166.8 6.6 copy-start.50
  171.4 5.7 copy-start.55
  171.4 5.7 copy-start.58
  171.4 29.7 %copy-start.53 = (f32[4]{0:T(128)S(1)}, f32[4]{0:T(128)}, u32[]{:S(2)}) copy-start(f32[4]{0:T(128)} %custom-call) | copy-start | bytes 52
  171.4 30.0 %copy-start.62 = (f32[4]{0:T(128)S(1)}, f32[4]{0:T(128)}, u32[]{:S(2)}) copy-start(f32[4]{0:T(128)} %convert_element_type.102) | copy-start | bytes 52
  171.4 30.0 %copy-start.36 = (f32[4,512]{1,0:T(4,128)S(1)}, f32[4,512]{1,0:T(4,128)}, u32[]{:S(2)}) copy-start(f32[4,512]{1,0:T(4,128)} %compare_convert_fusion) | copy-start | bytes 24580
  171.4 30.0 %copy-start.47 = (f32[4,64]{1,0:T(4,128)S(1)}, f32[4,64]{1,0:T(4,128)}, u32[]{:S(2)}) copy-start(f32[4,64]{1,0:T(4,128)} %fusion.118) | copy-start | bytes 3076
  171.5 30.0 %copy-start.59 = (f32[64]{0:T(128)S(1)}, f32[64]{0:T(128)}, u32[]{:S(2)}) copy-start(f32[64]{0:T(128)} %convert_add_fusion) | copy-start | bytes 772
  173.4 103.6 %copy-start.28 = (f32[4,64,512]{2,1,0:T(8,128)S(1)}, f32[4,64,512]{2,1,0:T(8,128)}, u32[]{:S(2)}) copy-start(f32[4,64,512]{2,1,0:T(8,128)} %param.47) | copy-start | bytes 1572868
  207.3 101.3 %copy-start.49 = (s32[512]{0:T(512)S(1)}, s32[512]{0:T(512)}, u32[]{:S(2)}) copy-start(s32[512]{0:T(512)} %copy-done.48) | copy-start | bytes 6148
  207.3 583.0 %all-reduce.14.cloned.1.call-start = ((), (), s32[]{:S(2)}) async-start(), calls=%async_computation.1 | async-start | bytes 26214400 | tf_op jit(solution)/shard_map/psum | solution.py:329
  308.6 4.6 copy-start.37
  339.6 11.3 %copy-start.10 = (f32[2048,512]{1,0:T(8,128)S(1)}, f32[2048,512]{1,0:T(8,128)}, u32[]{:S(2)}) copy-start(f32[2048,512]{1,0:T(8,128)} %copy-done.9) | copy-start | bytes 12582916
  339.6 11.3 %copy-start.76 = (bf16[2048,2048]{1,0:T(8,128)(2,1)S(1)}, bf16[2048,2048]{1,0:T(8,128)(2,1)}, u32[]{:S(2)}) copy-start(bf16[2048,2048]{1,0:T(8,128)(2,1)} %get-tuple-element.620) | copy-start | bytes 25165828
  350.9 7.0 copy-start.42
  368.7 5.5 copy-start.16
  376.8 4.3 copy-start.17
  382.0 4.3 copy-start.2
  393.9 7.0 copy-start.4
  393.9 7.0 copy-start.18
  410.9 4.3 copy-start.2
  422.8 7.0 copy-start.4
  422.9 7.1 copy-start.18
  434.7 4.3 copy-start.17
  439.9 4.3 copy-start.2
  451.8 7.0 copy-start.4
  451.8 7.0 copy-start.18
  468.8 4.3 copy-start.2
  480.7 7.1 copy-start.4
  480.7 7.1 copy-start.18
  490.1 11.7 %copy-start.31 = (bf16[2048,512]{1,0:T(8,128)(2,1)S(1)}, bf16[2048,512]{1,0:T(8,128)(2,1)}, u32[]{:S(2)}) copy-start(bf16[2048,512]{1,0:T(8,128)(2,1)} %fusion.76) | copy-start | bytes 6291460
  495.1 33.3 %collective-permute-start.2 = (bf16[4,64,1024]{2,1,0:T(8,128)(2,1)S(1)}, bf16[4,64,1024]{2,1,0:T(8,128)(2,1)}, u32[]{:S(2)}, u32[]{:S(2)}) collective-permute-start(bf16[4,64,1024]{2,1,0:T(8,128)(2,1)S(1)} %get-tuple-element.600), channel_id=1, source_target_pairs={{1,0},{2,1},{3,2},{4,3},{5,4},{6,5},{7,6},{9,8},{10,9},{11,10},{12... | collective-permute-start | bytes 1572872 | tf_op jit(solution)/shard_map/ppermute | solution.py:51
  496.4 32.0 %collective-permute-start.3 = (bf16[4,64,1024]{2,1,0:T(8,128)(2,1)S(1)}, bf16[4,64,1024]{2,1,0:T(8,128)(2,1)}, u32[]{:S(2)}, u32[]{:S(2)}) collective-permute-start(bf16[4,64,1024]{2,1,0:T(8,128)(2,1)S(1)} %get-tuple-element.601), channel_id=1, source_target_pairs={{0,1},{1,2},{2,3},{3,4},{4,5},{5,6},{6,7},{8,9},{9,10},{10,11},{11... | collective-permute-start | bytes 1572872 | tf_op jit(solution)/shard_map/ppermute | solution.py:51
  517.3 6.6 copy-start.21
  528.3 4.9 copy-start.7
  528.3 5.6 copy-start.32
  528.4 5.6 copy-start.46
  528.4 5.6 copy-start.52
  528.4 5.6 copy-start.65
  528.4 6.1 copy-start.69
  534.4 4.9 copy-start.74
  539.3 5.4 copy-start.40
  550.9 5.0 copy-start.54
  550.9 5.0 copy-start.56
  550.9 5.0 copy-start.60
  550.9 5.0 copy-start.61
  790.3 5.9 copy-start.35
  792.3 4.9 copy-start.30
  797.2 5.7 copy-start.1
  (50 other events, 132.8 us)
Sparse Core Ops, SparseCore 0:
  207.4 69.5 all-reduce.11
  551.0 239.3 all-reduce.13
where the time goes:
time: 816 us; the launch traced here: 810 us
  waiting for transfers between devices  249 us (31%)
  matrix products  211 us (26%)
  local copies, waits for them, and re-layouts  169 us (21%)
  blocking collectives  98.3 us (12%)
  other arithmetic  53 us (6%)
  between operations  15.8 us (2%)
  starting transfers between devices  12.9 us (2%)
    psum x1, waiting for transfers between devices, local(): lax.psum((d_embed, d_gain_one, d_shift_one, d_qkv, d_out, d_gain_two, d_s...  195 us
    psum x1, waiting for transfers between devices, local(): numer_whole, denom_whole = lax.psum((numer_term, denom_term), 'seq')  52.1 us
    dot_general x1, matrix products, local(): jnp.dot(normed_two_low, up_weight, preferred_element_type=jnp.float32)  43.8 us
    dot_general x4, matrix products, back_rows(): lax.dot_general(grad_rows, weight, (((1,), (1,)), ((), ())), preferred_el...  39.9 us
    psum x1, blocking collectives, local(): lax.psum((d_embed, d_gain_one, d_shift_one, d_qkv, d_out, d_gain_two, d_s...  39.2 us
    dynamic_update_slice x12, local copies, waits for them, and re-layouts, local(): lax.map(attend_back, (queries, keys_ext, values_ext, log_total, d_attended))  31.5 us
    unnamed x154, local copies, waits for them, and re-layouts  28.7 us
    dot_general x4, matrix products, cross_rows(): lax.dot_general(left_rows, right_rows, (((0,), (0,)), ((), ())), preferre...  26.8 us
  transfers between devices with their start and end apart: 6, of which 3 were waited for; matrix products, arithmetic and copies ran while one was open for 6% of the time, Pallas kernels for 0%

commit v1 on v0

v1 whole, which is shorter than its diff:
```python
import functools

import jax
import jax.numpy as jnp
from jax import lax
from jax.experimental import pallas as pl
from jax.experimental.pallas import tpu as pltpu
from jax.sharding import PartitionSpec as P

H = 8
HD = 64
WIN = 64
NB = 64
TILE = 128
SPAN_KEYS = TILE + 2 * WIN
PAIR = 2 * HD
STACK = 80

eps = 1e-05
spread = 2.0
LOG2E = 1.4426950408889634
F32 = jnp.float32
BF16 = jnp.bfloat16
VMEM_BYTES = 56 * 1024 * 1024


def dot(left, right):
    return jnp.dot(left, right, preferred_element_type=F32)


def dot_last(left, right):
    return lax.dot_general(left, right, (((1,), (1,)), ((), ())), preferred_element_type=F32)


def dot_first(left, right):
    return lax.dot_general(left, right, (((0,), (0,)), ((), ())), preferred_element_type=F32)


def split_two_outside(value):
    high = lax.reduce_precision(value, 8, 7)
    return high.astype(BF16), (value - high).astype(BF16)


def split_two(value):
    high = value.astype(BF16)
    return high, (value - high.astype(F32)).astype(BF16)


def iota(shape, dim):
    return lax.broadcasted_iota(jnp.int32, shape, dim)


def one_hot_rows(ids_column, vocab):
    cells = iota((ids_column.shape[0], vocab), 1)
    return jnp.where(cells == ids_column, 1.0, 0.0).astype(BF16)


def one_hot_columns(ids_row, vocab):
    cells = iota((vocab, ids_row.shape[1]), 0)
    return jnp.where(cells == ids_row, 1.0, 0.0).astype(BF16)


def gelu_with_slope(value):
    bell = jnp.exp2(value * value * (-0.5 * LOG2E))
    step = 1.0 / (1.0 + jnp.abs(value) * (0.3275911 * 0.7071067811865476))
    series = 0.5 * 1.061405429
    for term in (-1.453152027, 1.421413741, -0.284496736, 0.254829592):
        series = series * step + 0.5 * term
    tail = series * step * bell
    below = jnp.where(value >= 0, 1.0 - tail, tail)
    return value * below, below + value * (bell * 0.3989422804014327)


def window_bias(first, last):
    key_at = iota((SPAN_KEYS, 2 * TILE), 0)
    query_at = iota((SPAN_KEYS, 2 * TILE), 1) & (TILE - 1)
    reach = key_at - query_at
    seen = (reach >= 0) & (reach <= 2 * WIN)
    seen_first = seen & (key_at >= WIN * first)
    seen_last = seen & (key_at < SPAN_KEYS - WIN * last)
    return [jnp.where(kept, 0.0, -1e30) for kept in (seen_first, seen, seen_last)]


def head_blocks(pair_rows):
    lane = iota(pair_rows.shape, 1)
    blank = jnp.zeros_like(pair_rows)
    return jnp.concatenate(
        [jnp.where(lane < HD, pair_rows, blank), jnp.where(lane < HD, blank, pair_rows)], 0
    )


def head_columns(pair_columns):
    return jnp.concatenate([pair_columns[:HD, :TILE], pair_columns[HD:, TILE:]], 0)


def running_sum(row, ones_matrix):
    one, rest = split_two(row)
    high = one.astype(F32) + rest.astype(F32)
    two = (row - high).astype(BF16)
    width = row.shape[1]
    parts = jnp.concatenate([one, rest, two, jnp.zeros((13, width), BF16)], 0)
    sums = dot(parts, ones_matrix)
    return sums[0:1] + sums[1:2] + sums[2:3]


def forward_kernel(
    place, lengths, ids_column, ids_row, table, value_table, embed, out_weight, gain, shift,
    up_weight, up_bias, down_weight, down_bias, cot_stack,
    attended_out, log_out, middle_out, normed_out, act_out, slope_out, high_out, low_out,
    inner_out, frontier_out, running_out,
    bias, query_keys, value_columns, triangle,
):
    item = pl.program_id(0)
    span = middle_out.shape[1]
    model_width = middle_out.shape[2]
    vocab = table.shape[0]
    hidden_width = up_weight.shape[1]

    @pl.when(item == 0)
    def _():
        for at, tile in enumerate(window_bias(place[1], place[2])):
            bias[at] = tile
        triangle[...] = jnp.where(
            iota((span, span), 0) <= iota((span, span), 1), 1.0, 0.0
        ).astype(BF16)

    hot = one_hot_rows(ids_column[0], vocab)
    query_keys[...] = dot(hot, table[...]).astype(BF16)
    value_columns[...] = dot(value_table[...], one_hot_columns(ids_row[0], vocab)).astype(BF16)
    tiles = span // TILE
    for tile in range(tiles):
        begin = tile * TILE
        tile_bias = bias[0 if tile == 0 else (2 if tile == tiles - 1 else 1)]
        for pair in range(H // 2):
            lanes = slice(pair * PAIR, (pair + 1) * PAIR)
            key_lanes = slice(model_width + pair * PAIR, model_width + (pair + 1) * PAIR)
            query_block = head_blocks(query_keys[begin + WIN : begin + WIN + TILE, lanes])
            keys = query_keys[begin : begin + SPAN_KEYS, key_lanes]
            scores = dot_last(keys, query_block) + tile_bias
            peak = jnp.max(scores, 0, keepdims=True)
            weights = jnp.exp(scores - peak)
            weight_sum = jnp.sum(weights, 0, keepdims=True)
            probs = (weights * (1.0 / weight_sum)).astype(BF16)
            mixed = dot(value_columns[lanes, begin : begin + SPAN_KEYS], probs)
            attended_out[0, begin : begin + TILE, lanes] = head_columns(mixed).T.astype(BF16)
            at = tile * (H // 2) + pair
            log_out[0, at : at + 1, :] = peak + jnp.log(weight_sum)
    middle = dot(hot[WIN : WIN + span], embed[...]) + dot(attended_out[0], out_weight[...])
    middle_out[0] = middle
    centered = middle - jnp.mean(middle, -1, keepdims=True)
    variance = jnp.mean(centered * centered, -1, keepdims=True)
    normed = (centered * lax.rsqrt(variance + eps) * gain[...] + shift[...]).astype(BF16)
    normed_out[0] = normed
    chunk = 512
    hidden = middle + down_bias[...]
    for begin in range(0, hidden_width, chunk):
        cells = slice(begin, begin + chunk)
        preact = dot(normed, up_weight[:, cells]) + up_bias[:, cells]
        act, slope = gelu_with_slope(preact)
        act = act.astype(BF16)
        act_out[0, :, cells] = act
        slope_out[0, :, cells] = slope.astype(BF16)
        hidden = hidden + dot(act, down_weight[cells, :])
    high, low = split_two(hidden)
    high_out[0] = high
    low_out[0] = low
    products = dot_last(cot_stack[0, STACK:, :], high)
    inner = products[:STACK] + products[STACK:] + dot_last(cot_stack[0, :STACK, :], low)
    inner_out[0] = inner[:NB]
    frontier = 1.0 / (1.0 + jnp.exp(-inner[NB : NB + 1]))
    frontier_out[0] = frontier
    slot = place[0] + iota((1, span), 1)
    running_out[0] = running_sum(jnp.where(slot < lengths[item], frontier, 0.0), triangle[...])


def assignment(numbers, item, running, slot):
    before, total, count, length = (numbers[item, at] for at in range(4))
    position = count * (running + before) / total
    block_at = iota((NB, running.shape[1]), 0)
    distance = position - (block_at.astype(F32) + 0.5)
    kept = (slot < length) & (block_at.astype(F32) < count)
    assign = jnp.where(kept, jnp.exp(-spread * distance * distance), 0.0)
    return position, assign, assign * distance * (-2.0 * spread)


def pool_kernel(place, numbers, running, inner, high, low, stats_out, numer_out):
    item = pl.program_id(0)
    span = high.shape[1]
    slot = (place[0] + iota((1, span), 1)).astype(F32)
    position, assign, pull = assignment(numbers, item, running[0], slot)
    inner_products = inner[0]
    pull_inner = pull * inner_products
    lane = iota((NB, 128), 1)
    stats = jnp.zeros((NB, 128), F32)
    for at, terms in enumerate(
        (
            assign,
            assign * inner_products,
            pull,
            pull_inner,
            pull * position,
            pull_inner * position,
        )
    ):
        stats = jnp.where(lane == at, jnp.sum(terms, 1, keepdims=True), stats)
    stats_out[0] = stats.T[:8]
    assign_high, assign_low = split_two(assign)
    numer_out[0] = (
        dot(assign_high, high[0]) + dot(assign_low, high[0]) + dot(assign_high, low[0])
    )


def hidden_back_kernel(
    place, numbers, weights, running, frontier, inner, high, low, cot_stack,
    hidden_out, low_out, bias_out, frontier_grad_out,
    triangle,
):
    item = pl.program_id(0)
    span = high.shape[1]

    @pl.when(item == 0)
    def _():
        triangle[...] = jnp.where(
            iota((span, span), 0) >= iota((span, span), 1), 1.0, 0.0
        ).astype(BF16)
        bias_out[...] = jnp.zeros_like(bias_out)
        frontier_grad_out[...] = jnp.zeros_like(frontier_grad_out)

    slot = (place[0] + iota((1, span), 1)).astype(F32)
    position, assign, pull = assignment(numbers, item, running[0], slot)
    inverse = weights[0, :, 0:1]
    d_denom = weights[0, :, 1:2]
    d_position = jnp.sum((inner[0] * inverse + d_denom) * pull, 0, keepdims=True)
    d_cumulative = d_position * numbers[item, 2] / numbers[item, 1]
    d_prob = running_sum(d_cumulative, triangle[...]) + numbers[item, 4]
    share = frontier[0]
    d_logit = jnp.where(slot < numbers[item, 3], d_prob * share * (1.0 - share), 0.0)
    left = jnp.concatenate(
        [assign * inverse, d_logit, jnp.zeros((STACK - NB - 1, span), F32)], 0
    )
    left_high, left_low = split_two(left)
    d_hidden = dot_first(jnp.concatenate([left_high, left_low, left_high], 0), cot_stack[0])
    hidden_out[0] = d_hidden
    d_low = d_hidden.astype(BF16)
    low_out[0] = d_low
    bias_out[...] += jnp.sum(d_low.astype(F32), 0, keepdims=True)
    rows = slice(NB, STACK)
    products = (
        dot(left_high[rows], high[0]) + dot(left_low[rows], high[0]) + dot(left_high[rows], low[0])
    )
    frontier_grad_out[...] += products[0:1]


def feed_back_kernel(
    ids_row, d_hidden, d_hidden_low, slope, middle, gain, down_weight, up_weight, out_weight,
    preact_out, middle_out, attended_out, embed_out, up_bias_out, gain_out, shift_out,
):
    item = pl.program_id(0)
    hidden_width = up_weight.shape[1]
    vocab = embed_out.shape[0]

    @pl.when(item == 0)
    def _():
        for total in (embed_out, up_bias_out, gain_out, shift_out):
            total[...] = jnp.zeros_like(total)

    chunk = 512
    d_normed = None
    for begin in range(0, hidden_width, chunk):
        cells = slice(begin, begin + chunk)
        d_act = dot_last(d_hidden_low[0], down_weight[cells, :])
        d_preact = (d_act * slope[0, :, cells].astype(F32)).astype(BF16)
        preact_out[0, :, cells] = d_preact
        up_bias_out[:, cells] += jnp.sum(d_preact.astype(F32), 0, keepdims=True)
        part = dot_last(d_preact, up_weight[:, cells])
        d_normed = part if d_normed is None else d_normed + part
    rows = middle[0]
    centered = rows - jnp.mean(rows, -1, keepdims=True)
    scale = lax.rsqrt(jnp.mean(centered * centered, -1, keepdims=True) + eps)
    unit = centered * scale
    gain_out[...] += jnp.sum(d_normed * unit, 0, keepdims=True)
    shift_out[...] += jnp.sum(d_normed, 0, keepdims=True)
    pushed = d_normed * gain[...]
    d_middle = d_hidden[0] + scale * (
        pushed
        - jnp.mean(pushed, -1, keepdims=True)
        - unit * jnp.mean(pushed * unit, -1, keepdims=True)
    )
    high, low = split_two(d_middle)
    middle_out[0] = high
    attended_out[0] = dot_last(high, out_weight[...]).astype(BF16)
    hot = one_hot_columns(ids_row[0], vocab)
    embed_out[...] += dot(hot, high) + dot(hot, low)


def attend_back_kernel(
    place, ids_column, ids_row, table, key_table, d_attended, logs,
    queries_out, keys_out, values_out,
    bias, table_rows, key_columns, d_queries, d_keys, d_values, queries_total,
):
    item = pl.program_id(0)
    span = d_attended.shape[1]
    model_width = d_attended.shape[2]
    vocab = table.shape[0]

    @pl.when(item == 0)
    def _():
        for at, tile in enumerate(window_bias(place[1], place[2])):
            bias[at] = tile
        for total in (queries_total, keys_out, values_out):
            total[...] = jnp.zeros_like(total)

    hot = one_hot_rows(ids_column[0], vocab)
    hot_columns = one_hot_columns(ids_row[0], vocab)
    table_rows[...] = dot(hot, table[...]).astype(BF16)
    key_columns[...] = dot(key_table[...], hot_columns).astype(BF16)
    d_keys[...] = jnp.zeros_like(d_keys)
    d_values[...] = jnp.zeros_like(d_values)
    tiles = span // TILE
    for tile in range(tiles):
        begin = tile * TILE
        tile_bias = bias[0 if tile == 0 else (2 if tile == tiles - 1 else 1)]
        window = slice(begin, begin + SPAN_KEYS)
        for pair in range(H // 2):
            lanes = slice(pair * PAIR, (pair + 1) * PAIR)
            key_lanes = slice(model_width + pair * PAIR, model_width + (pair + 1) * PAIR)
            value_lanes = slice(2 * model_width + pair * PAIR, 2 * model_width + (pair + 1) * PAIR)
            query_block = head_blocks(table_rows[begin + WIN : begin + WIN + TILE, lanes])
            grad_block = head_blocks(d_attended[0, begin : begin + TILE, lanes])
            at = tile * (H // 2) + pair
            scores = dot_last(table_rows[window, key_lanes], query_block) + tile_bias
            probs = jnp.exp(scores - logs[0, at : at + 1, :])
            d_probs = dot_last(table_rows[window, value_lanes], grad_block)
            weighted = probs * d_probs
            d_scores = (weighted - probs * jnp.sum(weighted, 0, keepdims=True)).astype(BF16)
            d_values[window, lanes] += dot(probs.astype(BF16), grad_block)
            d_keys[window, lanes] += dot(d_scores, query_block)
            turned = dot(key_columns[lanes, window], d_scores)
            d_queries[lanes, begin : begin + TILE] = (
                head_columns(turned) * (HD**-0.5)
            ).astype(BF16)
    queries_total[...] += dot(d_queries[...], hot[WIN : WIN + span])
    keys_out[...] += dot(hot_columns, d_keys[...].astype(BF16))
    values_out[...] += dot(hot_columns, d_values[...].astype(BF16))

    @pl.when(item == pl.num_programs(0) - 1)
    def _():
        queries_out[...] = queries_total[...].T


def whole(shape):
    return pl.BlockSpec(shape, lambda item: (0,) * len(shape))


def per_item(shape):
    return pl.BlockSpec((1,) + shape, lambda item: (item,) + (0,) * len(shape))


def scalars():
    return pl.BlockSpec(memory_space=pltpu.SMEM)


def call(kernel, items, in_specs, outs, scratch, flops, arrays):
    shapes = [jax.ShapeDtypeStruct(shape, dtype) for _, shape, dtype in outs]
    return pl.pallas_call(
        kernel,
        grid=(items,),
        in_specs=in_specs,
        out_specs=[spec for spec, _, _ in outs],
        out_shape=shapes,
        scratch_shapes=scratch,
        compiler_params=pltpu.CompilerParams(vmem_limit_bytes=VMEM_BYTES),
        cost_estimate=pl.CostEstimate(
            flops=flops,
            bytes_accessed=sum(
                cells.size * cells.dtype.itemsize for cells in list(arrays) + shapes
            ),
            transcendentals=0,
        ),
    )(*arrays)


def item_out(items, shape, dtype):
    return per_item(shape), (items,) + shape, dtype


def total_out(shape, dtype=F32):
    return whole(shape), shape, dtype


def bits_of(count):
    return [1 << at for at in range(count.bit_length() - 1)]


def scan_over(axis, cells, index):
    count = lax.axis_size(axis)
    earlier = jnp.zeros_like(cells)
    later = jnp.zeros_like(cells)
    for bit in bits_of(count):
        other = lax.ppermute(cells, axis, [(at, at ^ bit) for at in range(count)])
        upper = (index & bit) != 0
        earlier = earlier + jnp.where(upper, other, 0.0)
        later = later + jnp.where(upper, 0.0, other)
        cells = cells + other
    return earlier, cells, later


class Exchange:
    def __init__(self):
        self.outer = lax.axis_size("dp")
        self.inner = lax.axis_size("seq")
        outer_bits = [("dp", bit) for bit in bits_of(self.outer)]
        inner_bits = [("seq", bit) for bit in bits_of(self.inner)]
        rest = outer_bits[1:] + inner_bits[:-1]
        turn = len(outer_bits) - 1
        first = outer_bits[:1]
        last = inner_bits[-1:]
        self.orders = (first + rest + last, first + rest[turn:] + rest[:turn] + last)
        self.steps = len(self.orders[0])
        self.at = {"dp": lax.axis_index("dp"), "seq": lax.axis_index("seq")}

    def partner(self, flat, step):
        outer, inner = divmod(flat, self.inner)
        axis, bit = self.orders[outer & 1][step]
        if axis == "dp":
            outer ^= bit
        else:
            inner ^= bit
        return outer * self.inner + inner

    def swap(self, cells, step):
        devices = self.outer * self.inner
        pairs = [(flat, self.partner(flat, step)) for flat in range(devices)]
        return lax.ppermute(cells, ("dp", "seq"), pairs)

    def side(self, step):
        picked = [
            ((self.at[axis] & bit) != 0).astype(jnp.int32)
            for axis, bit in (order[step] for order in self.orders)
        ]
        return jnp.where((self.at["dp"] & 1) == 0, picked[0], picked[1])

    def scatter_sum(self, cells, extra=None):
        for step in range(self.steps):
            half = cells.shape[0] // 2
            side = self.side(step)
            sent = lax.dynamic_slice_in_dim(cells, (1 - side) * half, half, 0)
            kept = lax.dynamic_slice_in_dim(cells, side * half, half, 0)
            if extra is not None:
                high, low = split_two_outside(extra)
                sent = jnp.concatenate([sent, high, low], 0)
            came = self.swap(sent, step)
            cells = (kept.astype(F32) + came[:half].astype(F32)).astype(BF16)
            if extra is not None:
                rows = extra.shape[0]
                mine = high.astype(F32) + low.astype(F32)
                extra = mine + (
                    came[half : half + rows].astype(F32) + came[half + rows :].astype(F32)
                )
        return cells, extra

    def gather(self, cells):
        for step in reversed(range(self.steps)):
            side = self.side(step)
            came = self.swap(cells, step)
            half = cells.shape[0]
            joined = jnp.zeros((2 * half,) + cells.shape[1:], cells.dtype)
            joined = lax.dynamic_update_slice_in_dim(joined, cells, side * half, 0)
            cells = lax.dynamic_update_slice_in_dim(joined, came, (1 - side) * half, 0)
        return cells


def local(
    byte_ids,
    item_lengths,
    block_counts,
    byte_embed,
    norm1_gain,
    norm1_shift,
    qkv_weight,
    out_weight,
    norm2_gain,
    norm2_shift,
    up_weight,
    up_bias,
    down_weight,
    down_bias,
    frontier_weight,
    pooled_cot,
):
    items, span = byte_ids.shape
    vocab, model_width = byte_embed.shape
    hidden_width = up_weight.shape[1]
    seq_count = lax.axis_size("seq")
    seq_place = lax.axis_index("seq")
    tokens = items * span
    wide = span + 2 * WIN
    tiles = span // TILE

    ends = range(seq_count - 1)
    ids_wide = jnp.concatenate(
        [
            lax.ppermute(byte_ids[:, span - WIN :], "seq", [(at, at + 1) for at in ends]),
            byte_ids,
            lax.ppermute(byte_ids[:, :WIN], "seq", [(at + 1, at) for at in ends]),
        ],
        1,
    )
    ids_column = ids_wide[:, :, None]
    ids_row = ids_wide[:, None, :]

    embed_rows = byte_embed.astype(F32)
    centered = embed_rows - jnp.mean(embed_rows, -1, keepdims=True)
    scale_one = lax.rsqrt(jnp.mean(centered * centered, -1, keepdims=True) + eps)
    unit_one = centered * scale_one
    normed_one = (unit_one * norm1_gain + norm1_shift).astype(BF16)
    table = dot(normed_one, qkv_weight).astype(BF16)
    query_scale = jnp.where(jnp.arange(3 * model_width) < model_width, HD**-0.5, 1.0).astype(BF16)
    scaled_table = table * query_scale
    key_table = table[:, model_width : 2 * model_width].T
    value_table = table[:, 2 * model_width :].T

    cot_rows = jnp.concatenate(
        [
            pooled_cot,
            jnp.broadcast_to(frontier_weight, (items, 1, model_width)),
            jnp.zeros((items, STACK - NB - 1, model_width), F32),
        ],
        1,
    )
    cot_high, cot_low = split_two_outside(cot_rows)
    cot_stack = jnp.concatenate([cot_high, cot_high, cot_low], 1)

    first = (seq_place == 0).astype(jnp.int32)
    last = (seq_place == seq_count - 1).astype(jnp.int32)
    place = jnp.stack([seq_place * span, first, last]).astype(jnp.int32)

    square = (span, model_width)
    full = (span, hidden_width)
    row = (1, span)
    (
        attended, logs, middle, normed_two, act, slope, hidden_high, hidden_low,
        inner, frontier, running,
    ) = call(
        forward_kernel,
        items,
        [scalars(), scalars(), per_item((wide, 1)), per_item((1, wide))]
        + [
            whole(shape)
            for shape in (
                (vocab, 2 * model_width), (model_width, vocab), (vocab, model_width),
                (model_width, model_width), (1, model_width), (1, model_width),
                (model_width, hidden_width), (1, hidden_width),
                (hidden_width, model_width), (1, model_width),
            )
        ]
        + [per_item((3 * STACK, model_width))],
        [
            item_out(items, square, BF16),
            item_out(items, (tiles * H // 2, 2 * TILE), F32),
            item_out(items, square, F32),
            item_out(items, square, BF16),
            item_out(items, full, BF16),
            item_out(items, full, BF16),
            item_out(items, square, BF16),
            item_out(items, square, BF16),
            item_out(items, (NB, span), F32),
            item_out(items, row, F32),
            item_out(items, row, F32),
        ],
        [
            pltpu.VMEM((3, SPAN_KEYS, 2 * TILE), F32),
            pltpu.VMEM((wide, 2 * model_width), BF16),
            pltpu.VMEM((model_width, wide), BF16),
            pltpu.VMEM((span, span), BF16),
        ],
        2 * tokens * model_width * (2 * hidden_width + 3 * model_width),
        (
            place, item_lengths, ids_column, ids_row, scaled_table[:, : 2 * model_width],
            value_table, byte_embed, out_weight, norm2_gain[None], norm2_shift[None],
            up_weight, up_bias[None], down_weight, down_bias[None], cot_stack,
        ),
    )

    mass = running[:, 0, span - 1]
    mass_before, item_total, _ = scan_over("seq", mass, seq_place)
    counts_real = block_counts.astype(F32)
    lengths_real = item_lengths.astype(F32)
    numbers = jnp.stack([mass_before, item_total, counts_real, lengths_real], 1)

    stats, numer = call(
        pool_kernel,
        items,
        [scalars(), scalars(), per_item(row), per_item((NB, span)), per_item(square), per_item(square)],
        [item_out(items, (8, NB), F32), item_out(items, (NB, model_width), F32)],
        [],
        6 * tokens * NB * model_width,
        (place, numbers, running, inner, hidden_high, hidden_low),
    )

    _, stats_whole, stats_after = scan_over("seq", stats, seq_place)
    inverse = 1.0 / (stats_whole[:, 0] + 1.0)
    d_denom = -inverse * inverse * stats_whole[:, 1]
    pooled = lax.psum(numer, "seq") * inverse[:, :, None]
    push_after = jnp.sum(d_denom * stats_after[:, 2] + inverse * stats_after[:, 3], 1)
    total_sum = jnp.sum(d_denom * stats_whole[:, 4] + inverse * stats_whole[:, 5], 1)
    constant = (push_after * counts_real - total_sum) / item_total
    numbers_back = jnp.concatenate([numbers, constant[:, None]], 1)
    block_weights = jnp.stack([inverse, d_denom], 2)

    d_hidden, d_hidden_low, d_down_bias, d_frontier = call(
        hidden_back_kernel,
        items,
        [scalars(), scalars(), per_item((NB, 2)), per_item(row), per_item(row), per_item((NB, span)),
         per_item(square), per_item(square), per_item((3 * STACK, model_width))],
        [
            item_out(items, square, F32),
            item_out(items, square, BF16),
            total_out((1, model_width)),
            total_out((1, model_width)),
        ],
        [pltpu.VMEM((span, span), BF16)],
        8 * tokens * NB * model_width,
        (place, numbers_back, block_weights, running, frontier, inner, hidden_high, hidden_low,
         cot_stack),
    )
    flat_act = act.reshape(tokens, hidden_width)
    d_down = dot_first(flat_act, d_hidden_low.reshape(tokens, model_width)).astype(BF16)

    (
        d_preact, d_middle, d_attended, d_embed_direct, d_up_bias, d_gain_two, d_shift_two,
    ) = call(
        feed_back_kernel,
        items,
        [per_item(row), per_item(square), per_item(square), per_item(full), per_item(square),
         whole((1, model_width)), whole((hidden_width, model_width)),
         whole((model_width, hidden_width)), whole((model_width, model_width))],
        [
            item_out(items, full, BF16),
            item_out(items, square, BF16),
            item_out(items, square, BF16),
            total_out((vocab, model_width)),
            total_out((1, hidden_width)),
            total_out((1, model_width)),
            total_out((1, model_width)),
        ],
        [],
        4 * tokens * model_width * hidden_width,
        (byte_ids[:, None, :], d_hidden, d_hidden_low, slope, middle, norm2_gain[None],
         down_weight, up_weight, out_weight),
    )
    d_up = dot_first(
        normed_two.reshape(tokens, model_width), d_preact.reshape(tokens, hidden_width)
    ).astype(BF16)
    d_out = dot_first(
        attended.reshape(tokens, model_width), d_middle.reshape(tokens, model_width)
    ).astype(BF16)

    d_queries, d_keys, d_values = call(
        attend_back_kernel,
        items,
        [scalars(), per_item((wide, 1)), per_item((1, wide)), whole((vocab, 3 * model_width)),
         whole((model_width, vocab)), per_item(square), per_item((tiles * H // 2, 2 * TILE))],
        [total_out((vocab, model_width))] * 3,
        [
            pltpu.VMEM((3, SPAN_KEYS, 2 * TILE), F32),
            pltpu.VMEM((wide, 3 * model_width), BF16),
            pltpu.VMEM((model_width, wide), BF16),
            pltpu.VMEM((model_width, span), BF16),
            pltpu.VMEM((wide, model_width), F32),
            pltpu.VMEM((wide, model_width), F32),
            pltpu.VMEM((model_width, vocab), F32),
        ],
        10 * tokens * SPAN_KEYS * model_width,
        (place, ids_column, ids_row, scaled_table, key_table, d_attended, logs),
    )

    exchange = Exchange()
    blocks = hidden_width // model_width
    big = jnp.concatenate(
        [d_down]
        + [d_up[:, at * model_width : (at + 1) * model_width] for at in range(blocks)]
        + [d_out],
        0,
    )
    small = jnp.concatenate(
        [d_embed_direct.astype(BF16), d_queries.astype(BF16), d_keys.astype(BF16),
         d_values.astype(BF16)],
        0,
    )
    vectors = jnp.concatenate(
        [d_gain_two, d_shift_two, d_down_bias, d_frontier,
         d_up_bias.reshape(blocks, model_width)],
        0,
    )
    big_share, _ = exchange.scatter_sum(big)
    small_share, vectors = exchange.scatter_sum(small, vectors)
    big = exchange.gather(big_share).astype(F32)
    small = exchange.gather(small_share)

    d_down = big[:hidden_width]
    d_up = jnp.concatenate(
        [
            big[hidden_width + at * model_width : hidden_width + (at + 1) * model_width]
            for at in range(blocks)
        ],
        1,
    )
    d_out = big[2 * hidden_width :]
    d_table = jnp.concatenate(
        [small[at * vocab : (at + 1) * vocab] for at in range(1, 4)], 1
    )
    d_qkv = dot_first(normed_one, d_table)
    d_normed_one = dot_last(d_table, qkv_weight)
    d_gain_one = jnp.sum(d_normed_one * unit_one, 0)
    d_shift_one = jnp.sum(d_normed_one, 0)
    pushed = d_normed_one * norm1_gain
    d_embed = small[:vocab].astype(F32) + scale_one * (
        pushed
        - jnp.mean(pushed, -1, keepdims=True)
        - unit_one * jnp.mean(pushed * unit_one, -1, keepdims=True)
    )
    return (
        pooled,
        d_embed,
        d_gain_one,
        d_shift_one,
        d_qkv,
        d_out,
        vectors[0],
        vectors[1],
        d_up,
        vectors[4:].reshape(-1),
        d_down,
        vectors[2],
        vectors[3],
    )


def solution(mesh):
    placed = (P("dp", "seq"), P("dp"), P("dp")) + (P(),) * 12 + (P("dp", None, None),)
    return jax.shard_map(
        local,
        mesh=mesh,
        in_specs=placed,
        out_specs=(P("dp", None, None),) + (P(),) * 12,
        check_vma=False,
    )
```

time: 816 us -> 393 us (0.48)
  matrix products: 211 us -> 24 us
  local copies, waits for them, and re-layouts: 169 us -> 30.8 us
  waiting for transfers between devices: 249 us -> 130 us
  Pallas kernels: 0 us -> 114 us
  blocking collectives: 98.3 us -> 0 us
  starting transfers between devices: 12.9 us -> 49.5 us
  other arithmetic: 53 us -> 25.5 us
    dot_general x47 -> x6, matrix products: 211 us -> 24 us  [the longest x4 20.8 us: dot_first(): lax.dot_general(left, right, (((0,), (0,)), ((), ())), preferred_element_...]
    psum x2 -> x1, waiting for transfers between devices: 247 us -> 61.3 us  [local(): pooled = lax.psum(numer, 'seq') * inverse[:, :, None]]
    pallas_call x0 -> x5, Pallas kernels: none -> 114 us  [call(): pl.pallas_call(kernel, grid=(items,), in_specs=in_specs, out_specs=[spec...]
    psum x4 -> x0, blocking collectives: 98.3 us -> none  [the longest x1 39.2 us: local(): lax.psum((d_embed, d_gain_one, d_shift_one, d_qkv, d_out, d_gain_two, d_s...]
    ppermute x4 -> x28, waiting for transfers between devices: 1.7 us -> 68.8 us  [the longest x20 58.5 us: swap(): return lax.ppermute(cells, ('dp', 'seq'), pairs)]
    ppermute x4 -> x28, starting transfers between devices: 12.8 us -> 49.5 us  [the longest x20 28.7 us: swap(): return lax.ppermute(cells, ('dp', 'seq'), pairs)]
    dynamic_update_slice x16 -> x18, local copies, waits for them, and re-layouts: 34.9 us -> 4.34 us  [the longest x10 3.79 us: gather(): cells = lax.dynamic_update_slice_in_dim(joined, came, (1 - side) * half, 0)]
    slice x17 -> x9, local copies, waits for them, and re-layouts: 37.9 us -> 7.73 us  [the longest x1 2.61 us: local(): d_down = big[:hidden_width]]
  transfers between devices with their start and end apart: 6 -> 29, of which waited for: 3 -> 17; matrix products, arithmetic and copies ran while one was open for 6% -> 8% of each run, Pallas kernels for 0% -> 7%
where the time goes in v1:
time: 393 us; the launch traced here: 390 us
  waiting for transfers between devices  130 us (33%)
  Pallas kernels  114 us (29%)
  starting transfers between devices  49.5 us (13%)
  local copies, waits for them, and re-layouts  30.8 us (8%)
  other arithmetic  25.5 us (6%)
  matrix products  24 us (6%)
  between operations  15.1 us (4%)
    pallas_call x5, Pallas kernels, call(): pl.pallas_call(kernel, grid=(items,), in_specs=in_specs, out_specs=[spec...  114 us
    psum x1, waiting for transfers between devices, local(): pooled = lax.psum(numer, 'seq') * inverse[:, :, None]  61.3 us
    ppermute x20, waiting for transfers between devices, swap(): return lax.ppermute(cells, ('dp', 'seq'), pairs)  58.5 us
    ppermute x20, starting transfers between devices, swap(): return lax.ppermute(cells, ('dp', 'seq'), pairs)  28.7 us
    dot_general x4, matrix products, dot_first(): lax.dot_general(left, right, (((0,), (0,)), ((), ())), preferred_element_...  20.8 us
    ppermute x6, starting transfers between devices, scan_over(): other = lax.ppermute(cells, axis, [(at, at ^ bit) for at in range(count)])  14.6 us
    ppermute x6, waiting for transfers between devices, scan_over(): other = lax.ppermute(cells, axis, [(at, at ^ bit) for at in range(count)])  10.3 us
  transfers between devices with their start and end apart: 29, of which 17 were waited for; matrix products, arithmetic and copies ran while one was open for 8% of the time, Pallas kernels for 7%

profile of v1, /device:TPU:0, one launch (start us, length us, event | category | flops | bytes accessed | tf_op | source)
XLA Modules:
  0.0 389.5 jit_solution(1391109159274599687)
XLA Ops:
  8.1 4.9 %collective-permute-start = (s32[4,64]{1,0:T(4,128)S(1)}, s32[4,64]{1,0:T(4,128)S(1)}, u32[]{:S(2)}, u32[]{:S(2)}) collective-permute-start(s32[4,64]{1,0:T(4,128)S(1)} %get-tuple-element.107), channel_id=1, source_target_pairs={{0,1},{1,2},{2,3},{3,4},{4,5},{5,6},{6,7},{8,9},{9,10},{10,11},{11... | collective-permute-start | bytes 3080 | tf_op jit(solution)/shard_map/ppermute | solution.py:503
  13.0 1.3 collective-permute-start.1
  15.4 1.2 fusion.17
  16.6 2.0 broadcast_multiply_fusion
  22.6 1.5 copy.101.ids_column
  24.8 55.2 %shard_map.255 = (bf16[4,512,512]{2,1,0:T(8,128)(2,1)}, f32[4,16,256]{2,1,0:T(8,128)}, f32[4,512,512]{2,1,0:T(8,128)}, bf16[4,512,512]{2,1,0:T(8,128)(2,1)}, bf1...) custom-call(s32[3]{0:T(128)} %pad_add_fusion.1.place, ...), custom_call_target="tpu_custom_call" | custom-call | flops 11811160064 | bytes 36751388 | tf_op jit(solution)/shard_map/pallas_call | solution.py:365
  80.8 2.7 collective-permute-start.2
  83.5 1.5 collective-permute-done.2
  85.1 3.0 collective-permute-start.3
  88.0 1.5 collective-permute-done.3
  89.6 3.0 collective-permute-start.4
  92.6 1.5 collective-permute-done.4
  95.0 4.7 %shard_map.256 = (f32[4,8,64]{2,1,0:T(8,128)}, f32[4,64,512]{2,1,0:T(8,128)}) custom-call(s32[3]{0:T(128)} %pad_add_fusion.1.place, f32[4,4]{1,0:T(4,128)} %pad_maximum_fusion.12.numbers, f32[4,1,512]{2,1,0:T(1,128)} %get-tuple-element.40.running, f32[4,64,512]{2,1,0:T(8,128)} %get-tuple-element.41.inner, bf16[4,512,512]{2,1,0:T(8,128)(2,1)} %get-tuple-element.42.high, ...), custom_call_target="tpu_custom_call" | custom-call | flops 402653184 | bytes 5259340 | tf_op jit(solution)/shard_map/pallas_call | solution.py:365
  101.4 2.8 collective-permute-done.5
  104.9 2.0 collective-permute-start.6
  106.9 1.8 collective-permute-done.6
  108.7 3.0 collective-permute-start.7
  112.3 1.1 collective-permute-done.7
  115.2 7.3 %shard_map.257 = (f32[4,512,512]{2,1,0:T(8,128)}, bf16[4,512,512]{2,1,0:T(8,128)(2,1)}, f32[1,512]{1,0:T(1,128)}, f32[1,512]{1,0:T(1,128)}) custom-call(s32[3]{0:T(128)} %pad_add_fusion.1.place, f32[4,5]{1,0:T(4,128)} %concatenate.46.numbers, f32[4,64,2]{2,1,0:T(8,128)} %copy.121.weights, f32[4,1,512]{2,1,0:T(1,128)} %get-tuple-element.40.running, ...), custom_call_target="tpu_custom_call" | custom-call | flops 536870912 | bytes 12015708 | tf_op jit(solution)/shard_map/pallas_call | solution.py:365
  122.5 8.5 %fusion = bf16[4608,512]{1,0:T(8,128)(2,1)S(1)} fusion(bf16[4,512,2048]{2,1,0:T(8,128)(2,1)} %get-tuple-element.62, bf16[4,512,512]{2,1,0:T(8,128)(2,1)} %get-tuple-element.48.d_hidden_low), kind=kOutput, calls=%fused_computation.4 | convolution fusion | flops 4296015872 | bytes 12582912 | tf_op jit(solution)/shard_map/dot_general | solution.py:36
  131.1 20.1 %shard_map.258 = (bf16[4,512,2048]{2,1,0:T(8,128)(2,1)}, bf16[4,512,512]{2,1,0:T(8,128)(2,1)}, bf16[4,512,512]{2,1,0:T(8,128)(2,1)}, f32[256,512]{1,0:T(8,128)},...) custom-call(s32[4,1,512]{2,1,0:T(1,128)} %broadcast_in_dim.106.ids_row, ...), custom_call_target="tpu_custom_call" | custom-call | flops 8589934592 | bytes 36722688 | tf_op jit(solution)/shard_map/pallas_call | solution.py:365
  151.2 8.6 %bitcast_convert_fusion = bf16[512,2048]{1,0:T(8,128)(2,1)S(1)} fusion(bf16[4,512,512]{2,1,0:T(8,128)(2,1)} %get-tuple-element.63, bf16[4,512,2048]{2,1,0:T(8,128)(2,1)} %get-tuple-element.64), kind=kOutput, calls=%fused_computation.2 | convolution fusion | flops 4296015872 | bytes 12582912 | tf_op jit(solution)/shard_map/dot_general | solution.py:36
  160.0 1.4 copy-done.4
  162.0 1.3 fusion.2
  163.3 1.7 constant_dynamic-slice_fusion.4
  164.9 1.2 copy-done.3
  166.1 1.2 copy.123.table
  167.3 27.2 %shard_map.259 = (f32[256,512]{1,0:T(8,128)}, f32[256,512]{1,0:T(8,128)}, f32[256,512]{1,0:T(8,128)}) custom-call(s32[3]{0:T(128)} %pad_add_fusion.1.place, s32[4,640,1]{2,1,0:T(8,128)} %copy.101.ids_column, s32[4,1,640]{2,1,0:T(1,128)} %broadcast_in_dim.91.ids_row, bf16[256,1536]{1,0:T(8,128)(2,1)} %copy.123.table, ...), custom_call_target="tpu_custom_call" | custom-call | flops 2684354560 | bytes 4804620 | tf_op jit(solution)/shard_map/pallas_call | solution.py:365
  194.6 1.1 convert_element_type.296
  201.6 1.7 collective-permute-done.8
  203.3 1.2 add_convert_fusion.3
  204.5 3.0 add_convert_fusion
  207.6 1.4 copy-done.1
  210.1 1.5 collective-permute-start.19
  212.9 16.6 %collective-permute-done.9 = bf16[272,512]{1,0:T(8,128)(2,1)S(1)} collective-permute-done((bf16[272,512]{1,0:T(8,128)(2,1)S(1)}, bf16[272,512]{1,0:T(8,128)(2,1)S(1)}, u32[]{:S(2)}, u32[]{:S(2)}) %collective-permute-start.9) | collective-permute-done | bytes 278560 | tf_op jit(solution)/shard_map/ppermute | solution.py:434
  229.6 2.0 add_convert_fusion.1
  233.4 1.2 collective-permute-start.10
  234.5 9.6 %collective-permute-done.10 = bf16[144,512]{1,0:T(8,128)(2,1)S(1)} collective-permute-done((bf16[144,512]{1,0:T(8,128)(2,1)S(1)}, bf16[144,512]{1,0:T(8,128)(2,1)S(1)}, u32[]{:S(2)}, u32[]{:S(2)}) %collective-permute-start.10) | collective-permute-done | bytes 147488 | tf_op jit(solution)/shard_map/ppermute | solution.py:434
  244.2 1.3 add_convert_fusion.2
  245.5 2.0 collective-permute-start.21
  247.6 4.6 %collective-permute-done.21 = bf16[288,512]{1,0:T(8,128)(2,1)S(1)} collective-permute-done((bf16[288,512]{1,0:T(8,128)(2,1)S(1)}, bf16[288,512]{1,0:T(8,128)(2,1)S(1)}, u32[]{:S(2)}, u32[]{:S(2)}) %collective-permute-start.21) | collective-permute-done | bytes 294944 | tf_op jit(solution)/shard_map/ppermute | solution.py:434
  252.4 3.0 collective-permute-start.22
  255.4 5.0 %collective-permute-done.22 = bf16[144,512]{1,0:T(8,128)(2,1)S(1)} collective-permute-done((bf16[144,512]{1,0:T(8,128)(2,1)S(1)}, bf16[144,512]{1,0:T(8,128)(2,1)S(1)}, u32[]{:S(2)}, u32[]{:S(2)}) %collective-permute-start.22) | collective-permute-done | bytes 147488 | tf_op jit(solution)/shard_map/ppermute | solution.py:434
  260.4 1.2 collective-permute-start.23
  261.6 4.9 %collective-permute-done.23 = bf16[144,512]{1,0:T(8,128)(2,1)S(1)} collective-permute-done((bf16[144,512]{1,0:T(8,128)(2,1)S(1)}, bf16[144,512]{1,0:T(8,128)(2,1)S(1)}, u32[]{:S(2)}, u32[]{:S(2)}) %collective-permute-start.23) | collective-permute-done | bytes 147488 | tf_op jit(solution)/shard_map/ppermute | solution.py:434
  266.5 4.6 %collective-permute-start.24 = (bf16[288,512]{1,0:T(8,128)(2,1)S(1)}, bf16[288,512]{1,0:T(8,128)(2,1)S(1)}, u32[]{:S(2)}, u32[]{:S(2)}) collective-permute-start(bf16[288,512]{1,0:T(8,128)(2,1)S(1)} %constant_dynamic-update-slice_fusion.8), channel_id=1, source_target_pairs={{0,2},{1,3},{2,0},{3,1},{4,6},{5,7},{6,4},{7,5},{8,24},{9,25},{10,... | collective-permute-start | bytes 884744 | tf_op jit(solution)/shard_map/ppermute | solution.py:434
  271.1 2.9 collective-permute-start.12
  274.1 5.7 %collective-permute-done.24 = bf16[288,512]{1,0:T(8,128)(2,1)S(1)} collective-permute-done((bf16[288,512]{1,0:T(8,128)(2,1)S(1)}, bf16[288,512]{1,0:T(8,128)(2,1)S(1)}, u32[]{:S(2)}, u32[]{:S(2)}) %collective-permute-start.24) | collective-permute-done | bytes 294944 | tf_op jit(solution)/shard_map/ppermute | solution.py:434
  280.6 2.5 collective-permute-start.13
  283.1 2.3 collective-permute-done.13
  285.4 2.3 collective-permute-start.14
  287.8 3.3 collective-permute-done.14
  291.2 1.1 collective-permute-start.15
  293.6 1.3 collective-permute-start.26
  294.9 61.3 %all-reduce.2.cloned.1.call-done = f32[4,64,512]{2,1,0:T(8,128)} async-done(((f32[4,64,512]{2,1,0:T(8,128)}), f32[4,64,512]{2,1,0:T(8,128)}) %all-reduce.2.cloned.1.call-update) | async-done | bytes 524304 | tf_op jit(solution)/shard_map/psum | solution.py:604
  356.2 1.9 broadcast_multiply_fusion.1
  359.1 1.5 collective-permute-start.16
  360.7 4.8 %collective-permute-done.16 = bf16[256,512]{1,0:T(8,128)(2,1)S(1)} collective-permute-done((bf16[256,512]{1,0:T(8,128)(2,1)S(1)}, bf16[256,512]{1,0:T(8,128)(2,1)S(1)}, u32[]{:S(2)}, u32[]{:S(2)}) %collective-permute-start.16) | collective-permute-done | bytes 262176 | tf_op jit(solution)/shard_map/ppermute | solution.py:434
  365.9 1.4 constant_dynamic-update-slice_fusion.2
  370.1 1.3 fusion.16
  372.5 2.4 fusion.18
  375.7 1.7 fusion.41
  377.4 2.6 slice.224
  380.0 2.4 pad_maximum_fusion
  (174 shorter events, 32.9 us)
Async XLA Ops:
  7.2 9.4 %copy-start = (bf16[512,1536]{1,0:T(8,128)(2,1)S(1)}, bf16[512,1536]{1,0:T(8,128)(2,1)}, u32[]{:S(2)}) copy-start(bf16[512,1536]{1,0:T(8,128)(2,1)} %param.22) | copy-start | bytes 4718596
  7.2 349.0 %all-reduce.2.cloned.1.call-start = ((), (), s32[]{:S(2)}) async-start(), calls=%async_computation | async-start | bytes 1048576 | tf_op jit(solution)/shard_map/psum | solution.py:604
  8.1 14.4 %collective-permute-start = (s32[4,64]{1,0:T(4,128)S(1)}, s32[4,64]{1,0:T(4,128)S(1)}, u32[]{:S(2)}, u32[]{:S(2)}) collective-permute-start(s32[4,64]{1,0:T(4,128)S(1)} %get-tuple-element.107), channel_id=1, source_target_pairs={{0,1},{1,2},{2,3},{3,4},{4,5},{5,6},{6,7},{8,9},{9,10},{10,11},{11... | collective-permute-start | bytes 3080 | tf_op jit(solution)/shard_map/ppermute | solution.py:503
  13.0 9.6 %collective-permute-start.1 = (s32[4,64]{1,0:T(4,128)S(1)}, s32[4,64]{1,0:T(4,128)S(1)}, u32[]{:S(2)}, u32[]{:S(2)}) collective-permute-start(s32[4,64]{1,0:T(4,128)S(1)} %get-tuple-element.108), channel_id=1, source_target_pairs={{1,0},{2,1},{3,2},{4,3},{5,4},{6,5},{7,6},{9,8},{10,9},{11,10},{12... | collective-permute-start | bytes 3080 | tf_op jit(solution)/shard_map/ppermute | solution.py:505
  16.6 2.8 copy-start.17
  16.6 2.8 copy-start.18
  16.6 2.9 copy-start.12
  16.6 2.9 copy-start.7
  19.7 2.9 copy-start.8
  80.8 4.2 %collective-permute-start.2 = (f32[4]{0:T(128)S(1)}, f32[4]{0:T(128)S(1)}, u32[]{:S(2)}, u32[]{:S(2)}) collective-permute-start(f32[4]{0:T(128)S(1)} %slice_reduce_fusion), channel_id=1, source_target_pairs={{0,1},{1,0},{2,3},{3,2},{4,5},{5,4},{6,7},{7,6},{8,9},{9,8},{10,11... | collective-permute-start | bytes 56 | tf_op jit(solution)/shard_map/ppermute | solution.py:400
  85.1 4.5 %collective-permute-start.3 = (f32[4]{0:T(128)S(1)}, f32[4]{0:T(128)S(1)}, u32[]{:S(2)}, u32[]{:S(2)}) collective-permute-start(f32[4]{0:T(128)S(1)} %add.228), channel_id=1, source_target_pairs={{0,2},{1,3},{2,0},{3,1},{4,6},{5,7},{6,4},{7,5},{8,10},{9,11},{10,... | collective-permute-start | bytes 56 | tf_op jit(solution)/shard_map/ppermute | solution.py:400
  89.6 4.6 %collective-permute-start.4 = (f32[4]{0:T(128)S(1)}, f32[4]{0:T(128)S(1)}, u32[]{:S(2)}, u32[]{:S(2)}) collective-permute-start(f32[4]{0:T(128)S(1)} %add.230), channel_id=1, source_target_pairs={{0,4},{1,5},{2,6},{3,7},{4,0},{5,1},{6,2},{7,3},{8,12},{9,13},{10,... | collective-permute-start | bytes 56 | tf_op jit(solution)/shard_map/ppermute | solution.py:400
  100.4 3.7 collective-permute-start.5
  104.9 3.8 collective-permute-start.6
  108.7 4.7 %collective-permute-start.7 = (f32[4,8,64]{2,0,1:T(4,128)S(1)}, f32[4,8,64]{2,0,1:T(4,128)S(1)}, u32[]{:S(2)}, u32[]{:S(2)}) collective-permute-start(f32[4,8,64]{2,0,1:T(4,128)S(1)} %copy.111), channel_id=1, source_target_pairs={{0,4},{1,5},{2,6},{3,7},{4,0},{5,1},{6,2},{7,3},{8,12},{9,13},{10,... | collective-permute-start | bytes 24584 | tf_op jit(solution)/shard_map/ppermute | solution.py:400
  159.8 1.6 copy-start.4
  159.8 2.2 copy-start.5
  163.3 2.8 copy-start.3
  166.1 38.4 %collective-permute-start.18 = (bf16[2304,512]{1,0:T(8,128)(2,1)}, bf16[2304,512]{1,0:T(8,128)(2,1)}, u32[]{:S(2)}, u32[]{:S(2)}) collective-permute-start(bf16[2304,512]{1,0:T(8,128)(2,1)} %constant_dynamic-slice_fusion.4), channel_id=1, source_target_pairs={{0,8},{1,9},{2,10},{3,11},{4,12},{5,13},{6,14},{7,15},{8,0},{9,1},... | collective-permute-start | bytes 7077896 | tf_op jit(solution)/shard_map/ppermute | solution.py:434
  194.5 3.4 copy-start.6
  194.5 4.6 %copy-start.11 = (f32[1,2048]{1,0:T(1,128)S(1)}, f32[1,2048]{1,0:T(1,128)}, u32[]{:S(2)}) copy-start(f32[1,2048]{1,0:T(1,128)} %get-tuple-element.61) | copy-start | bytes 24580
  194.5 5.3 %copy-start.13 = (f32[1,512]{1,0:T(1,128)S(1)}, f32[1,512]{1,0:T(1,128)}, u32[]{:S(2)}) copy-start(f32[1,512]{1,0:T(1,128)} %get-tuple-element.59) | copy-start | bytes 6148
  194.5 5.3 %copy-start.14 = (f32[1,512]{1,0:T(1,128)S(1)}, f32[1,512]{1,0:T(1,128)}, u32[]{:S(2)}) copy-start(f32[1,512]{1,0:T(1,128)} %get-tuple-element.60) | copy-start | bytes 6148
  194.5 5.3 %copy-start.15 = (f32[1,512]{1,0:T(1,128)S(1)}, f32[1,512]{1,0:T(1,128)}, u32[]{:S(2)}) copy-start(f32[1,512]{1,0:T(1,128)} %get-tuple-element.57) | copy-start | bytes 6148
  194.5 5.3 %copy-start.16 = (f32[1,512]{1,0:T(1,128)S(1)}, f32[1,512]{1,0:T(1,128)}, u32[]{:S(2)}) copy-start(f32[1,512]{1,0:T(1,128)} %get-tuple-element.58) | copy-start | bytes 6148
  201.0 2.3 collective-permute-start.8
  207.6 1.4 copy-start.1
  210.1 19.5 %collective-permute-start.19 = (bf16[1152,512]{1,0:T(8,128)(2,1)}, bf16[1152,512]{1,0:T(8,128)(2,1)}, u32[]{:S(2)}, u32[]{:S(2)}) collective-permute-start(bf16[1152,512]{1,0:T(8,128)(2,1)} %constant_dynamic-slice_fusion.3), channel_id=1, source_target_pairs={{0,16},{1,17},{2,18},{3,19},{4,20},{5,21},{6,22},{7,23},{8,9},{9,8... | collective-permute-start | bytes 3538952 | tf_op jit(solution)/shard_map/ppermute | solution.py:434
  212.3 17.2 %collective-permute-start.9 = (bf16[272,512]{1,0:T(8,128)(2,1)S(1)}, bf16[272,512]{1,0:T(8,128)(2,1)S(1)}, u32[]{:S(2)}, u32[]{:S(2)}) collective-permute-start(bf16[272,512]{1,0:T(8,128)(2,1)S(1)} %pad_maximum_fusion.7), channel_id=1, source_target_pairs={{0,16},{1,17},{2,18},{3,19},{4,20},{5,21},{6,22},{7,23},{8,9},{9,8... | collective-permute-start | bytes 835592 | tf_op jit(solution)/shard_map/ppermute | solution.py:434
  232.4 11.7 %collective-permute-start.20 = (bf16[576,512]{1,0:T(8,128)(2,1)}, bf16[576,512]{1,0:T(8,128)(2,1)}, u32[]{:S(2)}, u32[]{:S(2)}) collective-permute-start(bf16[576,512]{1,0:T(8,128)(2,1)} %constant_dynamic-slice_fusion.2), channel_id=1, source_target_pairs={{0,1},{1,0},{2,3},{3,2},{4,5},{5,4},{6,7},{7,6},{8,10},{9,11},{10,... | collective-permute-start | bytes 1769480 | tf_op jit(solution)/shard_map/ppermute | solution.py:434
  233.4 10.7 %collective-permute-start.10 = (bf16[144,512]{1,0:T(8,128)(2,1)S(1)}, bf16[144,512]{1,0:T(8,128)(2,1)S(1)}, u32[]{:S(2)}, u32[]{:S(2)}) collective-permute-start(bf16[144,512]{1,0:T(8,128)(2,1)S(1)} %pad_maximum_fusion.8), channel_id=1, source_target_pairs={{0,1},{1,0},{2,3},{3,2},{4,5},{5,4},{6,7},{7,6},{8,10},{9,11},{10,... | collective-permute-start | bytes 442376 | tf_op jit(solution)/shard_map/ppermute | solution.py:434
  245.5 6.8 %collective-permute-start.21 = (bf16[288,512]{1,0:T(8,128)(2,1)S(1)}, bf16[288,512]{1,0:T(8,128)(2,1)S(1)}, u32[]{:S(2)}, u32[]{:S(2)}) collective-permute-start(bf16[288,512]{1,0:T(8,128)(2,1)S(1)} %constant_dynamic-slice_fusion.1), channel_id=1, source_target_pairs={{0,2},{1,3},{2,0},{3,1},{4,6},{5,7},{6,4},{7,5},{8,24},{9,25},{10,... | collective-permute-start | bytes 884744 | tf_op jit(solution)/shard_map/ppermute | solution.py:434
  247.5 7.9 %collective-permute-start.11 = (bf16[80,512]{1,0:T(8,128)(2,1)S(1)}, bf16[80,512]{1,0:T(8,128)(2,1)S(1)}, u32[]{:S(2)}, u32[]{:S(2)}) collective-permute-start(bf16[80,512]{1,0:T(8,128)(2,1)S(1)} %pad_maximum_fusion.9), channel_id=1, source_target_pairs={{0,2},{1,3},{2,0},{3,1},{4,6},{5,7},{6,4},{7,5},{8,24},{9,25},{10,... | collective-permute-start | bytes 245768 | tf_op jit(solution)/shard_map/ppermute | solution.py:434
  252.4 8.0 %collective-permute-start.22 = (bf16[144,512]{1,0:T(8,128)(2,1)S(1)}, bf16[144,512]{1,0:T(8,128)(2,1)S(1)}, u32[]{:S(2)}, u32[]{:S(2)}) collective-permute-start(bf16[144,512]{1,0:T(8,128)(2,1)S(1)} %constant_dynamic-slice_fusion), channel_id=1, source_target_pairs={{0,4},{1,5},{2,6},{3,7},{4,0},{5,1},{6,2},{7,3},{8,12},{9,13},{10,... | collective-permute-start | bytes 442376 | tf_op jit(solution)/shard_map/ppermute | solution.py:434
  260.4 6.1 %collective-permute-start.23 = (bf16[144,512]{1,0:T(8,128)(2,1)S(1)}, bf16[144,512]{1,0:T(8,128)(2,1)S(1)}, u32[]{:S(2)}, u32[]{:S(2)}) collective-permute-start(bf16[144,512]{1,0:T(8,128)(2,1)S(1)} %get-tuple-element.74), channel_id=1, source_target_pairs={{0,4},{1,5},{2,6},{3,7},{4,0},{5,1},{6,2},{7,3},{8,12},{9,13},{10,... | collective-permute-start | bytes 442376 | tf_op jit(solution)/shard_map/ppermute | solution.py:434
  266.5 13.3 %collective-permute-start.24 = (bf16[288,512]{1,0:T(8,128)(2,1)S(1)}, bf16[288,512]{1,0:T(8,128)(2,1)S(1)}, u32[]{:S(2)}, u32[]{:S(2)}) collective-permute-start(bf16[288,512]{1,0:T(8,128)(2,1)S(1)} %constant_dynamic-update-slice_fusion.8), channel_id=1, source_target_pairs={{0,2},{1,3},{2,0},{3,1},{4,6},{5,7},{6,4},{7,5},{8,24},{9,25},{10,... | collective-permute-start | bytes 884744 | tf_op jit(solution)/shard_map/ppermute | solution.py:434
  271.1 9.4 %collective-permute-start.12 = (bf16[48,512]{1,0:T(8,128)(2,1)S(1)}, bf16[48,512]{1,0:T(8,128)(2,1)S(1)}, u32[]{:S(2)}, u32[]{:S(2)}) collective-permute-start(bf16[48,512]{1,0:T(8,128)(2,1)S(1)} %pad_maximum_fusion.10), channel_id=1, source_target_pairs={{0,4},{1,5},{2,6},{3,7},{4,0},{5,1},{6,2},{7,3},{8,12},{9,13},{10,... | collective-permute-start | bytes 147464 | tf_op jit(solution)/shard_map/ppermute | solution.py:434
  279.8 12.6 %collective-permute-start.25 = (bf16[576,512]{1,0:T(8,128)(2,1)S(1)}, bf16[576,512]{1,0:T(8,128)(2,1)}, u32[]{:S(2)}, u32[]{:S(2)}) collective-permute-start(bf16[576,512]{1,0:T(8,128)(2,1)S(1)} %constant_dynamic-update-slice_fusion.6), channel_id=1, source_target_pairs={{0,1},{1,0},{2,3},{3,2},{4,5},{5,4},{6,7},{7,6},{8,10},{9,11},{10,... | collective-permute-start | bytes 1769480 | tf_op jit(solution)/shard_map/ppermute | solution.py:434
  280.6 4.9 %collective-permute-start.13 = (bf16[32,512]{1,0:T(8,128)(2,1)S(1)}, bf16[32,512]{1,0:T(8,128)(2,1)S(1)}, u32[]{:S(2)}, u32[]{:S(2)}) collective-permute-start(bf16[32,512]{1,0:T(8,128)(2,1)S(1)} %get-tuple-element.76), channel_id=1, source_target_pairs={{0,4},{1,5},{2,6},{3,7},{4,0},{5,1},{6,2},{7,3},{8,12},{9,13},{10,... | collective-permute-start | bytes 98312 | tf_op jit(solution)/shard_map/ppermute | solution.py:434
  285.4 5.7 %collective-permute-start.14 = (bf16[64,512]{1,0:T(8,128)(2,1)S(1)}, bf16[64,512]{1,0:T(8,128)(2,1)S(1)}, u32[]{:S(2)}, u32[]{:S(2)}) collective-permute-start(bf16[64,512]{1,0:T(8,128)(2,1)S(1)} %constant_dynamic-update-slice_fusion.18), channel_id=1, source_target_pairs={{0,2},{1,3},{2,0},{3,1},{4,6},{5,7},{6,4},{7,5},{8,24},{9,25},{10,... | collective-permute-start | bytes 196616 | tf_op jit(solution)/shard_map/ppermute | solution.py:434
  291.2 67.0 %collective-permute-start.15 = (bf16[128,512]{1,0:T(8,128)(2,1)S(1)}, bf16[128,512]{1,0:T(8,128)(2,1)}, u32[]{:S(2)}, u32[]{:S(2)}) collective-permute-start(bf16[128,512]{1,0:T(8,128)(2,1)S(1)} %constant_dynamic-update-slice_fusion.16), channel_id=1, source_target_pairs={{0,1},{1,0},{2,3},{3,2},{4,5},{5,4},{6,7},{7,6},{8,10},{9,11},{10,... | collective-permute-start | bytes 393224 | tf_op jit(solution)/shard_map/ppermute | solution.py:434
  293.6 72.4 %collective-permute-start.26 = (bf16[1152,512]{1,0:T(8,128)(2,1)S(1)}, bf16[1152,512]{1,0:T(8,128)(2,1)}, u32[]{:S(2)}, u32[]{:S(2)}) collective-permute-start(bf16[1152,512]{1,0:T(8,128)(2,1)S(1)} %constant_dynamic-update-slice_fusion.4), channel_id=1, source_target_pairs={{0,16},{1,17},{2,18},{3,19},{4,20},{5,21},{6,22},{7,23},{8,9},{9,8... | collective-permute-start | bytes 3538952 | tf_op jit(solution)/shard_map/ppermute | solution.py:434
  359.1 6.4 %collective-permute-start.16 = (bf16[256,512]{1,0:T(8,128)(2,1)S(1)}, bf16[256,512]{1,0:T(8,128)(2,1)S(1)}, u32[]{:S(2)}, u32[]{:S(2)}) collective-permute-start(bf16[256,512]{1,0:T(8,128)(2,1)S(1)} %constant_dynamic-update-slice_fusion.14), channel_id=1, source_target_pairs={{0,16},{1,17},{2,18},{3,19},{4,20},{5,21},{6,22},{7,23},{8,9},{9,8... | collective-permute-start | bytes 786440 | tf_op jit(solution)/shard_map/ppermute | solution.py:434
  365.6 3.7 collective-permute-start.17
  367.3 8.1 %collective-permute-start.27 = (bf16[2304,512]{1,0:T(8,128)(2,1)S(1)}, bf16[2304,512]{1,0:T(8,128)(2,1)S(1)}, u32[]{:S(2)}, u32[]{:S(2)}) collective-permute-start(bf16[2304,512]{1,0:T(8,128)(2,1)S(1)} %constant_dynamic-update-slice_fusion.2), channel_id=1, source_target_pairs={{0,8},{1,9},{2,10},{3,11},{4,12},{5,13},{6,14},{7,15},{8,0},{9,1},... | collective-permute-start | bytes 7077896 | tf_op jit(solution)/shard_map/ppermute | solution.py:434
  369.2 1.0 copy-start.2
  369.2 0.9 copy-start.9
  370.1 2.4 copy-start.10
Sparse Core Ops, SparseCore 0:
  283.2 72.8 all-reduce.1

commit v2 on v1

v2 whole, which is shorter than its diff:
```python
import functools

import jax
import jax.numpy as jnp
from jax import lax
from jax.experimental import pallas as pl
from jax.experimental.pallas import tpu as pltpu
from jax.sharding import PartitionSpec as P

H = 8
HD = 64
WIN = 64
NB = 64
TILE = 128
SPAN_KEYS = TILE + 2 * WIN
PAIR = 2 * HD
STACK = 80

eps = 1e-05
spread = 2.0
LOG2E = 1.4426950408889634
F32 = jnp.float32
BF16 = jnp.bfloat16
VMEM_BYTES = 56 * 1024 * 1024


def dot(left, right):
    return jnp.dot(left, right, preferred_element_type=F32)


def dot_last(left, right):
    return lax.dot_general(left, right, (((1,), (1,)), ((), ())), preferred_element_type=F32)


def dot_first(left, right):
    return lax.dot_general(left, right, (((0,), (0,)), ((), ())), preferred_element_type=F32)


def split_two_outside(value):
    high = lax.reduce_precision(value, 8, 7)
    return high.astype(BF16), (value - high).astype(BF16)


def split_two(value):
    high = value.astype(BF16)
    return high, (value - high.astype(F32)).astype(BF16)


def iota(shape, dim):
    return lax.broadcasted_iota(jnp.int32, shape, dim)


def one_hot_columns(ids_row, vocab):
    cells = iota((vocab, ids_row.shape[1]), 0)
    return jnp.where(cells == ids_row, 1.0, 0.0).astype(BF16)


def gelu_with_slope(value):
    below = 0.5 + 0.5 * lax.erf(value * 0.7071067811865476)
    bell = jnp.exp2(value * value * (-0.5 * LOG2E))
    return value * below, below + value * (bell * 0.3989422804014327)


def window_bias(first, last):
    key_at = iota((SPAN_KEYS, 2 * TILE), 0)
    query_at = iota((SPAN_KEYS, 2 * TILE), 1) & (TILE - 1)
    reach = key_at - query_at
    seen = (reach >= 0) & (reach <= 2 * WIN)
    seen_first = seen & (key_at >= WIN * first)
    seen_last = seen & (key_at < SPAN_KEYS - WIN * last)
    return [jnp.where(kept, 0.0, -1e30) for kept in (seen_first, seen, seen_last)]


def head_blocks(pair_rows):
    lane = iota(pair_rows.shape, 1)
    blank = jnp.zeros_like(pair_rows)
    return jnp.concatenate(
        [jnp.where(lane < HD, pair_rows, blank), jnp.where(lane < HD, blank, pair_rows)], 0
    )


def head_columns(pair_columns):
    return jnp.concatenate([pair_columns[:HD, :TILE], pair_columns[HD:, TILE:]], 0)


def running_sum(row, ones_matrix):
    one, rest = split_two(row)
    high = one.astype(F32) + rest.astype(F32)
    two = (row - high).astype(BF16)
    width = row.shape[1]
    parts = jnp.concatenate([one, rest, two, jnp.zeros((13, width), BF16)], 0)
    sums = dot(parts, ones_matrix)
    return sums[0:1] + sums[1:2] + sums[2:3]


def table_kernel(
    embed, gain, shift, weight, cot, frontier_weight,
    normed_out, table_out, key_out, value_out, stack_out,
):
    rows = embed[...].astype(F32)
    centered = rows - jnp.mean(rows, -1, keepdims=True)
    scale = lax.rsqrt(jnp.mean(centered * centered, -1, keepdims=True) + eps)
    normed = (centered * scale * gain[...] + shift[...]).astype(BF16)
    normed_out[...] = normed
    model_width = rows.shape[1]
    table = dot(normed, weight[...])
    queries = table[:, :model_width].astype(BF16).astype(F32) * HD**-0.5
    table_out[:, :model_width] = queries.astype(BF16)
    table_out[:, model_width:] = table[:, model_width:].astype(BF16)
    key_out[...] = table[:, model_width : 2 * model_width].T.astype(BF16)
    value_out[...] = table[:, 2 * model_width :].T.astype(BF16)
    rim_high, rim_low = split_two(
        jnp.where(iota((STACK - NB, model_width), 0) == 0, frontier_weight[...], 0.0)
    )
    for item in range(cot.shape[0]):
        high, low = split_two(cot[item])
        for at, (block, rim) in enumerate(((high, rim_high), (high, rim_high), (low, rim_low))):
            stack_out[item, at * STACK : at * STACK + NB] = block
            stack_out[item, at * STACK + NB : (at + 1) * STACK] = rim


def forward_kernel(
    place, lengths, ids_row, table, value_table, embed, out_weight, gain, shift,
    up_weight, up_bias, down_weight, down_bias, cot_stack,
    attended_out, log_out, middle_out, normed_out, act_out, slope_out, high_out, low_out,
    inner_out, frontier_out, running_out,
    bias, query_keys, value_columns, triangle,
):
    item = pl.program_id(0)
    span = middle_out.shape[1]
    model_width = middle_out.shape[2]
    vocab = embed.shape[0]
    hidden_width = up_weight.shape[1]

    @pl.when(item == 0)
    def _():
        for at, tile in enumerate(window_bias(place[1], place[2])):
            bias[at] = tile
        triangle[...] = jnp.where(
            iota((span, span), 0) <= iota((span, span), 1), 1.0, 0.0
        ).astype(BF16)

    hot_columns = one_hot_columns(ids_row[0], vocab)
    hot = hot_columns.T
    query_keys[...] = dot(hot, table[:, : 2 * model_width]).astype(BF16)
    value_columns[...] = dot(value_table[...], hot_columns).astype(BF16)
    tiles = span // TILE
    pairs = H // 2
    for tile in range(tiles):
        begin = tile * TILE
        window = slice(begin, begin + SPAN_KEYS)
        tile_bias = bias[0 if tile == 0 else (2 if tile == tiles - 1 else 1)]
        lanes = [slice(pair * PAIR, (pair + 1) * PAIR) for pair in range(pairs)]
        scores = []
        for pair in range(pairs):
            key_lanes = slice(model_width + pair * PAIR, model_width + (pair + 1) * PAIR)
            query_block = head_blocks(query_keys[begin + WIN : begin + WIN + TILE, lanes[pair]])
            scores.append(dot_last(query_keys[window, key_lanes], query_block) + tile_bias)
        probs = []
        for pair in range(pairs):
            peak = jnp.max(scores[pair], 0, keepdims=True)
            weights = jnp.exp(scores[pair] - peak)
            weight_sum = jnp.sum(weights, 0, keepdims=True)
            probs.append((weights * pltpu.reciprocal(weight_sum, approx=True)).astype(BF16))
            at = tile * pairs + pair
            log_out[0, at : at + 1, :] = peak + jnp.log(weight_sum)
        mixed = [dot(value_columns[lanes[pair], window], probs[pair]) for pair in range(pairs)]
        for pair in range(pairs):
            attended_out[0, begin : begin + TILE, lanes[pair]] = (
                head_columns(mixed[pair]).T.astype(BF16)
            )
    middle = dot(hot[WIN : WIN + span], embed[...]) + dot(attended_out[0], out_weight[...])
    middle_out[0] = middle
    centered = middle - jnp.mean(middle, -1, keepdims=True)
    variance = jnp.mean(centered * centered, -1, keepdims=True)
    normed = (centered * lax.rsqrt(variance + eps) * gain[...] + shift[...]).astype(BF16)
    normed_out[0] = normed
    chunk = 512
    cuts = [slice(begin, begin + chunk) for begin in range(0, hidden_width, chunk)]
    hidden = middle + down_bias[...]
    preact = dot(normed, up_weight[:, cuts[0]]) + up_bias[:, cuts[0]]
    for at, cells in enumerate(cuts):
        held = preact
        if at + 1 < len(cuts):
            preact = dot(normed, up_weight[:, cuts[at + 1]]) + up_bias[:, cuts[at + 1]]
        act, slope = gelu_with_slope(held)
        act = act.astype(BF16)
        act_out[0, :, cells] = act
        slope_out[0, :, cells] = slope.astype(BF16)
        hidden = hidden + dot(act, down_weight[cells, :])
    high, low = split_two(hidden)
    high_out[0] = high
    low_out[0] = low
    products = dot_last(cot_stack[0, STACK:, :], high)
    inner = products[:STACK] + products[STACK:] + dot_last(cot_stack[0, :STACK, :], low)
    inner_out[0] = inner[:NB]
    frontier = 1.0 / (1.0 + jnp.exp(-inner[NB : NB + 1]))
    frontier_out[0] = frontier
    slot = place[0] + iota((1, span), 1)
    running_out[0] = running_sum(jnp.where(slot < lengths[item], frontier, 0.0), triangle[...])


def assignment(place, lengths, counts, before, total, running):
    item = pl.program_id(0)
    span = running.shape[2]
    slot = place[0] + iota((1, span), 1)
    inside = slot < lengths[item]
    count = counts[item].astype(F32)
    position = count * (running[0] + before[item]) / total[item]
    block_at = iota((NB, span), 0)
    distance = position - (block_at.astype(F32) + 0.5)
    kept = inside & (block_at < counts[item])
    assign = jnp.where(kept, jnp.exp(-spread * distance * distance), 0.0)
    return position, assign, assign * distance * (-2.0 * spread), inside, count


def stats_kernel(place, lengths, counts, before, total, running, inner, stats_out):
    position, assign, pull, _, _ = assignment(place, lengths, counts, before, total, running)
    pull_inner = pull * inner[0]
    lane = iota((NB, 128), 1)
    stats = jnp.zeros((NB, 128), F32)
    terms = (
        assign, assign * inner[0], pull, pull_inner, pull * position, pull_inner * position,
    )
    for at, cells in enumerate(terms):
        stats = jnp.where(lane == at, jnp.sum(cells, 1, keepdims=True), stats)
    stats_out[0] = stats.T[:8]


def numer_kernel(place, lengths, counts, before, total, running, high, low, numer_out):
    _, assign, _, _, _ = assignment(place, lengths, counts, before, total, running)
    assign_high, assign_low = split_two(assign)
    numer_out[0] = (
        dot(assign_high, high[0]) + dot(assign_low, high[0]) + dot(assign_high, low[0])
    )


def hidden_gradient(
    place, lengths, counts, before, total, running, frontier, inner, whole_stats, after_stats,
    triangle,
):
    item = pl.program_id(0)
    span = running.shape[2]
    position, assign, pull, inside, count = assignment(
        place, lengths, counts, before, total, running
    )
    whole_columns = whole_stats[0].T
    after_columns = after_stats[0].T
    inverse = 1.0 / (whole_columns[:, 0:1] + 1.0)
    d_denom = -inverse * inverse * whole_columns[:, 1:2]
    push = jnp.sum(
        d_denom * after_columns[:, 2:3] + inverse * after_columns[:, 3:4], 0, keepdims=True
    )
    pushed = jnp.sum(
        d_denom * whole_columns[:, 4:5] + inverse * whole_columns[:, 5:6], 0, keepdims=True
    )
    d_position = jnp.sum((inner[0] * inverse + d_denom) * pull, 0, keepdims=True)
    d_cumulative = d_position * count / total[item]
    d_prob = running_sum(d_cumulative, triangle[...]) + (push * count - pushed) / total[item]
    share = frontier[0]
    d_logit = jnp.where(inside, d_prob * share * (1.0 - share), 0.0)
    left = jnp.concatenate(
        [assign * inverse, d_logit, jnp.zeros((STACK - NB - 1, span), F32)], 0
    )
    return split_two(left)


def write_halves(place, total, sent_out, kept_out):
    half = kept_out.shape[0]
    core = place[3]
    sent_out[...] = total[pl.ds(pl.multiple_of((1 - core) * half, half), half)].astype(BF16)
    kept_out[...] = total[pl.ds(pl.multiple_of(core * half, half), half)].astype(BF16)


def suffix_ones(triangle):
    triangle[...] = jnp.where(
        iota(triangle.shape, 0) >= iota(triangle.shape, 1), 1.0, 0.0
    ).astype(BF16)


def back_kernel(
    place, lengths, counts, before, total, running, frontier, inner, whole_stats, after_stats,
    cot_stack, ids_row, act, slope, high, low, middle, normed, attended, gain, down_weight,
    up_weight, out_weight,
    down_sent, down_kept, up_sent, up_kept, attended_out, embed_out, rows_out,
    triangle, down_total, up_total,
):
    hidden_width = up_weight.shape[1]
    model_width = up_weight.shape[0]
    vocab = embed_out.shape[0]

    @pl.when(pl.program_id(0) == 0)
    def _():
        suffix_ones(triangle)
        for cells in (down_total, up_total, embed_out, rows_out):
            cells[...] = jnp.zeros_like(cells)

    left_high, left_low = hidden_gradient(
        place, lengths, counts, before, total, running, frontier, inner, whole_stats,
        after_stats, triangle,
    )
    d_hidden = dot_first(jnp.concatenate([left_high, left_low, left_high], 0), cot_stack[0])
    d_low = d_hidden.astype(BF16)
    cuts = [
        slice(begin, begin + model_width) for begin in range(0, hidden_width, model_width)
    ]
    d_act = dot_last(d_low, down_weight[cuts[0], :])
    d_normed = None
    for at, cells in enumerate(cuts):
        held = d_act
        if at + 1 < len(cuts):
            d_act = dot_last(d_low, down_weight[cuts[at + 1], :])
        d_preact = (held * slope[0, :, cells].astype(F32)).astype(BF16)
        down_total[cells, :] += dot_first(act[0, :, cells], d_low)
        part = dot_last(d_preact, up_weight[:, cells])
        d_normed = part if d_normed is None else d_normed + part
        up_total[cells, :] += dot_first(normed[0], d_preact)
        rows_out[4 + at : 5 + at] += jnp.sum(d_preact.astype(F32), 0, keepdims=True)
    rows = middle[0]
    centered = rows - jnp.mean(rows, -1, keepdims=True)
    scale = lax.rsqrt(jnp.mean(centered * centered, -1, keepdims=True) + eps)
    unit = centered * scale
    tail = slice(NB, STACK)
    products = (
        dot(left_high[tail], high[0]) + dot(left_low[tail], high[0]) + dot(left_high[tail], low[0])
    )
    rows_out[2:3] += jnp.sum(d_low.astype(F32), 0, keepdims=True)
    rows_out[3:4] += products[0:1]
    rows_out[0:1] += jnp.sum(d_normed * unit, 0, keepdims=True)
    rows_out[1:2] += jnp.sum(d_normed, 0, keepdims=True)
    pushed = d_normed * gain[...]
    d_middle = d_hidden + scale * (
        pushed
        - jnp.mean(pushed, -1, keepdims=True)
        - unit * jnp.mean(pushed * unit, -1, keepdims=True)
    )
    middle_high, middle_low = split_two(d_middle)
    attended_out[0] = dot_last(middle_high, out_weight[...]).astype(BF16)
    up_total[hidden_width:, :] += dot_first(attended[0], middle_high)
    hot = one_hot_columns(ids_row[0], vocab)
    embed_out[...] += dot(hot, middle_high) + dot(hot, middle_low)

    @pl.when(pl.program_id(0) == pl.num_programs(0) - 1)
    def _():
        write_halves(place, down_total, down_sent, down_kept)
        write_halves(place, up_total, up_sent, up_kept)


def attend_back_kernel(
    place, ids_row, table, key_table, d_attended, logs, rows_in,
    *outs_and_scratch,
):
    *outs, rows_total, bias, table_rows, key_columns, d_queries, d_keys, d_values, (
        queries_total
    ) = outs_and_scratch
    item = pl.program_id(0)
    span = d_attended.shape[1]
    model_width = d_attended.shape[2]
    vocab = table.shape[0]

    @pl.when(item == 0)
    def _():
        for at, tile in enumerate(window_bias(place[1], place[2])):
            bias[at] = tile
        given = rows_in.shape[0]
        rows_total[:given] = rows_in[...]
        if given < 4 * vocab:
            rows_total[given:] = jnp.zeros((4 * vocab - given, model_width), F32)
        queries_total[...] = jnp.zeros_like(queries_total)

    hot_columns = one_hot_columns(ids_row[0], vocab)
    hot = hot_columns.T
    table_rows[...] = dot(hot, table[...]).astype(BF16)
    key_columns[...] = dot(key_table[...], hot_columns).astype(BF16)
    d_keys[...] = jnp.zeros_like(d_keys)
    d_values[...] = jnp.zeros_like(d_values)
    tiles = span // TILE
    pairs = H // 2
    for tile in range(tiles):
        begin = tile * TILE
        tile_bias = bias[0 if tile == 0 else (2 if tile == tiles - 1 else 1)]
        window = slice(begin, begin + SPAN_KEYS)
        lanes = [slice(pair * PAIR, (pair + 1) * PAIR) for pair in range(pairs)]
        query_blocks, grad_blocks, scores, d_probs = [], [], [], []
        for pair in range(pairs):
            key_lanes = slice(model_width + pair * PAIR, model_width + (pair + 1) * PAIR)
            value_lanes = slice(2 * model_width + pair * PAIR, 2 * model_width + (pair + 1) * PAIR)
            query_blocks.append(
                head_blocks(table_rows[begin + WIN : begin + WIN + TILE, lanes[pair]])
            )
            grad_blocks.append(head_blocks(d_attended[0, begin : begin + TILE, lanes[pair]]))
            scores.append(dot_last(table_rows[window, key_lanes], query_blocks[pair]) + tile_bias)
            d_probs.append(dot_last(table_rows[window, value_lanes], grad_blocks[pair]))
        probs_low, d_scores = [], []
        for pair in range(pairs):
            at = tile * pairs + pair
            probs = jnp.exp(scores[pair] - logs[0, at : at + 1, :])
            weighted = probs * d_probs[pair]
            probs_low.append(probs.astype(BF16))
            d_scores.append(
                (weighted - probs * jnp.sum(weighted, 0, keepdims=True)).astype(BF16)
            )
        for pair in range(pairs):
            d_values[window, lanes[pair]] += dot(probs_low[pair], grad_blocks[pair])
            d_keys[window, lanes[pair]] += dot(d_scores[pair], query_blocks[pair])
        turned = [dot(key_columns[lanes[pair], window], d_scores[pair]) for pair in range(pairs)]
        for pair in range(pairs):
            d_queries[lanes[pair], begin : begin + TILE] = (
                head_columns(turned[pair]) * (HD**-0.5)
            ).astype(BF16)
    queries_total[...] += dot(d_queries[...], hot[WIN : WIN + span])
    rows_total[2 * vocab : 3 * vocab] += dot(hot_columns, d_keys[...].astype(BF16))
    rows_total[3 * vocab :] += dot(hot_columns, d_values[...].astype(BF16))

    @pl.when(item == pl.num_programs(0) - 1)
    def _():
        rows_total[vocab : 2 * vocab] += queries_total[...].T
        if len(outs) == 2:
            write_halves(place, rows_total, *outs)
        else:
            outs[0][...] = rows_total[...]


def whole(shape):
    return pl.BlockSpec(shape, lambda item: (0,) * len(shape))


def per_item(shape):
    return pl.BlockSpec((1,) + shape, lambda item: (item,) + (0,) * len(shape))


def item_from(shape, first):
    return pl.BlockSpec((1,) + shape, lambda item: (item + first,) + (0,) * len(shape))


def scalars():
    return pl.BlockSpec(memory_space=pltpu.SMEM)


def call(kernel, items, in_specs, outs, scratch, flops, arrays):
    flops = 1
    shapes = [jax.ShapeDtypeStruct(shape, dtype) for _, shape, dtype in outs]
    return pl.pallas_call(
        kernel,
        grid=(items,),
        in_specs=in_specs,
        out_specs=[spec for spec, _, _ in outs],
        out_shape=shapes,
        scratch_shapes=scratch,
        compiler_params=pltpu.CompilerParams(vmem_limit_bytes=VMEM_BYTES),
        cost_estimate=pl.CostEstimate(flops=flops, bytes_accessed=0, transcendentals=0),
    )(*arrays)


def item_out(items, shape, dtype):
    return per_item(shape), (items,) + shape, dtype


def halves_out(rows, width):
    return [total_out((rows // 2, width), BF16)] * 2


def total_out(shape, dtype=F32):
    return whole(shape), shape, dtype


def bits_of(count):
    return [1 << at for at in range(count.bit_length() - 1)]


def scan_over(axis, cells, index, beside=None):
    count = lax.axis_size(axis)
    earlier = jnp.zeros_like(cells)
    later = jnp.zeros_like(cells)
    for step, bit in enumerate(bits_of(count)):
        if step == 1 and beside is not None:
            cells, beside = lax.optimization_barrier((cells, beside))
        other = lax.ppermute(cells, axis, [(at, at ^ bit) for at in range(count)])
        upper = (index & bit) != 0
        earlier = earlier + jnp.where(upper, other, 0.0)
        later = later + jnp.where(upper, 0.0, other)
        cells = cells + other
    return earlier, cells, later, beside


def all_sum(axis, cells):
    count = lax.axis_size(axis)
    index = lax.axis_index(axis)
    steps = [
        (((index & bit) != 0).astype(jnp.int32), [(at, at ^ bit) for at in range(count)])
        for bit in bits_of(count)
    ]
    for side, pairs in steps:
        half = cells.shape[0] // 2
        sent = lax.dynamic_slice_in_dim(cells, (1 - side) * half, half, 0).astype(BF16)
        kept = lax.dynamic_slice_in_dim(cells, side * half, half, 0)
        cells = kept + lax.ppermute(sent, axis, pairs).astype(F32)
    cells = cells.astype(BF16)
    for side, pairs in reversed(steps):
        cells = joined(cells, lax.ppermute(cells, axis, pairs), side)
    return cells.astype(F32)


def joined(mine, came, side):
    half = mine.shape[0]
    cells = jnp.zeros((2 * half,) + mine.shape[1:], mine.dtype)
    cells = lax.dynamic_update_slice_in_dim(cells, mine, side * half, 0)
    return lax.dynamic_update_slice_in_dim(cells, came, (1 - side) * half, 0)


class Exchange:
    def __init__(self):
        self.outer = lax.axis_size("dp")
        self.inner = lax.axis_size("seq")
        outer_bits = [("dp", bit) for bit in bits_of(self.outer)]
        inner_bits = [("seq", bit) for bit in bits_of(self.inner)]
        rest = outer_bits[1:] + inner_bits[:-1]
        turn = len(outer_bits) - 1
        first = outer_bits[:1]
        last = inner_bits[-1:]
        self.orders = (first + rest + last, first + rest[turn:] + rest[:turn] + last)
        self.steps = len(self.orders[0])
        self.at = {"dp": lax.axis_index("dp"), "seq": lax.axis_index("seq")}

    def partner(self, flat, step):
        outer, inner = divmod(flat, self.inner)
        axis, bit = self.orders[outer & 1][step]
        if axis == "dp":
            outer ^= bit
        else:
            inner ^= bit
        return outer * self.inner + inner

    def swap(self, cells, step):
        devices = self.outer * self.inner
        pairs = [(flat, self.partner(flat, step)) for flat in range(devices)]
        return lax.ppermute(cells, ("dp", "seq"), pairs)

    def side(self, step):
        picked = [
            ((self.at[axis] & bit) != 0).astype(jnp.int32)
            for axis, bit in (order[step] for order in self.orders)
        ]
        return jnp.where((self.at["dp"] & 1) == 0, picked[0], picked[1])

    def scatter_sum(self, sent, kept, extra=None):
        for step in range(self.steps):
            if step > 0:
                half = cells.shape[0] // 2
                side = self.side(step)
                sent = lax.dynamic_slice_in_dim(cells, (1 - side) * half, half, 0).astype(BF16)
                kept = lax.dynamic_slice_in_dim(cells, side * half, half, 0)
            half = kept.shape[0]
            if extra is not None:
                high, low = split_two_outside(extra)
                sent = jnp.concatenate([sent, high, low], 0)
            came = self.swap(sent, step)
            cells = kept.astype(F32) + came[:half].astype(F32)
            if extra is not None:
                rows = extra.shape[0]
                mine = high.astype(F32) + low.astype(F32)
                extra = mine + (
                    came[half : half + rows].astype(F32) + came[half + rows :].astype(F32)
                )
        return cells.astype(BF16), extra

    def gather(self, cells):
        for step in reversed(range(self.steps)):
            cells = joined(cells, self.swap(cells, step), self.side(step))
        return cells


def local(
    byte_ids,
    item_lengths,
    block_counts,
    byte_embed,
    norm1_gain,
    norm1_shift,
    qkv_weight,
    out_weight,
    norm2_gain,
    norm2_shift,
    up_weight,
    up_bias,
    down_weight,
    down_bias,
    frontier_weight,
    pooled_cot,
):
    items, span = byte_ids.shape
    vocab, model_width = byte_embed.shape
    hidden_width = up_weight.shape[1]
    seq_count = lax.axis_size("seq")
    seq_place = lax.axis_index("seq")
    tokens = items * span
    wide = span + 2 * WIN
    tiles = span // TILE

    ends = range(seq_count - 1)
    ids_wide = jnp.concatenate(
        [
            lax.ppermute(byte_ids[:, span - WIN :], "seq", [(at, at + 1) for at in ends]),
            byte_ids,
            lax.ppermute(byte_ids[:, :WIN], "seq", [(at + 1, at) for at in ends]),
        ],
        1,
    )
    ids_row = ids_wide[:, None, :]
    ids_own = byte_ids[:, None, :]

    normed_one, table, key_table, value_table, cot_stack = call(
        table_kernel,
        1,
        [whole((vocab, model_width)), whole((1, model_width)), whole((1, model_width)),
         whole((model_width, 3 * model_width)), whole((items, NB, model_width)),
         whole((1, model_width))],
        [
            total_out((vocab, model_width), BF16),
            total_out((vocab, 3 * model_width), BF16),
            total_out((model_width, vocab), BF16),
            total_out((model_width, vocab), BF16),
            total_out((items, 3 * STACK, model_width), BF16),
        ],
        [],
        6 * vocab * model_width * model_width,
        (byte_embed, norm1_gain[None], norm1_shift[None], qkv_weight, pooled_cot,
         frontier_weight[None]),
    )

    first = (seq_place == 0).astype(jnp.int32)
    last = (seq_place == seq_count - 1).astype(jnp.int32)
    core = lax.axis_index("dp") & 1
    place = jnp.stack([seq_place * span, first, last, core]).astype(jnp.int32)

    square = (span, model_width)
    full = (span, hidden_width)
    row = (1, span)
    blocks = (NB, span)
    (
        attended, logs, middle, normed_two, act, slope, hidden_high, hidden_low,
        inner, frontier, running,
    ) = call(
        forward_kernel,
        items,
        [scalars(), scalars(), per_item((1, wide))]
        + [
            whole(shape)
            for shape in (
                (vocab, 3 * model_width), (model_width, vocab), (vocab, model_width),
                (model_width, model_width), (1, model_width), (1, model_width),
                (model_width, hidden_width), (1, hidden_width),
                (hidden_width, model_width), (1, model_width),
            )
        ]
        + [per_item((3 * STACK, model_width))],
        [
            item_out(items, square, BF16),
            item_out(items, (tiles * H // 2, 2 * TILE), F32),
            item_out(items, square, F32),
            item_out(items, square, BF16),
            item_out(items, full, BF16),
            item_out(items, full, BF16),
            item_out(items, square, BF16),
            item_out(items, square, BF16),
            item_out(items, blocks, F32),
            item_out(items, row, F32),
            item_out(items, row, F32),
        ],
        [
            pltpu.VMEM((3, SPAN_KEYS, 2 * TILE), F32),
            pltpu.VMEM((wide, 2 * model_width), BF16),
            pltpu.VMEM((model_width, wide), BF16),
            pltpu.VMEM((span, span), BF16),
        ],
        2 * tokens * model_width * (2 * hidden_width + 3 * model_width),
        (
            place, item_lengths, ids_row, table, value_table, byte_embed, out_weight,
            norm2_gain[None], norm2_shift[None], up_weight, up_bias[None], down_weight,
            down_bias[None], cot_stack,
        ),
    )

    mass_before, item_total, _, _ = scan_over("seq", running[:, 0, span - 1], seq_place)
    numbers = (place, item_lengths, block_counts, mass_before, item_total, running)
    numbers_specs = [scalars()] * 5 + [per_item(row)]

    (stats,) = call(
        stats_kernel,
        items,
        numbers_specs + [per_item(blocks)],
        [item_out(items, (8, NB), F32)],
        [],
        tokens * NB,
        numbers + (inner,),
    )
    (numer,) = call(
        numer_kernel,
        items,
        numbers_specs + [per_item(square), per_item(square)],
        [item_out(items, (NB, model_width), F32)],
        [],
        6 * tokens * NB * model_width,
        numbers + (hidden_high, hidden_low),
    )
    _, stats_whole, stats_after, numer = scan_over("seq", stats, seq_place, numer)

    back_specs = numbers_specs + [
        per_item(row), per_item(blocks), per_item((8, NB)), per_item((8, NB)),
        per_item((3 * STACK, model_width)),
    ]
    (
        down_sent, down_kept, up_sent, up_kept, d_attended, d_embed_direct, rows,
    ) = call(
        back_kernel,
        items,
        back_specs
        + [per_item(row), per_item(full), per_item(full)]
        + [per_item(square)] * 5
        + [whole((1, model_width)), whole((hidden_width, model_width)),
           whole((model_width, hidden_width)), whole((model_width, model_width))],
        halves_out(hidden_width, model_width)
        + halves_out(hidden_width + model_width, model_width)
        + [
            item_out(items, square, BF16),
            total_out((vocab, model_width)),
            total_out((8, model_width)),
        ],
        [
            pltpu.VMEM((span, span), BF16),
            pltpu.VMEM((hidden_width, model_width), F32),
            pltpu.VMEM((hidden_width + model_width, model_width), F32),
        ],
        6 * tokens * hidden_width * model_width,
        numbers
        + (frontier, inner, stats_whole, stats_after, cot_stack, ids_own, act, slope,
           hidden_high, hidden_low, middle, normed_two, attended, norm2_gain[None],
           down_weight, up_weight, out_weight),
    )

    exchange = Exchange()
    rows_sent, rows_kept = call(
        attend_back_kernel,
        items,
        [scalars(), per_item((1, wide)), whole((vocab, 3 * model_width)),
         whole((model_width, vocab)), per_item(square), per_item((tiles * H // 2, 2 * TILE)),
         whole((vocab, model_width))],
        halves_out(4 * vocab, model_width),
        [
            pltpu.VMEM((4 * vocab, model_width), F32),
            pltpu.VMEM((3, SPAN_KEYS, 2 * TILE), F32),
            pltpu.VMEM((wide, 3 * model_width), BF16),
            pltpu.VMEM((model_width, wide), BF16),
            pltpu.VMEM((model_width, span), BF16),
            pltpu.VMEM((wide, model_width), F32),
            pltpu.VMEM((wide, model_width), F32),
            pltpu.VMEM((model_width, vocab), F32),
        ],
        10 * tokens * SPAN_KEYS * model_width,
        (place, ids_row, table, key_table, d_attended, logs, d_embed_direct),
    )

    inverse = 1.0 / (stats_whole[:, 0] + 1.0)
    pooled = all_sum("seq", numer.reshape(items * NB, model_width)).reshape(
        items, NB, model_width
    ) * inverse[:, :, None]

    devices = exchange.outer * exchange.inner
    down_share, _ = exchange.scatter_sum(down_sent, down_kept)
    weights_share, rows = exchange.scatter_sum(up_sent, up_kept, rows)
    small_share, _ = exchange.scatter_sum(rows_sent, rows_kept)
    cut = down_share.shape[0]
    big = exchange.gather(jnp.concatenate([down_share, weights_share], 0))
    big = big.reshape(devices, -1, model_width)
    d_down = big[:, :cut].reshape(hidden_width, model_width).astype(F32)
    d_weights = big[:, cut:].reshape(-1, model_width).astype(F32)
    small = exchange.gather(small_share)

    d_up = jnp.concatenate(
        [
            d_weights[begin : begin + model_width]
            for begin in range(0, hidden_width, model_width)
        ],
        1,
    )
    d_out = d_weights[hidden_width:]
    d_table = jnp.concatenate(
        [small[at * vocab : (at + 1) * vocab] for at in range(1, 4)], 1
    )
    d_qkv = dot_first(normed_one, d_table)
    d_normed_one = dot_last(d_table, qkv_weight)
    embed_rows = byte_embed.astype(F32)
    centered = embed_rows - jnp.mean(embed_rows, -1, keepdims=True)
    scale_one = lax.rsqrt(jnp.mean(centered * centered, -1, keepdims=True) + eps)
    unit_one = centered * scale_one
    d_gain_one = jnp.sum(d_normed_one * unit_one, 0)
    d_shift_one = jnp.sum(d_normed_one, 0)
    pushed = d_normed_one * norm1_gain
    d_embed = small[:vocab].astype(F32) + scale_one * (
        pushed
        - jnp.mean(pushed, -1, keepdims=True)
        - unit_one * jnp.mean(pushed * unit_one, -1, keepdims=True)
    )
    return (
        pooled,
        d_embed,
        d_gain_one,
        d_shift_one,
        d_qkv,
        d_out,
        rows[0],
        rows[1],
        d_up,
        rows[4:].reshape(-1),
        d_down,
        rows[2],
        rows[3],
    )


def solution(mesh):
    placed = (P("dp", "seq"), P("dp"), P("dp")) + (P(),) * 12 + (P("dp", None, None),)
    return jax.shard_map(
        local,
        mesh=mesh,
        in_specs=placed,
        out_specs=(P("dp", None, None),) + (P(),) * 12,
        check_vma=False,
    )
```

time: 393 us -> 268 us (0.68)
  waiting for transfers between devices: 130 us -> 81.6 us
  local copies, waits for them, and re-layouts: 30.8 us -> 9.54 us
  matrix products: 24 us -> 3.53 us
  between operations: 15.1 us -> 1.48 us
  Pallas kernels: 114 us -> 102 us
  other arithmetic: 25.5 us -> 15.8 us
  starting transfers between devices: 49.5 us -> 54 us
    psum x1 -> x0, waiting for transfers between devices: 61.3 us -> none  [local(): pooled = lax.psum(numer, 'seq') * inverse[:, :, None]]
    dot_general x4 -> x1, matrix products: 20.8 us -> 2.26 us  [dot_first(): lax.dot_general(left, right, (((0,), (0,)), ((), ())), preferred_element_...]
    ppermute x20 -> x25, waiting for transfers between devices: 58.5 us -> 72.2 us  [swap(): return lax.ppermute(cells, ('dp', 'seq'), pairs)]
    pallas_call x5 -> x6, Pallas kernels: 114 us -> 102 us  [call(): pl.pallas_call(kernel, grid=(items,), in_specs=in_specs, out_specs=[spec...]
    ppermute x0 -> x6, starting transfers between devices: none -> 9.8 us  [the longest x3 5.35 us: all_sum(): cells = kept + lax.ppermute(sent, axis, pairs).astype(F32)]
    convert_element_type x13 -> x4, other arithmetic: 11.7 us -> 3.68 us  [the longest x1 2.74 us: local(): d_down = big[:, :cut].reshape(hidden_width, model_width).astype(F32)]
    unnamed x44 -> x24, local copies, waits for them, and re-layouts: 6.19 us -> 0.66 us
    ppermute x20 -> x25, starting transfers between devices: 28.7 us -> 24.1 us  [swap(): return lax.ppermute(cells, ('dp', 'seq'), pairs)]
  transfers between devices with their start and end apart: 29 -> 39, of which waited for: 17 -> 19; matrix products, arithmetic and copies ran while one was open for 8% -> 7% of each run, Pallas kernels for 7% -> 24%
where the time goes in v2:
time: 268 us
  Pallas kernels  102 us (38%)
  waiting for transfers between devices  81.6 us (30%)
  starting transfers between devices  54 us (20%)
  other arithmetic  15.8 us (6%)
  local copies, waits for them, and re-layouts  9.54 us (4%)
  matrix products  3.53 us (1%)
    pallas_call x6, Pallas kernels, call(): pl.pallas_call(kernel, grid=(items,), in_specs=in_specs, out_specs=[spec...  102 us
    ppermute x25, waiting for transfers between devices, swap(): return lax.ppermute(cells, ('dp', 'seq'), pairs)  72.2 us
    ppermute x25, starting transfers between devices, swap(): return lax.ppermute(cells, ('dp', 'seq'), pairs)  24.1 us
    ppermute x6, starting transfers between devices, scan_over(): other = lax.ppermute(cells, axis, [(at, at ^ bit) for at in range(count)])  13.9 us
    ppermute x6, waiting for transfers between devices, scan_over(): other = lax.ppermute(cells, axis, [(at, at ^ bit) for at in range(count)])  6.72 us
  transfers between devices with their start and end apart: 39, of which 19 were waited for; matrix products, arithmetic and copies ran while one was open for 7% of the time, Pallas kernels for 24%

profile of v2, /device:TPU:0, one launch (start us, length us, event | category | flops | bytes accessed | tf_op | source)
XLA Modules:
  0.0 267.8 jit_solution(3488099842012816663)
XLA Ops:
  0.7 0.8 fusion.26
  1.5 4.9 %collective-permute-start = (s32[4,64]{1,0:T(4,128)S(1)}, s32[4,64]{1,0:T(4,128)S(1)}, u32[]{:S(2)}, u32[]{:S(2)}) collective-permute-start(s32[4,64]{1,0:T(4,128)S(1)} %get-tuple-element.101), channel_id=1, source_target_pairs={{0,1},{1,2},{2,3},{3,4},{4,5},{5,6},{6,7},{8,9},{9,10},{10,11},{11... | collective-permute-start | bytes 3080 | tf_op jit(solution)/shard_map/ppermute | solution.py:603
  6.3 1.3 collective-permute-start.1
  7.6 1.1 convert_reduce_fusion
  8.7 1.2 fusion.10
  10.5 3.8 %shard_map.255 = (bf16[256,512]{1,0:T(8,128)(2,1)}, bf16[256,1536]{1,0:T(8,128)(2,1)}, bf16[512,256]{1,0:T(8,128)(2,1)}, bf16[512,256]{1,0:T(8,128)(2,1)}, bf16[4,240,512]{2,1,0:T(8,128)(2,1)}) custom-call(bf16[256,512]{1,0:T(8,128)(2,1)} %embed.3, f32[1,512]{1,0:T(1,128)} %bitcast.41, f32[1,512]{1,0:T(1,128)} %bitcast.48, bf16[512,1536]{1,0:T(8,128)(2,1)} %weight.1, ...), custom_call_target="tpu_custom_call" | custom-call | flops 1 | tf_op jit(solution)/shard_map/pallas_call | solution.py:443
  15.0 34.0 %shard_map.256 = (bf16[4,512,512]{2,1,0:T(8,128)(2,1)}, f32[4,16,256]{2,1,0:T(8,128)}, f32[4,512,512]{2,1,0:T(8,128)}, bf16[4,512,512]{2,1,0:T(8,128)(2,1)}, bf1...) custom-call(s32[4]{0:T(128)} %pad_add_fusion.1.place, ...), custom_call_target="tpu_custom_call" | custom-call | flops 1 | tf_op jit(solution)/shard_map/pallas_call | solution.py:443
  49.0 0.9 slice_reduce_fusion
  49.9 2.7 %collective-permute-start.2 = (f32[4]{0:T(128)S(1)}, f32[4]{0:T(128)S(1)}, u32[]{:S(2)}, u32[]{:S(2)}) collective-permute-start(f32[4]{0:T(128)S(1)} %slice_reduce_fusion), channel_id=1, source_target_pairs={{0,1},{1,0},{2,3},{3,2},{4,5},{5,4},{6,7},{7,6},{8,9},{9,8},{10,11... | collective-permute-start | bytes 56 | tf_op jit(solution)/shard_map/ppermute | solution.py:478
  52.6 1.5 collective-permute-done.2
  54.1 3.0 %collective-permute-start.3 = (f32[4]{0:T(128)S(1)}, f32[4]{0:T(128)S(1)}, u32[]{:S(2)}, u32[]{:S(2)}) collective-permute-start(f32[4]{0:T(128)S(1)} %add.271), channel_id=1, source_target_pairs={{0,2},{1,3},{2,0},{3,1},{4,6},{5,7},{6,4},{7,5},{8,10},{9,11},{10,... | collective-permute-start | bytes 56 | tf_op jit(solution)/shard_map/ppermute | solution.py:478
  57.1 1.5 collective-permute-done.3
  58.6 3.0 %collective-permute-start.4 = (f32[4]{0:T(128)S(1)}, f32[4]{0:T(128)S(1)}, u32[]{:S(2)}, u32[]{:S(2)}) collective-permute-start(f32[4]{0:T(128)S(1)} %add.273), channel_id=1, source_target_pairs={{0,4},{1,5},{2,6},{3,7},{4,0},{5,1},{6,2},{7,3},{8,12},{9,13},{10,... | collective-permute-start | bytes 56 | tf_op jit(solution)/shard_map/ppermute | solution.py:478
  61.6 1.5 collective-permute-done.4
  63.7 3.5 %shard_map.257 = f32[4,8,64]{2,1,0:T(8,128)} custom-call(s32[4]{0:T(128)} %pad_add_fusion.1.place, s32[4]{0:T(128)} %lengths.7, s32[4]{0:T(128)} %counts.5, f32[4]{0:T(128)} %get-tuple-element.104.before, f32[4]{0:T(128)} %get-tuple-element.103.total, f32[4,1,512]{2,1,0:T(1,128)} %get-tuple-element.43.running, f32[4,64,512]{2,1,0:T(8,128)} %get-tuple-element.44.inner), custom_call_target="tpu_custom_call" | custom-call | flops 1 | tf_op jit(solution)/shard_map/pallas_call | solution.py:443
  67.1 1.0 collective-permute-start.5
  68.7 4.6 %shard_map.258 = f32[4,64,512]{2,1,0:T(8,128)} custom-call(s32[4]{0:T(128)} %pad_add_fusion.1.place, s32[4]{0:T(128)} %lengths.7, s32[4]{0:T(128)} %counts.5, f32[4]{0:T(128)} %get-tuple-element.104.before, f32[4]{0:T(128)} %get-tuple-element.103.total, f32[4,1,512]{2,1,0:T(1,128)} %get-tuple-element.43.running, ...), custom_call_target="tpu_custom_call" | custom-call | flops 1 | tf_op jit(solution)/shard_map/pallas_call | solution.py:443
  73.4 1.6 collective-permute-start.12
  75.0 2.2 collective-permute-done.12
  77.2 2.6 collective-permute-start.13
  79.8 1.0 dynamic-slice_convert_fusion.8
  80.7 1.5 collective-permute-start.6
  82.8 35.3 %shard_map.259 = (bf16[1024,512]{1,0:T(8,128)(2,1)}, bf16[1024,512]{1,0:T(8,128)(2,1)}, bf16[1280,512]{1,0:T(8,128)(2,1)}, bf16[1280,512]{1,0:T(8,128)(2,1)}, bf...) custom-call(s32[4]{0:T(128)} %pad_add_fusion.1.place, s32[4]{0:T(128)} %lengths.7, s32[4]{0:T(128)} %counts.5, ...), custom_call_target="tpu_custom_call" | custom-call | flops 1 | tf_op jit(solution)/shard_map/pallas_call | solution.py:443
  118.2 20.6 %shard_map.260 = (bf16[512,512]{1,0:T(8,128)(2,1)}, bf16[512,512]{1,0:T(8,128)(2,1)}) custom-call(s32[4]{0:T(128)} %pad_add_fusion.1.place, s32[4,1,640]{2,1,0:T(1,128)} %broadcast_in_dim.67.ids_row, bf16[256,1536]{1,0:T(8,128)(2,1)} %get-tuple-element.40.table, bf16[512,256]{1,0:T(8,128)(2,1)} %get-tuple-element.49.key_table, ...), custom_call_target="tpu_custom_call" | custom-call | flops 1 | tf_op jit(solution)/shard_map/pallas_call | solution.py:443
  139.4 1.6 collective-permute-start.7
  141.0 2.7 collective-permute-done.7
  143.7 2.3 collective-permute-start.8
  146.0 1.2 convert_add_fusion.4
  147.2 1.6 collective-permute-start.15
  149.0 1.9 collective-permute-start.9
  150.9 2.8 %collective-permute-done.15 = bf16[256,512]{1,0:T(8,128)(2,1)S(1)} collective-permute-done((bf16[256,512]{1,0:T(8,128)(2,1)S(1)}, bf16[256,512]{1,0:T(8,128)(2,1)S(1)}, u32[]{:S(2)}, u32[]{:S(2)}) %collective-permute-start.15) | collective-permute-done | bytes 262176 | tf_op jit(solution)/shard_map/ppermute | solution.py:537
  153.8 1.5 collective-permute-start.16
  156.0 1.7 collective-permute-start.10
  157.7 1.1 collective-permute-done.16
  158.9 1.7 collective-permute-start.17
  161.0 1.6 collective-permute-start.25
  163.1 0.9 collective-permute-start.30
  164.8 5.5 %collective-permute-done.25 = bf16[512,512]{1,0:T(8,128)(2,1)S(1)} collective-permute-done((bf16[512,512]{1,0:T(8,128)(2,1)S(1)}, bf16[512,512]{1,0:T(8,128)(2,1)S(1)}, u32[]{:S(2)}, u32[]{:S(2)}) %collective-permute-start.25) | collective-permute-done | bytes 524320 | tf_op jit(solution)/shard_map/ppermute | solution.py:537
  170.5 1.5 collective-permute-start.26
  171.9 5.5 %collective-permute-done.30 = bf16[656,512]{1,0:T(8,128)(2,1)S(1)} collective-permute-done((bf16[656,512]{1,0:T(8,128)(2,1)S(1)}, bf16[656,512]{1,0:T(8,128)(2,1)S(1)}, u32[]{:S(2)}, u32[]{:S(2)}) %collective-permute-start.30) | collective-permute-done | bytes 671776 | tf_op jit(solution)/shard_map/ppermute | solution.py:537
  177.8 1.5 collective-permute-start.31
  179.8 5.3 %collective-permute-done.31 = bf16[336,512]{1,0:T(8,128)(2,1)S(1)} collective-permute-done((bf16[336,512]{1,0:T(8,128)(2,1)S(1)}, bf16[336,512]{1,0:T(8,128)(2,1)S(1)}, u32[]{:S(2)}, u32[]{:S(2)}) %collective-permute-start.31) | collective-permute-done | bytes 344096 | tf_op jit(solution)/shard_map/ppermute | solution.py:537
  186.6 5.1 %collective-permute-done.32 = bf16[176,512]{1,0:T(8,128)(2,1)S(1)} collective-permute-done((bf16[176,512]{1,0:T(8,128)(2,1)S(1)}, bf16[176,512]{1,0:T(8,128)(2,1)S(1)}, u32[]{:S(2)}, u32[]{:S(2)}) %collective-permute-start.32) | collective-permute-done | bytes 180256 | tf_op jit(solution)/shard_map/ppermute | solution.py:537
  192.5 6.4 %collective-permute-done.33 = bf16[96,512]{1,0:T(8,128)(2,1)S(1)} collective-permute-done((bf16[96,512]{1,0:T(8,128)(2,1)S(1)}, bf16[96,512]{1,0:T(8,128)(2,1)S(1)}, u32[]{:S(2)}, u32[]{:S(2)}) %collective-permute-start.33) | collective-permute-done | bytes 98336 | tf_op jit(solution)/shard_map/ppermute | solution.py:537
  199.1 3.0 %collective-permute-start.19 = (bf16[32,512]{1,0:T(8,128)(2,1)S(1)}, bf16[32,512]{1,0:T(8,128)(2,1)S(1)}, u32[]{:S(2)}, u32[]{:S(2)}) collective-permute-start(bf16[32,512]{1,0:T(8,128)(2,1)S(1)} %get-tuple-element.72), channel_id=1, source_target_pairs={{0,4},{1,5},{2,6},{3,7},{4,0},{5,1},{6,2},{7,3},{8,12},{9,13},{10,... | collective-permute-start | bytes 98312 | tf_op jit(solution)/shard_map/ppermute | solution.py:537
  202.0 3.5 %collective-permute-done.34 = bf16[144,512]{1,0:T(8,128)(2,1)S(1)} collective-permute-done((bf16[144,512]{1,0:T(8,128)(2,1)S(1)}, bf16[144,512]{1,0:T(8,128)(2,1)S(1)}, u32[]{:S(2)}, u32[]{:S(2)}) %collective-permute-start.34) | collective-permute-done | bytes 147488 | tf_op jit(solution)/shard_map/ppermute | solution.py:537
  205.9 1.9 collective-permute-start.20
  207.9 7.7 %collective-permute-done.35 = bf16[288,512]{1,0:T(8,128)(2,1)S(1)} collective-permute-done((bf16[288,512]{1,0:T(8,128)(2,1)S(1)}, bf16[288,512]{1,0:T(8,128)(2,1)S(1)}, u32[]{:S(2)}, u32[]{:S(2)}) %collective-permute-start.35) | collective-permute-done | bytes 294944 | tf_op jit(solution)/shard_map/ppermute | solution.py:537
  215.6 1.4 collective-permute-start.36
  217.1 1.3 collective-permute-start.21
  218.4 0.8 collective-permute-start.11
  219.3 14.0 %collective-permute-done.21 = bf16[128,512]{1,0:T(8,128)(2,1)S(1)} collective-permute-done((bf16[128,512]{1,0:T(8,128)(2,1)S(1)}, bf16[128,512]{1,0:T(8,128)(2,1)S(1)}, u32[]{:S(2)}, u32[]{:S(2)}) %collective-permute-start.21) | collective-permute-done | bytes 131104 | tf_op jit(solution)/shard_map/ppermute | solution.py:537
  233.4 2.5 collective-permute-start.22
  236.2 4.0 %collective-permute-done.22 = bf16[256,512]{1,0:T(8,128)(2,1)S(1)} collective-permute-done((bf16[256,512]{1,0:T(8,128)(2,1)S(1)}, bf16[256,512]{1,0:T(8,128)(2,1)S(1)}, u32[]{:S(2)}, u32[]{:S(2)}) %collective-permute-start.22) | collective-permute-done | bytes 262176 | tf_op jit(solution)/shard_map/ppermute | solution.py:537
  240.4 0.9 convert_multiply_fusion
  241.4 0.8 collective-permute-done.23
  242.6 10.3 %collective-permute-done.37 = bf16[1152,512]{1,0:T(8,128)(2,1)S(1)} collective-permute-done((bf16[1152,512]{1,0:T(8,128)(2,1)S(1)}, bf16[1152,512]{1,0:T(8,128)(2,1)S(1)}, u32[]{:S(2)}, u32[]{:S(2)}) %collective-permute-start.37) | collective-permute-done | bytes 1179680 | tf_op jit(solution)/shard_map/ppermute | solution.py:537
  253.2 1.3 fusion.9
  254.4 1.1 fusion.8
  255.5 2.3 fusion.11
  260.2 0.9 bitcast_convert_fusion
  261.1 1.6 fusion.23
  262.7 2.7 %bitcast_convert_fusion.1 = f32[2048,512]{1,0:T(8,128)} fusion(bf16[32,64,512]{2,1,0:T(8,128)(2,1)S(1)} %slice.169), kind=kLoop, calls=%fused_computation.3 | loop fusion | flops 1048576 | bytes 6291456 | tf_op jit(solution)/shard_map/convert_element_type | solution.py:775
  265.4 2.4 pad_maximum_fusion
  (155 shorter events, 14.0 us)
Async XLA Ops:
  0.6 13.7 %copy-start.8 = (s32[4,512]{1,0:T(4,128)S(1)}, s32[4,512]{1,0:T(4,128)}, u32[]{:S(2)}) copy-start(s32[4,512]{1,0:T(4,128)} %param.16) | copy-start | bytes 24580
  1.5 12.8 %collective-permute-start = (s32[4,64]{1,0:T(4,128)S(1)}, s32[4,64]{1,0:T(4,128)S(1)}, u32[]{:S(2)}, u32[]{:S(2)}) collective-permute-start(s32[4,64]{1,0:T(4,128)S(1)} %get-tuple-element.101), channel_id=1, source_target_pairs={{0,1},{1,2},{2,3},{3,4},{4,5},{5,6},{6,7},{8,9},{9,10},{10,11},{11... | collective-permute-start | bytes 3080 | tf_op jit(solution)/shard_map/ppermute | solution.py:603
  6.3 8.0 %collective-permute-start.1 = (s32[4,64]{1,0:T(4,128)S(1)}, s32[4,64]{1,0:T(4,128)S(1)}, u32[]{:S(2)}, u32[]{:S(2)}) collective-permute-start(s32[4,64]{1,0:T(4,128)S(1)} %get-tuple-element.102), channel_id=1, source_target_pairs={{1,0},{2,1},{3,2},{4,3},{5,4},{6,5},{7,6},{9,8},{10,9},{11,10},{12... | collective-permute-start | bytes 3080 | tf_op jit(solution)/shard_map/ppermute | solution.py:605
  49.9 4.2 %collective-permute-start.2 = (f32[4]{0:T(128)S(1)}, f32[4]{0:T(128)S(1)}, u32[]{:S(2)}, u32[]{:S(2)}) collective-permute-start(f32[4]{0:T(128)S(1)} %slice_reduce_fusion), channel_id=1, source_target_pairs={{0,1},{1,0},{2,3},{3,2},{4,5},{5,4},{6,7},{7,6},{8,9},{9,8},{10,11... | collective-permute-start | bytes 56 | tf_op jit(solution)/shard_map/ppermute | solution.py:478
  54.1 4.5 %collective-permute-start.3 = (f32[4]{0:T(128)S(1)}, f32[4]{0:T(128)S(1)}, u32[]{:S(2)}, u32[]{:S(2)}) collective-permute-start(f32[4]{0:T(128)S(1)} %add.271), channel_id=1, source_target_pairs={{0,2},{1,3},{2,0},{3,1},{4,6},{5,7},{6,4},{7,5},{8,10},{9,11},{10,... | collective-permute-start | bytes 56 | tf_op jit(solution)/shard_map/ppermute | solution.py:478
  58.6 4.5 %collective-permute-start.4 = (f32[4]{0:T(128)S(1)}, f32[4]{0:T(128)S(1)}, u32[]{:S(2)}, u32[]{:S(2)}) collective-permute-start(f32[4]{0:T(128)S(1)} %add.273), channel_id=1, source_target_pairs={{0,4},{1,5},{2,6},{3,7},{4,0},{5,1},{6,2},{7,3},{8,12},{9,13},{10,... | collective-permute-start | bytes 56 | tf_op jit(solution)/shard_map/ppermute | solution.py:478
  67.1 6.2 %collective-permute-start.5 = (f32[4,8,64]{2,1,0:T(8,128)}, f32[4,8,64]{2,1,0:T(8,128)S(1)}, u32[]{:S(2)}, u32[]{:S(2)}) collective-permute-start(f32[4,8,64]{2,1,0:T(8,128)} %shard_map.257), channel_id=1, source_target_pairs={{0,1},{1,0},{2,3},{3,2},{4,5},{5,4},{6,7},{7,6},{8,9},{9,8},{10,11... | collective-permute-start | bytes 24584 | tf_op jit(solution)/shard_map/ppermute | solution.py:478
  68.7 4.6 %copy-start.7 = (f32[4,8,64]{2,1,0:T(8,128)S(1)}, f32[4,8,64]{2,1,0:T(8,128)}, u32[]{:S(2)}) copy-start(f32[4,8,64]{2,1,0:T(8,128)} %shard_map.257) | copy-start | bytes 24580
  73.4 3.8 %collective-permute-start.12 = (f32[4,8,64]{2,1,0:T(8,128)S(1)}, f32[4,8,64]{2,1,0:T(8,128)S(1)}, u32[]{:S(2)}, u32[]{:S(2)}) collective-permute-start(f32[4,8,64]{2,1,0:T(8,128)S(1)} %add.276), channel_id=1, source_target_pairs={{0,2},{1,3},{2,0},{3,1},{4,6},{5,7},{6,4},{7,5},{8,10},{9,11},{10,... | collective-permute-start | bytes 24584 | tf_op jit(solution)/shard_map/ppermute | solution.py:478
  77.2 5.0 %collective-permute-start.13 = (f32[4,8,64]{2,1,0:T(8,128)S(1)}, f32[4,8,64]{2,1,0:T(8,128)S(1)}, u32[]{:S(2)}, u32[]{:S(2)}) collective-permute-start(f32[4,8,64]{2,1,0:T(8,128)S(1)} %add.283), channel_id=1, source_target_pairs={{0,4},{1,5},{2,6},{3,7},{4,0},{5,1},{6,2},{7,3},{8,12},{9,13},{10,... | collective-permute-start | bytes 24584 | tf_op jit(solution)/shard_map/ppermute | solution.py:478
  80.7 58.6 %collective-permute-start.6 = (bf16[128,512]{1,0:T(8,128)(2,1)S(1)}, bf16[128,512]{1,0:T(8,128)(2,1)S(1)}, u32[]{:S(2)}, u32[]{:S(2)}) collective-permute-start(bf16[128,512]{1,0:T(8,128)(2,1)S(1)} %dynamic-slice_convert_fusion.8), channel_id=1, source_target_pairs={{0,1},{1,0},{2,3},{3,2},{4,5},{5,4},{6,7},{7,6},{8,9},{9,8},{10,11... | collective-permute-start | bytes 393224 | tf_op jit(solution)/shard_map/ppermute | solution.py:497
  118.1 21.2 %copy-start.1 = (f32[4,64,512]{2,1,0:T(8,128)S(1)}, f32[4,64,512]{2,1,0:T(8,128)}, u32[]{:S(2)}) copy-start(f32[4,64,512]{2,1,0:T(8,128)} %shard_map.258) | copy-start | bytes 1572868
  118.1 42.5 %collective-permute-start.24 = (bf16[1024,512]{1,0:T(8,128)(2,1)}, bf16[1024,512]{1,0:T(8,128)(2,1)S(1)}, u32[]{:S(2)}, u32[]{:S(2)}) collective-permute-start(bf16[1024,512]{1,0:T(8,128)(2,1)} %get-tuple-element.63), channel_id=1, source_target_pairs={{0,8},{1,9},{2,10},{3,11},{4,12},{5,13},{6,14},{7,15},{8,0},{9,1},... | collective-permute-start | bytes 3145736 | tf_op jit(solution)/shard_map/ppermute | solution.py:537
  118.2 22.8 %copy-start.9 = (f32[8,512]{1,0:T(8,128)S(1)}, f32[8,512]{1,0:T(8,128)}, u32[]{:S(2)}) copy-start(f32[8,512]{1,0:T(8,128)} %get-tuple-element.66) | copy-start | bytes 49156
  138.9 9.9 %copy-start.4 = (bf16[1280,512]{1,0:T(8,128)(2,1)S(1)}, bf16[1280,512]{1,0:T(8,128)(2,1)}, u32[]{:S(2)}) copy-start(bf16[1280,512]{1,0:T(8,128)(2,1)} %get-tuple-element.65) | copy-start | bytes 3932164
  138.9 7.1 %collective-permute-start.14 = (bf16[512,512]{1,0:T(8,128)(2,1)}, bf16[512,512]{1,0:T(8,128)(2,1)S(1)}, u32[]{:S(2)}, u32[]{:S(2)}) collective-permute-start(bf16[512,512]{1,0:T(8,128)(2,1)} %get-tuple-element.60), channel_id=1, source_target_pairs={{0,8},{1,9},{2,10},{3,11},{4,12},{5,13},{6,14},{7,15},{8,0},{9,1},... | collective-permute-start | bytes 1572872 | tf_op jit(solution)/shard_map/ppermute | solution.py:537
  139.4 4.3 %collective-permute-start.7 = (bf16[64,512]{1,0:T(8,128)(2,1)S(1)}, bf16[64,512]{1,0:T(8,128)(2,1)S(1)}, u32[]{:S(2)}, u32[]{:S(2)}) collective-permute-start(bf16[64,512]{1,0:T(8,128)(2,1)S(1)} %dynamic-slice_convert_fusion.12), channel_id=1, source_target_pairs={{0,2},{1,3},{2,0},{3,1},{4,6},{5,7},{6,4},{7,5},{8,10},{9,11},{10,... | collective-permute-start | bytes 196616 | tf_op jit(solution)/shard_map/ppermute | solution.py:497
  143.7 5.2 %collective-permute-start.8 = (bf16[32,512]{1,0:T(8,128)(2,1)S(1)}, bf16[32,512]{1,0:T(8,128)(2,1)S(1)}, u32[]{:S(2)}, u32[]{:S(2)}) collective-permute-start(bf16[32,512]{1,0:T(8,128)(2,1)S(1)} %dynamic-slice_convert_fusion.14), channel_id=1, source_target_pairs={{0,4},{1,5},{2,6},{3,7},{4,0},{5,1},{6,2},{7,3},{8,12},{9,13},{10,... | collective-permute-start | bytes 98312 | tf_op jit(solution)/shard_map/ppermute | solution.py:497
  147.2 6.4 %collective-permute-start.15 = (bf16[256,512]{1,0:T(8,128)(2,1)S(1)}, bf16[256,512]{1,0:T(8,128)(2,1)S(1)}, u32[]{:S(2)}, u32[]{:S(2)}) collective-permute-start(bf16[256,512]{1,0:T(8,128)(2,1)S(1)} %dynamic-slice_convert_fusion.4), channel_id=1, source_target_pairs={{0,16},{1,17},{2,18},{3,19},{4,20},{5,21},{6,22},{7,23},{8,9},{9,8... | collective-permute-start | bytes 786440 | tf_op jit(solution)/shard_map/ppermute | solution.py:537
  148.8 11.8 %copy-start.5 = (bf16[1024,512]{1,0:T(8,128)(2,1)S(1)}, bf16[1024,512]{1,0:T(8,128)(2,1)}, u32[]{:S(2)}) copy-start(bf16[1024,512]{1,0:T(8,128)(2,1)} %get-tuple-element.62) | copy-start | bytes 3145732
  148.9 13.7 %collective-permute-start.29 = (bf16[1296,512]{1,0:T(8,128)(2,1)S(1)}, bf16[1296,512]{1,0:T(8,128)(2,1)S(1)}, u32[]{:S(2)}, u32[]{:S(2)}) collective-permute-start(bf16[1296,512]{1,0:T(8,128)(2,1)S(1)} %pad_maximum_fusion.1), channel_id=1, source_target_pairs={{0,8},{1,9},{2,10},{3,11},{4,12},{5,13},{6,14},{7,15},{8,0},{9,1},... | collective-permute-start | bytes 3981320 | tf_op jit(solution)/shard_map/ppermute | solution.py:537
  149.0 7.0 %collective-permute-start.9 = (bf16[32,512]{1,0:T(8,128)(2,1)S(1)}, bf16[32,512]{1,0:T(8,128)(2,1)S(1)}, u32[]{:S(2)}, u32[]{:S(2)}) collective-permute-start(bf16[32,512]{1,0:T(8,128)(2,1)S(1)} %get-tuple-element.74), channel_id=1, source_target_pairs={{0,4},{1,5},{2,6},{3,7},{4,0},{5,1},{6,2},{7,3},{8,12},{9,13},{10,... | collective-permute-start | bytes 98312 | tf_op jit(solution)/shard_map/ppermute | solution.py:500
  153.8 5.0 %collective-permute-start.16 = (bf16[128,512]{1,0:T(8,128)(2,1)S(1)}, bf16[128,512]{1,0:T(8,128)(2,1)S(1)}, u32[]{:S(2)}, u32[]{:S(2)}) collective-permute-start(bf16[128,512]{1,0:T(8,128)(2,1)S(1)} %dynamic-slice_convert_fusion.7), channel_id=1, source_target_pairs={{0,1},{1,0},{2,3},{3,2},{4,5},{5,4},{6,7},{7,6},{8,10},{9,11},{10,... | collective-permute-start | bytes 393224 | tf_op jit(solution)/shard_map/ppermute | solution.py:537
  156.0 62.4 %collective-permute-start.10 = (bf16[64,512]{1,0:T(8,128)(2,1)S(1)}, bf16[64,512]{1,0:T(8,128)(2,1)S(1)}, u32[]{:S(2)}, u32[]{:S(2)}) collective-permute-start(bf16[64,512]{1,0:T(8,128)(2,1)S(1)} %constant_dynamic-update-slice_fusion.24), channel_id=1, source_target_pairs={{0,2},{1,3},{2,0},{3,1},{4,6},{5,7},{6,4},{7,5},{8,10},{9,11},{10,... | collective-permute-start | bytes 196616 | tf_op jit(solution)/shard_map/ppermute | solution.py:500
  158.9 5.1 %collective-permute-start.17 = (bf16[64,512]{1,0:T(8,128)(2,1)S(1)}, bf16[64,512]{1,0:T(8,128)(2,1)S(1)}, u32[]{:S(2)}, u32[]{:S(2)}) collective-permute-start(bf16[64,512]{1,0:T(8,128)(2,1)S(1)} %dynamic-slice_convert_fusion.11), channel_id=1, source_target_pairs={{0,2},{1,3},{2,0},{3,1},{4,6},{5,7},{6,4},{7,5},{8,24},{9,25},{10,... | collective-permute-start | bytes 196616 | tf_op jit(solution)/shard_map/ppermute | solution.py:537
  160.6 2.0 copy-start.3
  161.0 9.2 %collective-permute-start.25 = (bf16[512,512]{1,0:T(8,128)(2,1)S(1)}, bf16[512,512]{1,0:T(8,128)(2,1)S(1)}, u32[]{:S(2)}, u32[]{:S(2)}) collective-permute-start(bf16[512,512]{1,0:T(8,128)(2,1)S(1)} %dynamic-slice_convert_fusion.1), channel_id=1, source_target_pairs={{0,16},{1,17},{2,18},{3,19},{4,20},{5,21},{6,22},{7,23},{8,9},{9,8... | collective-permute-start | bytes 1572872 | tf_op jit(solution)/shard_map/ppermute | solution.py:537
  163.1 14.3 %collective-permute-start.30 = (bf16[656,512]{1,0:T(8,128)(2,1)S(1)}, bf16[656,512]{1,0:T(8,128)(2,1)S(1)}, u32[]{:S(2)}, u32[]{:S(2)}) collective-permute-start(bf16[656,512]{1,0:T(8,128)(2,1)S(1)} %pad_maximum_fusion.3), channel_id=1, source_target_pairs={{0,16},{1,17},{2,18},{3,19},{4,20},{5,21},{6,22},{7,23},{8,9},{9,8... | collective-permute-start | bytes 2015240 | tf_op jit(solution)/shard_map/ppermute | solution.py:537
  164.1 35.0 %collective-permute-start.18 = (bf16[32,512]{1,0:T(8,128)(2,1)S(1)}, bf16[32,512]{1,0:T(8,128)(2,1)S(1)}, u32[]{:S(2)}, u32[]{:S(2)}) collective-permute-start(bf16[32,512]{1,0:T(8,128)(2,1)S(1)} %dynamic-slice_convert_fusion.13), channel_id=1, source_target_pairs={{0,4},{1,5},{2,6},{3,7},{4,0},{5,1},{6,2},{7,3},{8,12},{9,13},{10,... | collective-permute-start | bytes 98312 | tf_op jit(solution)/shard_map/ppermute | solution.py:537
  170.5 8.8 %collective-permute-start.26 = (bf16[256,512]{1,0:T(8,128)(2,1)S(1)}, bf16[256,512]{1,0:T(8,128)(2,1)S(1)}, u32[]{:S(2)}, u32[]{:S(2)}) collective-permute-start(bf16[256,512]{1,0:T(8,128)(2,1)S(1)} %dynamic-slice_convert_fusion.3), channel_id=1, source_target_pairs={{0,1},{1,0},{2,3},{3,2},{4,5},{5,4},{6,7},{7,6},{8,10},{9,11},{10,... | collective-permute-start | bytes 786440 | tf_op jit(solution)/shard_map/ppermute | solution.py:537
  177.8 7.3 %collective-permute-start.31 = (bf16[336,512]{1,0:T(8,128)(2,1)S(1)}, bf16[336,512]{1,0:T(8,128)(2,1)S(1)}, u32[]{:S(2)}, u32[]{:S(2)}) collective-permute-start(bf16[336,512]{1,0:T(8,128)(2,1)S(1)} %pad_maximum_fusion.4), channel_id=1, source_target_pairs={{0,1},{1,0},{2,3},{3,2},{4,5},{5,4},{6,7},{7,6},{8,10},{9,11},{10,... | collective-permute-start | bytes 1032200 | tf_op jit(solution)/shard_map/ppermute | solution.py:537
  179.4 6.4 %collective-permute-start.27 = (bf16[128,512]{1,0:T(8,128)(2,1)S(1)}, bf16[128,512]{1,0:T(8,128)(2,1)S(1)}, u32[]{:S(2)}, u32[]{:S(2)}) collective-permute-start(bf16[128,512]{1,0:T(8,128)(2,1)S(1)} %dynamic-slice_convert_fusion.6), channel_id=1, source_target_pairs={{0,2},{1,3},{2,0},{3,1},{4,6},{5,7},{6,4},{7,5},{8,24},{9,25},{10,... | collective-permute-start | bytes 393224 | tf_op jit(solution)/shard_map/ppermute | solution.py:537
  185.3 6.4 %collective-permute-start.32 = (bf16[176,512]{1,0:T(8,128)(2,1)S(1)}, bf16[176,512]{1,0:T(8,128)(2,1)S(1)}, u32[]{:S(2)}, u32[]{:S(2)}) collective-permute-start(bf16[176,512]{1,0:T(8,128)(2,1)S(1)} %pad_maximum_fusion.7), channel_id=1, source_target_pairs={{0,2},{1,3},{2,0},{3,1},{4,6},{5,7},{6,4},{7,5},{8,24},{9,25},{10,... | collective-permute-start | bytes 540680 | tf_op jit(solution)/shard_map/ppermute | solution.py:537
  185.8 6.6 %collective-permute-start.28 = (bf16[64,512]{1,0:T(8,128)(2,1)S(1)}, bf16[64,512]{1,0:T(8,128)(2,1)S(1)}, u32[]{:S(2)}, u32[]{:S(2)}) collective-permute-start(bf16[64,512]{1,0:T(8,128)(2,1)S(1)} %dynamic-slice_convert_fusion.10), channel_id=1, source_target_pairs={{0,4},{1,5},{2,6},{3,7},{4,0},{5,1},{6,2},{7,3},{8,12},{9,13},{10,... | collective-permute-start | bytes 196616 | tf_op jit(solution)/shard_map/ppermute | solution.py:537
  191.8 7.1 %collective-permute-start.33 = (bf16[96,512]{1,0:T(8,128)(2,1)S(1)}, bf16[96,512]{1,0:T(8,128)(2,1)S(1)}, u32[]{:S(2)}, u32[]{:S(2)}) collective-permute-start(bf16[96,512]{1,0:T(8,128)(2,1)S(1)} %pad_maximum_fusion.9), channel_id=1, source_target_pairs={{0,4},{1,5},{2,6},{3,7},{4,0},{5,1},{6,2},{7,3},{8,12},{9,13},{10,... | collective-permute-start | bytes 294920 | tf_op jit(solution)/shard_map/ppermute | solution.py:537
  198.9 6.6 %collective-permute-start.34 = (bf16[144,512]{1,0:T(8,128)(2,1)S(1)}, bf16[144,512]{1,0:T(8,128)(2,1)S(1)}, u32[]{:S(2)}, u32[]{:S(2)}) collective-permute-start(bf16[144,512]{1,0:T(8,128)(2,1)S(1)} %get-tuple-element.91), channel_id=1, source_target_pairs={{0,4},{1,5},{2,6},{3,7},{4,0},{5,1},{6,2},{7,3},{8,12},{9,13},{10,... | collective-permute-start | bytes 442376 | tf_op jit(solution)/shard_map/ppermute | solution.py:537
  199.1 6.9 %collective-permute-start.19 = (bf16[32,512]{1,0:T(8,128)(2,1)S(1)}, bf16[32,512]{1,0:T(8,128)(2,1)S(1)}, u32[]{:S(2)}, u32[]{:S(2)}) collective-permute-start(bf16[32,512]{1,0:T(8,128)(2,1)S(1)} %get-tuple-element.72), channel_id=1, source_target_pairs={{0,4},{1,5},{2,6},{3,7},{4,0},{5,1},{6,2},{7,3},{8,12},{9,13},{10,... | collective-permute-start | bytes 98312 | tf_op jit(solution)/shard_map/ppermute | solution.py:537
  205.6 10.0 %collective-permute-start.35 = (bf16[288,512]{1,0:T(8,128)(2,1)S(1)}, bf16[288,512]{1,0:T(8,128)(2,1)S(1)}, u32[]{:S(2)}, u32[]{:S(2)}) collective-permute-start(bf16[288,512]{1,0:T(8,128)(2,1)S(1)} %constant_dynamic-update-slice_fusion.8), channel_id=1, source_target_pairs={{0,2},{1,3},{2,0},{3,1},{4,6},{5,7},{6,4},{7,5},{8,24},{9,25},{10,... | collective-permute-start | bytes 884744 | tf_op jit(solution)/shard_map/ppermute | solution.py:537
  205.9 11.1 %collective-permute-start.20 = (bf16[64,512]{1,0:T(8,128)(2,1)S(1)}, bf16[64,512]{1,0:T(8,128)(2,1)S(1)}, u32[]{:S(2)}, u32[]{:S(2)}) collective-permute-start(bf16[64,512]{1,0:T(8,128)(2,1)S(1)} %constant_dynamic-update-slice_fusion.18), channel_id=1, source_target_pairs={{0,2},{1,3},{2,0},{3,1},{4,6},{5,7},{6,4},{7,5},{8,24},{9,25},{10,... | collective-permute-start | bytes 196616 | tf_op jit(solution)/shard_map/ppermute | solution.py:537
  215.6 20.4 %collective-permute-start.36 = (bf16[576,512]{1,0:T(8,128)(2,1)S(1)}, bf16[576,512]{1,0:T(8,128)(2,1)S(1)}, u32[]{:S(2)}, u32[]{:S(2)}) collective-permute-start(bf16[576,512]{1,0:T(8,128)(2,1)S(1)} %constant_dynamic-update-slice_fusion.6), channel_id=1, source_target_pairs={{0,1},{1,0},{2,3},{3,2},{4,5},{5,4},{6,7},{7,6},{8,10},{9,11},{10,... | collective-permute-start | bytes 1769480 | tf_op jit(solution)/shard_map/ppermute | solution.py:537
  217.1 16.3 %collective-permute-start.21 = (bf16[128,512]{1,0:T(8,128)(2,1)S(1)}, bf16[128,512]{1,0:T(8,128)(2,1)S(1)}, u32[]{:S(2)}, u32[]{:S(2)}) collective-permute-start(bf16[128,512]{1,0:T(8,128)(2,1)S(1)} %constant_dynamic-update-slice_fusion.16), channel_id=1, source_target_pairs={{0,1},{1,0},{2,3},{3,2},{4,5},{5,4},{6,7},{7,6},{8,10},{9,11},{10,... | collective-permute-start | bytes 393224 | tf_op jit(solution)/shard_map/ppermute | solution.py:537
  218.4 22.0 %collective-permute-start.11 = (bf16[128,512]{1,0:T(8,128)(2,1)S(1)}, bf16[128,512]{1,0:T(8,128)(2,1)S(1)}, u32[]{:S(2)}, u32[]{:S(2)}) collective-permute-start(bf16[128,512]{1,0:T(8,128)(2,1)S(1)} %constant_dynamic-update-slice_fusion.22), channel_id=1, source_target_pairs={{0,1},{1,0},{2,3},{3,2},{4,5},{5,4},{6,7},{7,6},{8,9},{9,8},{10,11... | collective-permute-start | bytes 393224 | tf_op jit(solution)/shard_map/ppermute | solution.py:500
  233.4 6.9 %collective-permute-start.22 = (bf16[256,512]{1,0:T(8,128)(2,1)S(1)}, bf16[256,512]{1,0:T(8,128)(2,1)S(1)}, u32[]{:S(2)}, u32[]{:S(2)}) collective-permute-start(bf16[256,512]{1,0:T(8,128)(2,1)S(1)} %constant_dynamic-update-slice_fusion.14), channel_id=1, source_target_pairs={{0,16},{1,17},{2,18},{3,19},{4,20},{5,21},{6,22},{7,23},{8,9},{9,8... | collective-permute-start | bytes 786440 | tf_op jit(solution)/shard_map/ppermute | solution.py:537
  236.1 16.8 %collective-permute-start.37 = (bf16[1152,512]{1,0:T(8,128)(2,1)S(1)}, bf16[1152,512]{1,0:T(8,128)(2,1)S(1)}, u32[]{:S(2)}, u32[]{:S(2)}) collective-permute-start(bf16[1152,512]{1,0:T(8,128)(2,1)S(1)} %constant_dynamic-update-slice_fusion.4), channel_id=1, source_target_pairs={{0,16},{1,17},{2,18},{3,19},{4,20},{5,21},{6,22},{7,23},{8,9},{9,8... | collective-permute-start | bytes 3538952 | tf_op jit(solution)/shard_map/ppermute | solution.py:537
  240.2 2.0 collective-permute-start.23
  242.6 10.6 %copy-start = (bf16[256,512]{1,0:T(8,128)(2,1)S(1)}, bf16[256,512]{1,0:T(8,128)(2,1)}, u32[]{:S(2)}) copy-start(bf16[256,512]{1,0:T(8,128)(2,1)} %embed.3) | copy-start | bytes 786436
  242.6 10.6 %copy-start.2 = (bf16[512,1536]{1,0:T(8,128)(2,1)S(1)}, bf16[512,1536]{1,0:T(8,128)(2,1)}, u32[]{:S(2)}) copy-start(bf16[512,1536]{1,0:T(8,128)(2,1)} %weight.1) | copy-start | bytes 4718596
  242.6 10.6 %copy-start.10 = (f32[512]{0:T(512)S(1)}, f32[512]{0:T(512)}, u32[]{:S(2)}) copy-start(f32[512]{0:T(512)} %param.20) | copy-start | bytes 6148
  253.0 6.6 %collective-permute-start.38 = (bf16[2304,512]{1,0:T(8,128)(2,1)S(1)}, bf16[2304,512]{1,0:T(8,128)(2,1)S(1)}, u32[]{:S(2)}, u32[]{:S(2)}) collective-permute-start(bf16[2304,512]{1,0:T(8,128)(2,1)S(1)} %constant_dynamic-update-slice_fusion.2), channel_id=1, source_target_pairs={{0,8},{1,9},{2,10},{3,11},{4,12},{5,13},{6,14},{7,15},{8,0},{9,1},... | collective-permute-start | bytes 7077896 | tf_op jit(solution)/shard_map/ppermute | solution.py:537
  253.2 2.4 copy-start.6

commit v3 on v2

--- a/solution.py
+++ b/solution.py
@@ -119,20 +119,29 @@
             stack_out[item, at * STACK + NB : (at + 1) * STACK] = rim
 
 
+def take_turns(*parts):
+    parts = list(parts)
+    while parts:
+        for part in list(parts):
+            if next(part, None) is None:
+                parts.remove(part)
+
+
 def forward_kernel(
     place, lengths, ids_row, table, value_table, embed, out_weight, gain, shift,
     up_weight, up_bias, down_weight, down_bias, cot_stack,
     attended_out, log_out, middle_out, normed_out, act_out, slope_out, high_out, low_out,
     inner_out, frontier_out, running_out,
-    bias, query_keys, value_columns, triangle,
+    bias, query_keys, value_columns, triangle, held_hot, held_attended,
 ):
-    item = pl.program_id(0)
+    step = pl.program_id(0)
+    items = pl.num_programs(0) - 1
     span = middle_out.shape[1]
     model_width = middle_out.shape[2]
     vocab = embed.shape[0]
     hidden_width = up_weight.shape[1]
 
-    @pl.when(item == 0)
+    @pl.when(step == 0)
     def _():
         for at, tile in enumerate(window_bias(place[1], place[2])):
             bias[at] = tile
@@ -140,64 +149,91 @@
             iota((span, span), 0) <= iota((span, span), 1), 1.0, 0.0
         ).astype(BF16)
 
-    hot_columns = one_hot_columns(ids_row[0], vocab)
-    hot = hot_columns.T
-    query_keys[...] = dot(hot, table[:, : 2 * model_width]).astype(BF16)
-    value_columns[...] = dot(value_table[...], hot_columns).astype(BF16)
-    tiles = span // TILE
-    pairs = H // 2
-    for tile in range(tiles):
-        begin = tile * TILE
-        window = slice(begin, begin + SPAN_KEYS)
-        tile_bias = bias[0 if tile == 0 else (2 if tile == tiles - 1 else 1)]
-        lanes = [slice(pair * PAIR, (pair + 1) * PAIR) for pair in range(pairs)]
-        scores = []
-        for pair in range(pairs):
-            key_lanes = slice(model_width + pair * PAIR, model_width + (pair + 1) * PAIR)
-            query_block = head_blocks(query_keys[begin + WIN : begin + WIN + TILE, lanes[pair]])
-            scores.append(dot_last(query_keys[window, key_lanes], query_block) + tile_bias)
-        probs = []
-        for pair in range(pairs):
-            peak = jnp.max(scores[pair], 0, keepdims=True)
-            weights = jnp.exp(scores[pair] - peak)
-            weight_sum = jnp.sum(weights, 0, keepdims=True)
-            probs.append((weights * pltpu.reciprocal(weight_sum, approx=True)).astype(BF16))
-            at = tile * pairs + pair
-            log_out[0, at : at + 1, :] = peak + jnp.log(weight_sum)
-        mixed = [dot(value_columns[lanes[pair], window], probs[pair]) for pair in range(pairs)]
-        for pair in range(pairs):
-            attended_out[0, begin : begin + TILE, lanes[pair]] = (
-                head_columns(mixed[pair]).T.astype(BF16)
-            )
-    middle = dot(hot[WIN : WIN + span], embed[...]) + dot(attended_out[0], out_weight[...])
-    middle_out[0] = middle
-    centered = middle - jnp.mean(middle, -1, keepdims=True)
-    variance = jnp.mean(centered * centered, -1, keepdims=True)
-    normed = (centered * lax.rsqrt(variance + eps) * gain[...] + shift[...]).astype(BF16)
-    normed_out[0] = normed
-    chunk = 512
-    cuts = [slice(begin, begin + chunk) for begin in range(0, hidden_width, chunk)]
-    hidden = middle + down_bias[...]
-    preact = dot(normed, up_weight[:, cuts[0]]) + up_bias[:, cuts[0]]
-    for at, cells in enumerate(cuts):
-        held = preact
-        if at + 1 < len(cuts):
-            preact = dot(normed, up_weight[:, cuts[at + 1]]) + up_bias[:, cuts[at + 1]]
-        act, slope = gelu_with_slope(held)
-        act = act.astype(BF16)
-        act_out[0, :, cells] = act
-        slope_out[0, :, cells] = slope.astype(BF16)
-        hidden = hidden + dot(act, down_weight[cells, :])
-    high, low = split_two(hidden)
-    high_out[0] = high
-    low_out[0] = low
-    products = dot_last(cot_stack[0, STACK:, :], high)
-    inner = products[:STACK] + products[STACK:] + dot_last(cot_stack[0, :STACK, :], low)
-    inner_out[0] = inner[:NB]
-    frontier = 1.0 / (1.0 + jnp.exp(-inner[NB : NB + 1]))
-    frontier_out[0] = frontier
-    slot = place[0] + iota((1, span), 1)
-    running_out[0] = running_sum(jnp.where(slot < lengths[item], frontier, 0.0), triangle[...])
+    def attend():
+        hot_columns = one_hot_columns(ids_row[0], vocab)
+        hot = hot_columns.T
+        query_keys[...] = dot(hot, table[:, : 2 * model_width]).astype(BF16)
+        value_columns[...] = dot(value_table[...], hot_columns).astype(BF16)
+        held_hot[...] = hot[WIN : WIN + span]
+        yield True
+        tiles = span // TILE
+        pairs = H // 2
+        for tile in range(tiles):
+            begin = tile * TILE
+            window = slice(begin, begin + SPAN_KEYS)
+            tile_bias = bias[0 if tile == 0 else (2 if tile == tiles - 1 else 1)]
+            lanes = [slice(pair * PAIR, (pair + 1) * PAIR) for pair in range(pairs)]
+            scores = []
+            for pair in range(pairs):
+                key_lanes = slice(model_width + pair * PAIR, model_width + (pair + 1) * PAIR)
+                query_block = head_blocks(query_keys[begin + WIN : begin + WIN + TILE, lanes[pair]])
+                scores.append(dot_last(query_keys[window, key_lanes], query_block) + tile_bias)
+            yield True
+            probs = []
+            for pair in range(pairs):
+                peak = jnp.max(scores[pair], 0, keepdims=True)
+                weights = jnp.exp(scores[pair] - peak)
+                weight_sum = jnp.sum(weights, 0, keepdims=True)
+                probs.append((weights * pltpu.reciprocal(weight_sum, approx=True)).astype(BF16))
+                at = tile * pairs + pair
+                log_out[0, at : at + 1, :] = peak + jnp.log(weight_sum)
+            yield True
+            mixed = [dot(value_columns[lanes[pair], window], probs[pair]) for pair in range(pairs)]
+            for pair in range(pairs):
+                rows = head_columns(mixed[pair]).T.astype(BF16)
+                attended_out[0, begin : begin + TILE, lanes[pair]] = rows
+                held_attended[begin : begin + TILE, lanes[pair]] = rows
+            yield True
+
+    def feed():
+        middle = dot(held_hot[...], embed[...]) + dot(held_attended[...], out_weight[...])
+        middle_out[0] = middle
+        centered = middle - jnp.mean(middle, -1, keepdims=True)
+        variance = jnp.mean(centered * centered, -1, keepdims=True)
+        normed = (centered * lax.rsqrt(variance + eps) * gain[...] + shift[...]).astype(BF16)
+        normed_out[0] = normed
+        yield True
+        chunk = 512
+        cuts = [slice(begin, begin + chunk) for begin in range(0, hidden_width, chunk)]
+        hidden = middle + down_bias[...]
+        preact = dot(normed, up_weight[:, cuts[0]]) + up_bias[:, cuts[0]]
+        for at, cells in enumerate(cuts):
+            held = preact
+            if at + 1 < len(cuts):
+                preact = dot(normed, up_weight[:, cuts[at + 1]]) + up_bias[:, cuts[at + 1]]
+            yield True
+            act, slope = gelu_with_slope(held)
+            act = act.astype(BF16)
+            act_out[0, :, cells] = act
+            slope_out[0, :, cells] = slope.astype(BF16)
+            yield True
+            hidden = hidden + dot(act, down_weight[cells, :])
+            yield True
+        high, low = split_two(hidden)
+        high_out[0] = high
+        low_out[0] = low
+        products = dot_last(cot_stack[0, STACK:, :], high)
+        inner = products[:STACK] + products[STACK:] + dot_last(cot_stack[0, :STACK, :], low)
+        inner_out[0] = inner[:NB]
+        frontier = 1.0 / (1.0 + jnp.exp(-inner[NB : NB + 1]))
+        frontier_out[0] = frontier
+        slot = place[0] + iota((1, span), 1)
+        running_out[0] = running_sum(
+            jnp.where(slot < lengths[step - 1], frontier, 0.0), triangle[...]
+        )
+        yield True
+
+    @pl.when(step == 0)
+    def _():
+        take_turns(attend())
+
+    @pl.when((step > 0) & (step < items))
+    def _():
+        take_turns(feed(), attend())
+
+    @pl.when(step == items)
+    def _():
+        take_turns(feed())
 
 
 def assignment(place, lengths, counts, before, total, running):
@@ -268,7 +304,7 @@
 def write_halves(place, total, sent_out, kept_out):
     half = kept_out.shape[0]
     core = place[3]
-    sent_out[...] = total[pl.ds(pl.multiple_of((1 - core) * half, half), half)].astype(BF16)
+    sent_out[:half] = total[pl.ds(pl.multiple_of((1 - core) * half, half), half)].astype(BF16)
     kept_out[...] = total[pl.ds(pl.multiple_of(core * half, half), half)].astype(BF16)
 
 
@@ -344,6 +380,9 @@
     def _():
         write_halves(place, down_total, down_sent, down_kept)
         write_halves(place, up_total, up_sent, up_kept)
+        rows = up_kept.shape[0]
+        high, low = split_two(rows_out[...])
+        up_sent[rows:] = jnp.concatenate([high, low], 0)
 
 
 def attend_back_kernel(
@@ -421,6 +460,32 @@
             outs[0][...] = rows_total[...]
 
 
+def finish_kernel(
+    embed, normed, gain, weight, sums,
+    embed_out, weight_out, gain_out, shift_out,
+):
+    vocab, model_width = embed.shape
+    rows = embed[...].astype(F32)
+    centered = rows - jnp.mean(rows, -1, keepdims=True)
+    scale = lax.rsqrt(jnp.mean(centered * centered, -1, keepdims=True) + eps)
+    unit = centered * scale
+    d_normed = None
+    for at in range(3):
+        lanes = slice(at * model_width, (at + 1) * model_width)
+        part = sums[(at + 1) * vocab : (at + 2) * vocab]
+        weight_out[:, lanes] = dot_first(normed[...], part)
+        back = dot_last(part, weight[:, lanes])
+        d_normed = back if d_normed is None else d_normed + back
+    gain_out[...] = jnp.sum(d_normed * unit, 0, keepdims=True)
+    shift_out[...] = jnp.sum(d_normed, 0, keepdims=True)
+    pushed = d_normed * gain[...]
+    embed_out[...] = sums[:vocab].astype(F32) + scale * (
+        pushed
+        - jnp.mean(pushed, -1, keepdims=True)
+        - unit * jnp.mean(pushed * unit, -1, keepdims=True)
+    )
+
+
 def whole(shape):
     return pl.BlockSpec(shape, lambda item: (0,) * len(shape))
 
@@ -456,8 +521,8 @@
     return per_item(shape), (items,) + shape, dtype
 
 
-def halves_out(rows, width):
-    return [total_out((rows // 2, width), BF16)] * 2
+def halves_out(rows, width, more=0):
+    return [total_out((rows // 2 + more, width), BF16), total_out((rows // 2, width), BF16)]
 
 
 def total_out(shape, dtype=F32):
@@ -483,24 +548,6 @@
     return earlier, cells, later, beside
 
 
-def all_sum(axis, cells):
-    count = lax.axis_size(axis)
-    index = lax.axis_index(axis)
-    steps = [
-        (((index & bit) != 0).astype(jnp.int32), [(at, at ^ bit) for at in range(count)])
-        for bit in bits_of(count)
-    ]
-    for side, pairs in steps:
-        half = cells.shape[0] // 2
-        sent = lax.dynamic_slice_in_dim(cells, (1 - side) * half, half, 0).astype(BF16)
-        kept = lax.dynamic_slice_in_dim(cells, side * half, half, 0)
-        cells = kept + lax.ppermute(sent, axis, pairs).astype(F32)
-    cells = cells.astype(BF16)
-    for side, pairs in reversed(steps):
-        cells = joined(cells, lax.ppermute(cells, axis, pairs), side)
-    return cells.astype(F32)
-
-
 def joined(mine, came, side):
     half = mine.shape[0]
     cells = jnp.zeros((2 * half,) + mine.shape[1:], mine.dtype)
@@ -509,65 +556,126 @@
 
 
 class Exchange:
-    def __init__(self):
-        self.outer = lax.axis_size("dp")
-        self.inner = lax.axis_size("seq")
-        outer_bits = [("dp", bit) for bit in bits_of(self.outer)]
-        inner_bits = [("seq", bit) for bit in bits_of(self.inner)]
-        rest = outer_bits[1:] + inner_bits[:-1]
-        turn = len(outer_bits) - 1
-        first = outer_bits[:1]
-        last = inner_bits[-1:]
-        self.orders = (first + rest + last, first + rest[turn:] + rest[:turn] + last)
+    def __init__(self, outer_first):
+        outer_bits = [("dp", bit) for bit in bits_of(lax.axis_size("dp"))]
+        inner_bits = [("seq", bit) for bit in bits_of(lax.axis_size("seq"))]
+        core, last = outer_bits[:1], inner_bits[-1:]
+        outer_bits, inner_bits = outer_bits[1:], inner_bits[:-1]
+        if outer_first:
+            cut = len(outer_bits)
+            near, far = inner_bits[:cut], inner_bits[cut:]
+            self.orders = (
+                core + outer_bits + near + far + last,
+                core + near + outer_bits + far + last,
+            )
+        else:
+            self.orders = (
+                core + inner_bits + outer_bits + last,
+                core + inner_bits[::-1] + outer_bits + last,
+            )
         self.steps = len(self.orders[0])
-        self.at = {"dp": lax.axis_index("dp"), "seq": lax.axis_index("seq")}
-
-    def partner(self, flat, step):
-        outer, inner = divmod(flat, self.inner)
-        axis, bit = self.orders[outer & 1][step]
-        if axis == "dp":
-            outer ^= bit
-        else:
-            inner ^= bit
-        return outer * self.inner + inner
 
     def swap(self, cells, step):
-        devices = self.outer * self.inner
-        pairs = [(flat, self.partner(flat, step)) for flat in range(devices)]
+        outer_size, inner_size = lax.axis_size("dp"), lax.axis_size("seq")
+        pairs = []
+        for flat in range(outer_size * inner_size):
+            outer, inner = divmod(flat, inner_size)
+            axis, bit = self.orders[outer & 1][step]
+            other = (outer ^ bit, inner) if axis == "dp" else (outer, inner ^ bit)
+            pairs.append((flat, other[0] * inner_size + other[1]))
         return lax.ppermute(cells, ("dp", "seq"), pairs)
 
     def side(self, step):
-        picked = [
-            ((self.at[axis] & bit) != 0).astype(jnp.int32)
+        sides = [
+            ((lax.axis_index(axis) & bit) != 0).astype(jnp.int32)
             for axis, bit in (order[step] for order in self.orders)
         ]
-        return jnp.where((self.at["dp"] & 1) == 0, picked[0], picked[1])
-
-    def scatter_sum(self, sent, kept, extra=None):
-        for step in range(self.steps):
-            if step > 0:
-                half = cells.shape[0] // 2
-                side = self.side(step)
-                sent = lax.dynamic_slice_in_dim(cells, (1 - side) * half, half, 0).astype(BF16)
-                kept = lax.dynamic_slice_in_dim(cells, side * half, half, 0)
-            half = kept.shape[0]
-            if extra is not None:
-                high, low = split_two_outside(extra)
-                sent = jnp.concatenate([sent, high, low], 0)
-            came = self.swap(sent, step)
-            cells = kept.astype(F32) + came[:half].astype(F32)
-            if extra is not None:
-                rows = extra.shape[0]
-                mine = high.astype(F32) + low.astype(F32)
-                extra = mine + (
-                    came[half : half + rows].astype(F32) + came[half + rows :].astype(F32)
-                )
-        return cells.astype(BF16), extra
-
-    def gather(self, cells):
-        for step in reversed(range(self.steps)):
-            cells = joined(cells, self.swap(cells, step), self.side(step))
-        return cells
+        return jnp.where((lax.axis_index("dp") & 1) == 0, sides[0], sides[1])
+
+    def shared(self, step):
+        axis, _ = self.orders[0][step]
+        return axis == "seq" and self.orders[0][step] == self.orders[1][step]
+
+
+def halves(cells, side):
+    half = cells.shape[0] // 2
+    return (
+        lax.dynamic_slice_in_dim(cells, (1 - side) * half, half, 0),
+        lax.dynamic_slice_in_dim(cells, side * half, half, 0),
+    )
+
+
+class Chain:
+    def __init__(self, exchange, sent, kept, vectors=None, stop=None):
+        self.exchange = exchange
+        self.sent = sent
+        self.kept = kept
+        self.cells = None
+        self.vectors = vectors
+        self.rider = None
+        self.stop = exchange.steps if stop is None else stop
+        gathers = range(self.stop - 1, -1, -1)
+        self.plan = [("sum", step) for step in range(exchange.steps)]
+        self.plan += [("gather", step) for step in gathers]
+        self.at = 0
+        self.came = None
+
+    def start(self):
+        kind, step = self.plan[self.at]
+        if kind == "gather" or step >= self.stop:
+            moved = [self.cells]
+        else:
+            moved = [self.sent]
+            if self.vectors is not None and step > 0:
+                moved += split_two_outside(self.vectors)
+        if self.rider is not None and self.exchange.shared(step):
+            if kind == "sum":
+                away, self.rider = halves(self.rider, self.exchange.side(step))
+                moved.append(away.astype(BF16))
+            else:
+                moved.append(self.rider.astype(BF16))
+        moved = moved[0] if len(moved) == 1 else jnp.concatenate(moved, 0)
+        self.came = self.exchange.swap(moved, step)
+
+    def finish(self):
+        kind, step = self.plan[self.at]
+        came, self.came = self.came, None
+        self.at += 1
+        side = self.exchange.side(step)
+        if kind == "gather":
+            rows = self.cells.shape[0]
+            if self.rider is not None and self.exchange.shared(step):
+                self.rider = joined(self.rider.astype(BF16), came[rows:], side)
+            self.cells = joined(self.cells, came[:rows], side)
+            return
+        if step >= self.stop:
+            self.cells = (self.cells.astype(F32) + came.astype(F32)).astype(BF16)
+            return
+        half = self.kept.shape[0]
+        if self.vectors is not None:
+            rows = self.vectors.shape[0]
+            high, low = split_two_outside(self.vectors)
+            self.vectors = (high.astype(F32) + low.astype(F32)) + (
+                came[half : half + rows].astype(F32)
+                + came[half + rows : half + 2 * rows].astype(F32)
+            )
+        if self.rider is not None and self.exchange.shared(step):
+            self.rider = self.rider + came[half : half + self.rider.shape[0]].astype(F32)
+        if step + 1 == self.stop:
+            self.cells = (self.kept.astype(F32) + came[:half].astype(F32)).astype(BF16)
+            return
+        side = self.exchange.side(step + 1)
+        away, stay = halves(self.kept, side)
+        came_away, came_stay = halves(came[:half], side)
+        self.sent = (away.astype(F32) + came_away.astype(F32)).astype(BF16)
+        self.kept = stay.astype(F32) + came_stay.astype(F32)
+
+    def run(self, until=None):
+        until = len(self.plan) if until is None else until
+        while self.at < until:
+            if self.came is None:
+                self.start()
+            self.finish()
 
 
 def local(
@@ -637,13 +745,25 @@
     full = (span, hidden_width)
     row = (1, span)
     blocks = (NB, span)
+    logs_shape = (tiles * H // 2, 2 * TILE)
+
+    def item_ahead(shape):
+        return pl.BlockSpec(
+            (1,) + shape, lambda step: (jnp.minimum(step, items - 1),) + (0,) * len(shape)
+        )
+
+    def item_behind(shape):
+        return pl.BlockSpec(
+            (1,) + shape, lambda step: (jnp.maximum(step - 1, 0),) + (0,) * len(shape)
+        )
+
     (
         attended, logs, middle, normed_two, act, slope, hidden_high, hidden_low,
         inner, frontier, running,
     ) = call(
         forward_kernel,
-        items,
-        [scalars(), scalars(), per_item((1, wide))]
+        items + 1,
+        [scalars(), scalars(), item_ahead((1, wide))]
         + [
             whole(shape)
             for shape in (
@@ -653,25 +773,25 @@
                 (hidden_width, model_width), (1, model_width),
             )
         ]
-        + [per_item((3 * STACK, model_width))],
+        + [item_behind((3 * STACK, model_width))],
         [
-            item_out(items, square, BF16),
-            item_out(items, (tiles * H // 2, 2 * TILE), F32),
-            item_out(items, square, F32),
-            item_out(items, square, BF16),
-            item_out(items, full, BF16),
-            item_out(items, full, BF16),
-            item_out(items, square, BF16),
-            item_out(items, square, BF16),
-            item_out(items, blocks, F32),
-            item_out(items, row, F32),
-            item_out(items, row, F32),
+            (item_ahead(square), (items,) + square, BF16),
+            (item_ahead(logs_shape), (items,) + logs_shape, F32),
+        ]
+        + [
+            (item_behind(shape), (items,) + shape, dtype)
+            for shape, dtype in (
+                (square, F32), (square, BF16), (full, BF16), (full, BF16), (square, BF16),
+                (square, BF16), (blocks, F32), (row, F32), (row, F32),
+            )
         ],
         [
             pltpu.VMEM((3, SPAN_KEYS, 2 * TILE), F32),
             pltpu.VMEM((wide, 2 * model_width), BF16),
             pltpu.VMEM((model_width, wide), BF16),
             pltpu.VMEM((span, span), BF16),
+            pltpu.VMEM((span, vocab), BF16),
+            pltpu.VMEM(square, BF16),
         ],
         2 * tokens * model_width * (2 * hidden_width + 3 * model_width),
         (
@@ -705,6 +825,20 @@
     )
     _, stats_whole, stats_after, numer = scan_over("seq", stats, seq_place, numer)
 
+    numer = numer.reshape(items * NB, model_width)
+    near, near_came = [], []
+    down_exchange = Exchange(True)
+    exchange_steps = down_exchange.steps
+    for step, (axis, bit) in enumerate(down_exchange.orders[0]):
+        if axis == "seq" and not down_exchange.shared(step):
+            pairs = [(at, at ^ bit) for at in range(seq_count)]
+            side = ((seq_place & bit) != 0).astype(jnp.int32)
+            if near_came:
+                numer = numer + near_came.pop().astype(F32)
+            near.append((side, pairs))
+            away, numer = halves(numer, side)
+            away, stats_whole = lax.optimization_barrier((away.astype(BF16), stats_whole))
+            near_came.append(lax.ppermute(away, "seq", pairs))
     back_specs = numbers_specs + [
         per_item(row), per_item(blocks), per_item((8, NB)), per_item((8, NB)),
         per_item((3 * STACK, model_width)),
@@ -720,7 +854,7 @@
         + [whole((1, model_width)), whole((hidden_width, model_width)),
            whole((model_width, hidden_width)), whole((model_width, model_width))],
         halves_out(hidden_width, model_width)
-        + halves_out(hidden_width + model_width, model_width)
+        + halves_out(hidden_width + model_width, model_width, 16)
         + [
             item_out(items, square, BF16),
             total_out((vocab, model_width)),
@@ -738,7 +872,16 @@
            down_weight, up_weight, out_weight),
     )
 
-    exchange = Exchange()
+    down = Chain(down_exchange, down_sent, down_kept)
+    up = Chain(Exchange(False), up_sent, up_kept, rows)
+    down.run(1)
+    up.run(1)
+    down.sent, up.sent, d_attended, near_came = lax.optimization_barrier(
+        (down.sent, up.sent, d_attended, near_came)
+    )
+    down.rider = numer + near_came[0].astype(F32)
+    down.start()
+    up.start()
     rows_sent, rows_kept = call(
         attend_back_kernel,
         items,
@@ -760,22 +903,29 @@
         (place, ids_row, table, key_table, d_attended, logs, d_embed_direct),
     )
 
+    rows_sent, down.came, up.came = lax.optimization_barrier((rows_sent, down.came, up.came))
+    table_rows = Chain(Exchange(False), rows_sent, rows_kept, stop=exchange_steps - 2)
+    chains = (up, down, table_rows)
+    while any(chain.at < len(chain.plan) for chain in chains):
+        ahead = None
+        for chain in chains:
+            if chain.at == len(chain.plan):
+                continue
+            if chain.came is None:
+                chain.start()
+            if ahead is not None:
+                chain.came, _ = lax.optimization_barrier((chain.came, ahead))
+            chain.finish()
+            ahead = chain.sent if chain.cells is None else chain.cells
+    d_rows = table_rows.cells
+    d_weights = up.cells.astype(F32)
+    d_down = down.cells.astype(F32)
+    rows = up.vectors
+    numer = down.rider
+    for side, pairs in reversed(near):
+        numer = joined(numer, lax.ppermute(numer, "seq", pairs), side)
     inverse = 1.0 / (stats_whole[:, 0] + 1.0)
-    pooled = all_sum("seq", numer.reshape(items * NB, model_width)).reshape(
-        items, NB, model_width
-    ) * inverse[:, :, None]
-
-    devices = exchange.outer * exchange.inner
-    down_share, _ = exchange.scatter_sum(down_sent, down_kept)
-    weights_share, rows = exchange.scatter_sum(up_sent, up_kept, rows)
-    small_share, _ = exchange.scatter_sum(rows_sent, rows_kept)
-    cut = down_share.shape[0]
-    big = exchange.gather(jnp.concatenate([down_share, weights_share], 0))
-    big = big.reshape(devices, -1, model_width)
-    d_down = big[:, :cut].reshape(hidden_width, model_width).astype(F32)
-    d_weights = big[:, cut:].reshape(-1, model_width).astype(F32)
-    small = exchange.gather(small_share)
-
+    pooled = numer.astype(F32).reshape(items, NB, model_width) * inverse[:, :, None]
     d_up = jnp.concatenate(
         [
             d_weights[begin : begin + model_width]
@@ -784,28 +934,26 @@
         1,
     )
     d_out = d_weights[hidden_width:]
-    d_table = jnp.concatenate(
-        [small[at * vocab : (at + 1) * vocab] for at in range(1, 4)], 1
-    )
-    d_qkv = dot_first(normed_one, d_table)
-    d_normed_one = dot_last(d_table, qkv_weight)
-    embed_rows = byte_embed.astype(F32)
-    centered = embed_rows - jnp.mean(embed_rows, -1, keepdims=True)
-    scale_one = lax.rsqrt(jnp.mean(centered * centered, -1, keepdims=True) + eps)
-    unit_one = centered * scale_one
-    d_gain_one = jnp.sum(d_normed_one * unit_one, 0)
-    d_shift_one = jnp.sum(d_normed_one, 0)
-    pushed = d_normed_one * norm1_gain
-    d_embed = small[:vocab].astype(F32) + scale_one * (
-        pushed
-        - jnp.mean(pushed, -1, keepdims=True)
-        - unit_one * jnp.mean(pushed * unit_one, -1, keepdims=True)
+    d_embed, d_qkv, d_gain_one, d_shift_one = call(
+        finish_kernel,
+        1,
+        [whole((vocab, model_width)), whole((vocab, model_width)), whole((1, model_width)),
+         whole((model_width, 3 * model_width)), whole((4 * vocab, model_width))],
+        [
+            total_out((vocab, model_width)),
+            total_out((model_width, 3 * model_width)),
+            total_out((1, model_width)),
+            total_out((1, model_width)),
+        ],
+        [],
+        8 * vocab * model_width * model_width,
+        (byte_embed, normed_one, norm1_gain[None], qkv_weight, d_rows),
     )
     return (
         pooled,
         d_embed,
-        d_gain_one,
-        d_shift_one,
+        d_gain_one.reshape(-1),
+        d_shift_one.reshape(-1),
         d_qkv,
         d_out,
         rows[0],

time: 268 us -> 234 us (0.87)
  waiting for transfers between devices: 81.6 us -> 47.6 us
  local copies, waits for them, and re-layouts: 9.54 us -> 14.3 us
  matrix products: 3.53 us -> 0 us
  Pallas kernels: 102 us -> 105 us
    ppermute x25 -> x28, waiting for transfers between devices: 72.2 us -> 38.9 us  [swap(): return lax.ppermute(cells, ('dp', 'seq'), pairs)]
    ppermute x6 -> x2, starting transfers between devices: 9.8 us -> 2.21 us  [the longest x1 1.12 us: local(): numer = joined(numer, lax.ppermute(numer, 'seq', pairs), side)]
    ppermute x25 -> x28, starting transfers between devices: 24.1 us -> 29.5 us  [swap(): return lax.ppermute(cells, ('dp', 'seq'), pairs)]
    dot_general x2 -> x0, matrix products: 3.53 us -> none  [the longest x1 2.26 us: dot_first(): lax.dot_general(left, right, (((0,), (0,)), ((), ())), preferred_element_...]
    pallas_call x6 -> x7, Pallas kernels: 102 us -> 105 us  [call(): pl.pallas_call(kernel, grid=(items,), in_specs=in_specs, out_specs=[spec...]
  transfers between devices with their start and end apart: 39 -> 38, of which waited for: 19 -> 22; matrix products, arithmetic and copies ran while one was open for 7% -> 6% of each run, Pallas kernels for 24% -> 14%
where the time goes in v3:
time: 234 us
  Pallas kernels  105 us (45%)
  starting transfers between devices  51.8 us (22%)
  waiting for transfers between devices  47.6 us (20%)
  local copies, waits for them, and re-layouts  14.3 us (6%)
  other arithmetic  13.9 us (6%)
    pallas_call x7, Pallas kernels, call(): pl.pallas_call(kernel, grid=(items,), in_specs=in_specs, out_specs=[spec...  105 us
    ppermute x28, waiting for transfers between devices, swap(): return lax.ppermute(cells, ('dp', 'seq'), pairs)  38.9 us
    ppermute x28, starting transfers between devices, swap(): return lax.ppermute(cells, ('dp', 'seq'), pairs)  29.5 us
    ppermute x6, starting transfers between devices, scan_over(): other = lax.ppermute(cells, axis, [(at, at ^ bit) for at in range(count)])  13.9 us
    ppermute x6, waiting for transfers between devices, scan_over(): other = lax.ppermute(cells, axis, [(at, at ^ bit) for at in range(count)])  7.18 us
    ppermute x1, starting transfers between devices, local(): lax.ppermute(byte_ids[:, span - WIN:], 'seq', [(at, at + 1) for at in ends])  4.86 us
  transfers between devices with their start and end apart: 38, of which 22 were waited for; matrix products, arithmetic and copies ran while one was open for 6% of the time, Pallas kernels for 14%

profile of v3, /device:TPU:0, one launch (start us, length us, event | category | flops | bytes accessed | tf_op | source)
XLA Modules:
  0.0 233.7 jit_solution(1743506357719010413)
XLA Ops:
  1.5 4.9 %collective-permute-start = (s32[4,64]{1,0:T(4,128)S(1)}, s32[4,64]{1,0:T(4,128)S(1)}, u32[]{:S(2)}, u32[]{:S(2)}) collective-permute-start(s32[4,64]{1,0:T(4,128)S(1)} %get-tuple-element.168), channel_id=1, source_target_pairs={{0,1},{1,2},{2,3},{3,4},{4,5},{5,6},{6,7},{8,9},{9,10},{10,11},{11... | collective-permute-start | bytes 3080 | tf_op jit(solution)/shard_map/ppermute | solution.py:711
  6.3 1.3 collective-permute-start.1
  8.2 3.8 %shard_map.255 = (bf16[256,512]{1,0:T(8,128)(2,1)}, bf16[256,1536]{1,0:T(8,128)(2,1)}, bf16[512,256]{1,0:T(8,128)(2,1)}, bf16[512,256]{1,0:T(8,128)(2,1)}, bf16[4,240,512]{2,1,0:T(8,128)(2,1)}) custom-call(bf16[256,512]{1,0:T(8,128)(2,1)} %embed.5, f32[1,512]{1,0:T(1,128)} %bitcast.32, f32[1,512]{1,0:T(1,128)} %bitcast.40, bf16[512,1536]{1,0:T(8,128)(2,1)} %weight.3, ...), custom_call_target="tpu_custom_call" | custom-call | flops 1 | tf_op jit(solution)/shard_map/pallas_call | solution.py:508
  12.7 32.3 %shard_map.256 = (bf16[4,512,512]{2,1,0:T(8,128)(2,1)}, f32[4,16,256]{2,1,0:T(8,128)}, f32[4,512,512]{2,1,0:T(8,128)}, bf16[4,512,512]{2,1,0:T(8,128)(2,1)}, bf1...) custom-call(s32[4]{0:T(128)} %pad_add_fusion.1.place, ...), custom_call_target="tpu_custom_call" | custom-call | flops 1 | tf_op jit(solution)/shard_map/pallas_call | solution.py:508
  45.0 0.9 slice_reduce_fusion
  45.9 2.7 %collective-permute-start.2 = (f32[4]{0:T(128)S(1)}, f32[4]{0:T(128)S(1)}, u32[]{:S(2)}, u32[]{:S(2)}) collective-permute-start(f32[4]{0:T(128)S(1)} %slice_reduce_fusion), channel_id=1, source_target_pairs={{0,1},{1,0},{2,3},{3,2},{4,5},{5,4},{6,7},{7,6},{8,9},{9,8},{10,11... | collective-permute-start | bytes 56 | tf_op jit(solution)/shard_map/ppermute | solution.py:543
  48.6 1.5 collective-permute-done.2
  50.1 3.0 %collective-permute-start.3 = (f32[4]{0:T(128)S(1)}, f32[4]{0:T(128)S(1)}, u32[]{:S(2)}, u32[]{:S(2)}) collective-permute-start(f32[4]{0:T(128)S(1)} %add.289), channel_id=1, source_target_pairs={{0,2},{1,3},{2,0},{3,1},{4,6},{5,7},{6,4},{7,5},{8,10},{9,11},{10,... | collective-permute-start | bytes 56 | tf_op jit(solution)/shard_map/ppermute | solution.py:543
  53.1 1.5 collective-permute-done.3
  54.6 3.0 %collective-permute-start.4 = (f32[4]{0:T(128)S(1)}, f32[4]{0:T(128)S(1)}, u32[]{:S(2)}, u32[]{:S(2)}) collective-permute-start(f32[4]{0:T(128)S(1)} %add.291), channel_id=1, source_target_pairs={{0,4},{1,5},{2,6},{3,7},{4,0},{5,1},{6,2},{7,3},{8,12},{9,13},{10,... | collective-permute-start | bytes 56 | tf_op jit(solution)/shard_map/ppermute | solution.py:543
  57.7 1.5 collective-permute-done.4
  59.7 3.5 %shard_map.257 = f32[4,8,64]{2,1,0:T(8,128)} custom-call(s32[4]{0:T(128)} %pad_add_fusion.1.place, s32[4]{0:T(128)} %lengths.7, s32[4]{0:T(128)} %counts.5, f32[4]{0:T(128)} %get-tuple-element.171.before, f32[4]{0:T(128)} %get-tuple-element.170.total, f32[4,1,512]{2,1,0:T(1,128)} %get-tuple-element.73.running, f32[4,64,512]{2,1,0:T(8,128)} %get-tuple-element.74.inner), custom_call_target="tpu_custom_call" | custom-call | flops 1 | tf_op jit(solution)/shard_map/pallas_call | solution.py:508
  63.2 0.9 collective-permute-start.5
  64.1 4.6 %shard_map.258 = f32[4,64,512]{2,1,0:T(8,128)} custom-call(s32[4]{0:T(128)} %pad_add_fusion.1.place, s32[4]{0:T(128)} %lengths.7, s32[4]{0:T(128)} %counts.5, f32[4]{0:T(128)} %get-tuple-element.171.before, f32[4]{0:T(128)} %get-tuple-element.170.total, f32[4,1,512]{2,1,0:T(1,128)} %get-tuple-element.73.running, ...), custom_call_target="tpu_custom_call" | custom-call | flops 1 | tf_op jit(solution)/shard_map/pallas_call | solution.py:508
  68.8 1.7 collective-permute-start.6
  71.0 1.6 collective-permute-done.6
  72.6 2.6 %collective-permute-start.7 = (f32[4,8,64]{2,1,0:T(8,128)S(1)}, f32[4,8,64]{2,1,0:T(8,128)S(1)}, u32[]{:S(2)}, u32[]{:S(2)}) collective-permute-start(f32[4,8,64]{2,1,0:T(8,128)S(1)} %add.296), channel_id=1, source_target_pairs={{0,4},{1,5},{2,6},{3,7},{4,0},{5,1},{6,2},{7,3},{8,12},{9,13},{10,... | collective-permute-start | bytes 24584 | tf_op jit(solution)/shard_map/ppermute | solution.py:543
  75.2 1.0 dynamic-slice_convert_fusion
  76.2 1.1 collective-permute-done.7
  77.8 35.2 %shard_map.259 = (bf16[1024,512]{1,0:T(8,128)(2,1)}, bf16[1024,512]{1,0:T(8,128)(2,1)}, bf16[1296,512]{1,0:T(8,128)(2,1)}, bf16[1280,512]{1,0:T(8,128)(2,1)}, bf...) custom-call(s32[4]{0:T(128)} %pad_add_fusion.1.place, s32[4]{0:T(128)} %lengths.7, s32[4]{0:T(128)} %counts.5, ...), custom_call_target="tpu_custom_call" | custom-call | flops 1 | tf_op jit(solution)/shard_map/pallas_call | solution.py:508
  113.6 1.1 collective-permute-start.10
  114.7 3.2 %collective-permute-done.8 = bf16[1024,512]{1,0:T(8,128)(2,1)S(1)} collective-permute-done((bf16[1024,512]{1,0:T(8,128)(2,1)}, bf16[1024,512]{1,0:T(8,128)(2,1)S(1)}, u32[]{:S(2)}, u32[]{:S(2)}) %collective-permute-start.8) | collective-permute-done | bytes 1048608 | tf_op jit(solution)/shard_map/ppermute | solution.py:586
  117.8 2.3 convert_add_fusion.1
  120.1 1.5 slice.148
  123.3 0.9 pad_maximum_fusion.1
  124.2 1.2 collective-permute-start.12
  125.3 1.5 collective-permute-start.11
  127.6 20.8 %shard_map.260 = (bf16[512,512]{1,0:T(8,128)(2,1)}, bf16[512,512]{1,0:T(8,128)(2,1)}) custom-call(s32[4]{0:T(128)} %pad_add_fusion.1.place, s32[4,1,640]{2,1,0:T(1,128)} %broadcast_in_dim.64.ids_row, bf16[256,1536]{1,0:T(8,128)(2,1)} %get-tuple-element.70.table, bf16[512,256]{1,0:T(8,128)(2,1)} %get-tuple-element.93.key_table, ...), custom_call_target="tpu_custom_call" | custom-call | flops 1 | tf_op jit(solution)/shard_map/pallas_call | solution.py:508
  148.8 2.0 collective-permute-start.14
  151.6 4.4 %collective-permute-done.14 = bf16[336,512]{1,0:T(8,128)(2,1)S(1)} collective-permute-done((bf16[336,512]{1,0:T(8,128)(2,1)S(1)}, bf16[336,512]{1,0:T(8,128)(2,1)S(1)}, u32[]{:S(2)}, u32[]{:S(2)}) %collective-permute-start.14) | collective-permute-done | bytes 344096 | tf_op jit(solution)/shard_map/ppermute | solution.py:586
  156.9 1.0 collective-permute-done.13
  158.0 0.9 collective-permute-start.15
  158.9 4.1 %collective-permute-done.16 = bf16[176,512]{1,0:T(8,128)(2,1)S(1)} collective-permute-done((bf16[176,512]{1,0:T(8,128)(2,1)S(1)}, bf16[176,512]{1,0:T(8,128)(2,1)S(1)}, u32[]{:S(2)}, u32[]{:S(2)}) %collective-permute-start.16) | collective-permute-done | bytes 180256 | tf_op jit(solution)/shard_map/ppermute | solution.py:586
  163.1 2.7 %collective-permute-start.18 = (bf16[96,512]{1,0:T(8,128)(2,1)S(1)}, bf16[96,512]{1,0:T(8,128)(2,1)S(1)}, u32[]{:S(2)}, u32[]{:S(2)}) collective-permute-start(bf16[96,512]{1,0:T(8,128)(2,1)S(1)} %pad_maximum_fusion.7), channel_id=1, source_target_pairs={{0,4},{1,5},{2,6},{3,7},{4,0},{5,1},{6,2},{7,3},{8,12},{9,13},{10,... | collective-permute-start | bytes 294920 | tf_op jit(solution)/shard_map/ppermute | solution.py:586
  166.8 1.9 collective-permute-start.17
  168.6 2.7 %collective-permute-done.18 = bf16[96,512]{1,0:T(8,128)(2,1)S(1)} collective-permute-done((bf16[96,512]{1,0:T(8,128)(2,1)S(1)}, bf16[96,512]{1,0:T(8,128)(2,1)S(1)}, u32[]{:S(2)}, u32[]{:S(2)}) %collective-permute-start.18) | collective-permute-done | bytes 98336 | tf_op jit(solution)/shard_map/ppermute | solution.py:586
  172.1 1.1 collective-permute-start.20
  173.8 2.1 collective-permute-done.17
  176.0 3.7 %collective-permute-done.20 = bf16[80,512]{1,0:T(8,128)(2,1)S(1)} collective-permute-done((bf16[80,512]{1,0:T(8,128)(2,1)S(1)}, bf16[80,512]{1,0:T(8,128)(2,1)S(1)}, u32[]{:S(2)}, u32[]{:S(2)}) %collective-permute-start.20) | collective-permute-done | bytes 81952 | tf_op jit(solution)/shard_map/ppermute | solution.py:586
  179.7 0.8 collective-permute-start.22
  180.6 2.0 collective-permute-done.19
  183.3 1.6 collective-permute-start.26
  185.1 1.0 collective-permute-start.32
  186.2 3.6 %collective-permute-done.26 = bf16[128,512]{1,0:T(8,128)(2,1)S(1)} collective-permute-done((bf16[128,512]{1,0:T(8,128)(2,1)S(1)}, bf16[128,512]{1,0:T(8,128)(2,1)S(1)}, u32[]{:S(2)}, u32[]{:S(2)}) %collective-permute-start.26) | collective-permute-done | bytes 131104 | tf_op jit(solution)/shard_map/ppermute | solution.py:586
  189.8 2.0 collective-permute-start.27
  191.9 1.0 collective-permute-start.31
  193.0 1.1 collective-permute-start.23
  194.9 2.1 collective-permute-start.28
  197.0 1.8 collective-permute-start.35
  198.8 1.5 collective-permute-done.23
  200.3 2.0 collective-permute-done.28
  202.9 1.8 collective-permute-start.34
  204.9 3.6 %collective-permute-done.29 = bf16[128,512]{1,0:T(8,128)(2,1)S(1)} collective-permute-done((bf16[128,512]{1,0:T(8,128)(2,1)S(1)}, bf16[128,512]{1,0:T(8,128)(2,1)S(1)}, u32[]{:S(2)}, u32[]{:S(2)}) %collective-permute-start.29) | collective-permute-done | bytes 131104 | tf_op jit(solution)/shard_map/ppermute | solution.py:586
  208.5 1.8 collective-permute-start.30
  210.3 3.5 %collective-permute-done.35 = bf16[640,512]{1,0:T(8,128)(2,1)S(1)} collective-permute-done((bf16[640,512]{1,0:T(8,128)(2,1)S(1)}, bf16[640,512]{1,0:T(8,128)(2,1)S(1)}, u32[]{:S(2)}, u32[]{:S(2)}) %collective-permute-start.35) | collective-permute-done | bytes 655392 | tf_op jit(solution)/shard_map/ppermute | solution.py:586
  213.9 0.9 convert_multiply_fusion
  215.0 1.6 collective-permute-done.30
  218.6 1.0 copy-done
  219.6 4.6 %shard_map.261 = (f32[256,512]{1,0:T(8,128)}, f32[512,1536]{1,0:T(8,128)}, f32[1,512]{1,0:T(1,128)}, f32[1,512]{1,0:T(1,128)}) custom-call(bf16[256,512]{1,0:T(8,128)(2,1)} %embed.5, bf16[256,512]{1,0:T(8,128)(2,1)} %get-tuple-element.109.normed, f32[1,512]{1,0:T(1,128)} %bitcast.33, bf16[512,1536]{1,0:T(8,128)(2,1)} %weight.3, bf16[1024,512]{1,0:T(8,128)(2,1)} %copy-done), custom_call_target="tpu_custom_call" | custom-call | flops 1 | tf_op jit(solution)/shard_map/pallas_call | solution.py:508
  224.2 1.5 constant_dynamic-update-slice_fusion.26
  225.6 1.7 fusion.7
  227.3 1.3 constant_dynamic-update-slice_fusion.12
  228.7 2.6 %convert_element_type.425 = f32[2048,512]{1,0:T(8,128)} convert(bf16[2048,512]{1,0:T(8,128)(2,1)S(1)} %constant_dynamic-update-slice_fusion.12) | non-fusion elementwise | flops 1048576 | bytes 6291456 | tf_op jit(solution)/shard_map/convert_element_type | solution.py:922
  231.3 2.4 %pad_maximum_fusion = f32[512,2048]{1,0:T(8,128)} fusion(f32[512,512]{1,0:T(8,128)S(1)} %get-tuple-element.138, f32[512,512]{1,0:T(8,128)S(1)} %get-tuple-element.137, f32[512,512]{1,0:T(8,128)S(1)} %get-tuple-element.136, f32[512,512]{1,0:T(8,128)S(1)} %get-tuple-element.135), kind=kLoop, calls=%fused_computation | loop fusion | flops 3145728 | bytes 8388608 | tf_op jit(solution)/shard_map/concatenate | solution.py:929
  (150 shorter events, 16.1 us)
Async XLA Ops:
  0.6 11.4 %copy-start.11 = (s32[4,512]{1,0:T(4,128)S(1)}, s32[4,512]{1,0:T(4,128)}, u32[]{:S(2)}) copy-start(s32[4,512]{1,0:T(4,128)} %param.16) | copy-start | bytes 24580
  1.5 10.5 %collective-permute-start = (s32[4,64]{1,0:T(4,128)S(1)}, s32[4,64]{1,0:T(4,128)S(1)}, u32[]{:S(2)}, u32[]{:S(2)}) collective-permute-start(s32[4,64]{1,0:T(4,128)S(1)} %get-tuple-element.168), channel_id=1, source_target_pairs={{0,1},{1,2},{2,3},{3,4},{4,5},{5,6},{6,7},{8,9},{9,10},{10,11},{11... | collective-permute-start | bytes 3080 | tf_op jit(solution)/shard_map/ppermute | solution.py:711
  6.3 5.7 %collective-permute-start.1 = (s32[4,64]{1,0:T(4,128)S(1)}, s32[4,64]{1,0:T(4,128)S(1)}, u32[]{:S(2)}, u32[]{:S(2)}) collective-permute-start(s32[4,64]{1,0:T(4,128)S(1)} %get-tuple-element.169), channel_id=1, source_target_pairs={{1,0},{2,1},{3,2},{4,3},{5,4},{6,5},{7,6},{9,8},{10,9},{11,10},{12... | collective-permute-start | bytes 3080 | tf_op jit(solution)/shard_map/ppermute | solution.py:713
  45.9 4.2 %collective-permute-start.2 = (f32[4]{0:T(128)S(1)}, f32[4]{0:T(128)S(1)}, u32[]{:S(2)}, u32[]{:S(2)}) collective-permute-start(f32[4]{0:T(128)S(1)} %slice_reduce_fusion), channel_id=1, source_target_pairs={{0,1},{1,0},{2,3},{3,2},{4,5},{5,4},{6,7},{7,6},{8,9},{9,8},{10,11... | collective-permute-start | bytes 56 | tf_op jit(solution)/shard_map/ppermute | solution.py:543
  50.1 4.5 %collective-permute-start.3 = (f32[4]{0:T(128)S(1)}, f32[4]{0:T(128)S(1)}, u32[]{:S(2)}, u32[]{:S(2)}) collective-permute-start(f32[4]{0:T(128)S(1)} %add.289), channel_id=1, source_target_pairs={{0,2},{1,3},{2,0},{3,1},{4,6},{5,7},{6,4},{7,5},{8,10},{9,11},{10,... | collective-permute-start | bytes 56 | tf_op jit(solution)/shard_map/ppermute | solution.py:543
  54.6 4.6 %collective-permute-start.4 = (f32[4]{0:T(128)S(1)}, f32[4]{0:T(128)S(1)}, u32[]{:S(2)}, u32[]{:S(2)}) collective-permute-start(f32[4]{0:T(128)S(1)} %add.291), channel_id=1, source_target_pairs={{0,4},{1,5},{2,6},{3,7},{4,0},{5,1},{6,2},{7,3},{8,12},{9,13},{10,... | collective-permute-start | bytes 56 | tf_op jit(solution)/shard_map/ppermute | solution.py:543
  63.2 5.6 %collective-permute-start.5 = (f32[4,8,64]{2,1,0:T(8,128)}, f32[4,8,64]{2,1,0:T(8,128)S(1)}, u32[]{:S(2)}, u32[]{:S(2)}) collective-permute-start(f32[4,8,64]{2,1,0:T(8,128)} %shard_map.257), channel_id=1, source_target_pairs={{0,1},{1,0},{2,3},{3,2},{4,5},{5,4},{6,7},{7,6},{8,9},{9,8},{10,11... | collective-permute-start | bytes 24584 | tf_op jit(solution)/shard_map/ppermute | solution.py:543
  64.1 4.6 %copy-start.10 = (f32[4,8,64]{2,1,0:T(8,128)S(1)}, f32[4,8,64]{2,1,0:T(8,128)}, u32[]{:S(2)}) copy-start(f32[4,8,64]{2,1,0:T(8,128)} %shard_map.257) | copy-start | bytes 24580
  68.8 3.8 %collective-permute-start.6 = (f32[4,8,64]{2,1,0:T(8,128)S(1)}, f32[4,8,64]{2,1,0:T(8,128)S(1)}, u32[]{:S(2)}, u32[]{:S(2)}) collective-permute-start(f32[4,8,64]{2,1,0:T(8,128)S(1)} %add.294), channel_id=1, source_target_pairs={{0,2},{1,3},{2,0},{3,1},{4,6},{5,7},{6,4},{7,5},{8,10},{9,11},{10,... | collective-permute-start | bytes 24584 | tf_op jit(solution)/shard_map/ppermute | solution.py:543
  72.6 4.6 %collective-permute-start.7 = (f32[4,8,64]{2,1,0:T(8,128)S(1)}, f32[4,8,64]{2,1,0:T(8,128)S(1)}, u32[]{:S(2)}, u32[]{:S(2)}) collective-permute-start(f32[4,8,64]{2,1,0:T(8,128)S(1)} %add.296), channel_id=1, source_target_pairs={{0,4},{1,5},{2,6},{3,7},{4,0},{5,1},{6,2},{7,3},{8,12},{9,13},{10,... | collective-permute-start | bytes 24584 | tf_op jit(solution)/shard_map/ppermute | solution.py:543
  113.0 7.1 %collective-permute-start.9 = (bf16[1296,512]{1,0:T(8,128)(2,1)}, bf16[1296,512]{1,0:T(8,128)(2,1)}, u32[]{:S(2)}, u32[]{:S(2)}) collective-permute-start(bf16[1296,512]{1,0:T(8,128)(2,1)} %get-tuple-element.89), channel_id=1, source_target_pairs={{0,8},{1,9},{2,10},{3,11},{4,12},{5,13},{6,14},{7,15},{8,0},{9,1},... | collective-permute-start | bytes 3981320 | tf_op jit(solution)/shard_map/ppermute | solution.py:586
  113.1 4.8 %collective-permute-start.8 = (bf16[1024,512]{1,0:T(8,128)(2,1)}, bf16[1024,512]{1,0:T(8,128)(2,1)S(1)}, u32[]{:S(2)}, u32[]{:S(2)}) collective-permute-start(bf16[1024,512]{1,0:T(8,128)(2,1)} %get-tuple-element.87), channel_id=1, source_target_pairs={{0,8},{1,9},{2,10},{3,11},{4,12},{5,13},{6,14},{7,15},{8,0},{9,1},... | collective-permute-start | bytes 3145736 | tf_op jit(solution)/shard_map/ppermute | solution.py:586
  113.6 8.6 %collective-permute-start.10 = (bf16[128,512]{1,0:T(8,128)(2,1)S(1)}, bf16[128,512]{1,0:T(8,128)(2,1)S(1)}, u32[]{:S(2)}, u32[]{:S(2)}) collective-permute-start(bf16[128,512]{1,0:T(8,128)(2,1)S(1)} %dynamic-slice_convert_fusion), channel_id=1, source_target_pairs={{0,1},{1,0},{2,3},{3,2},{4,5},{5,4},{6,7},{7,6},{8,9},{9,8},{10,11... | collective-permute-start | bytes 393224 | tf_op jit(solution)/shard_map/ppermute | solution.py:841
  120.1 1.7 copy-start.2
  121.8 0.7 copy-start.12
  122.2 2.0 copy-start.4
  123.3 0.9 copy-start.6
  123.3 0.9 copy-start.8
  124.2 24.2 %collective-permute-start.12 = (bf16[656,512]{1,0:T(8,128)(2,1)}, bf16[656,512]{1,0:T(8,128)(2,1)S(1)}, u32[]{:S(2)}, u32[]{:S(2)}) collective-permute-start(bf16[656,512]{1,0:T(8,128)(2,1)} %pad_maximum_fusion.1), channel_id=1, source_target_pairs={{0,1},{1,0},{2,3},{3,2},{4,5},{5,4},{6,7},{7,6},{8,10},{9,11},{10,... | collective-permute-start | bytes 2015240 | tf_op jit(solution)/shard_map/ppermute | solution.py:586
  125.3 23.0 %collective-permute-start.11 = (bf16[512,512]{1,0:T(8,128)(2,1)}, bf16[512,512]{1,0:T(8,128)(2,1)S(1)}, u32[]{:S(2)}, u32[]{:S(2)}) collective-permute-start(bf16[512,512]{1,0:T(8,128)(2,1)} %get-tuple-element.98), channel_id=1, source_target_pairs={{0,16},{1,17},{2,18},{3,19},{4,20},{5,21},{6,22},{7,23},{8,9},{9,8... | collective-permute-start | bytes 1572872 | tf_op jit(solution)/shard_map/ppermute | solution.py:586
  126.8 21.6 %copy-start.7 = (bf16[8,512]{1,0:T(8,128)(2,1)S(1)}, bf16[8,512]{1,0:T(8,128)(2,1)}, u32[]{:S(2)}) copy-start(bf16[8,512]{1,0:T(8,128)(2,1)} %copy-done.6) | copy-start | bytes 24580
  126.8 21.6 %copy-start.9 = (bf16[8,512]{1,0:T(8,128)(2,1)S(1)}, bf16[8,512]{1,0:T(8,128)(2,1)}, u32[]{:S(2)}) copy-start(bf16[8,512]{1,0:T(8,128)(2,1)} %copy-done.8) | copy-start | bytes 24580
  148.5 2.3 copy-start.1
  148.5 2.2 copy-start.5
  148.7 2.9 %copy-start.13 = (bf16[512,512]{1,0:T(8,128)(2,1)S(1)}, bf16[512,512]{1,0:T(8,128)(2,1)}, u32[]{:S(2)}) copy-start(bf16[512,512]{1,0:T(8,128)(2,1)} %get-tuple-element.111) | copy-start | bytes 1572868
  148.8 7.3 %collective-permute-start.14 = (bf16[336,512]{1,0:T(8,128)(2,1)S(1)}, bf16[336,512]{1,0:T(8,128)(2,1)S(1)}, u32[]{:S(2)}, u32[]{:S(2)}) collective-permute-start(bf16[336,512]{1,0:T(8,128)(2,1)S(1)} %pad_maximum_fusion.2), channel_id=1, source_target_pairs={{0,2},{1,3},{2,0},{3,1},{4,6},{5,7},{6,4},{7,5},{8,9},{9,8},{10,11... | collective-permute-start | bytes 1032200 | tf_op jit(solution)/shard_map/ppermute | solution.py:586
  151.0 6.9 %collective-permute-start.13 = (bf16[256,512]{1,0:T(8,128)(2,1)S(1)}, bf16[256,512]{1,0:T(8,128)(2,1)S(1)}, u32[]{:S(2)}, u32[]{:S(2)}) collective-permute-start(bf16[256,512]{1,0:T(8,128)(2,1)S(1)} %get-tuple-element.146), channel_id=1, source_target_pairs={{0,1},{1,0},{2,3},{3,2},{4,5},{5,4},{6,7},{7,6},{8,24},{9,25},{10,... | collective-permute-start | bytes 786440 | tf_op jit(solution)/shard_map/ppermute | solution.py:586
  151.6 14.2 %collective-permute-start.24 = (bf16[512,512]{1,0:T(8,128)(2,1)S(1)}, bf16[512,512]{1,0:T(8,128)(2,1)S(1)}, u32[]{:S(2)}, u32[]{:S(2)}) collective-permute-start(bf16[512,512]{1,0:T(8,128)(2,1)S(1)} %copy-done.13), channel_id=1, source_target_pairs={{0,8},{1,9},{2,10},{3,11},{4,12},{5,13},{6,14},{7,15},{8,0},{9,1},... | collective-permute-start | bytes 1572872 | tf_op jit(solution)/shard_map/ppermute | solution.py:586
  156.1 9.8 %copy-start.3 = (bf16[512,512]{1,0:T(8,128)(2,1)S(1)}, bf16[512,512]{1,0:T(8,128)(2,1)}, u32[]{:S(2)}) copy-start(bf16[512,512]{1,0:T(8,128)(2,1)} %get-tuple-element.110) | copy-start | bytes 1572868
  156.3 6.8 %collective-permute-start.16 = (bf16[176,512]{1,0:T(8,128)(2,1)S(1)}, bf16[176,512]{1,0:T(8,128)(2,1)S(1)}, u32[]{:S(2)}, u32[]{:S(2)}) collective-permute-start(bf16[176,512]{1,0:T(8,128)(2,1)S(1)} %pad_maximum_fusion.5), channel_id=1, source_target_pairs={{0,16},{1,17},{2,18},{3,19},{4,20},{5,21},{6,22},{7,23},{8,24},{9,... | collective-permute-start | bytes 540680 | tf_op jit(solution)/shard_map/ppermute | solution.py:586
  158.0 8.7 %collective-permute-start.15 = (bf16[192,512]{1,0:T(8,128)(2,1)S(1)}, bf16[192,512]{1,0:T(8,128)(2,1)S(1)}, u32[]{:S(2)}, u32[]{:S(2)}) collective-permute-start(bf16[192,512]{1,0:T(8,128)(2,1)S(1)} %pad_maximum_fusion.3), channel_id=1, source_target_pairs={{0,2},{1,3},{2,0},{3,1},{4,6},{5,7},{6,4},{7,5},{8,10},{9,11},{10,... | collective-permute-start | bytes 589832 | tf_op jit(solution)/shard_map/ppermute | solution.py:586
  163.1 8.2 %collective-permute-start.18 = (bf16[96,512]{1,0:T(8,128)(2,1)S(1)}, bf16[96,512]{1,0:T(8,128)(2,1)S(1)}, u32[]{:S(2)}, u32[]{:S(2)}) collective-permute-start(bf16[96,512]{1,0:T(8,128)(2,1)S(1)} %pad_maximum_fusion.7), channel_id=1, source_target_pairs={{0,4},{1,5},{2,6},{3,7},{4,0},{5,1},{6,2},{7,3},{8,12},{9,13},{10,... | collective-permute-start | bytes 294920 | tf_op jit(solution)/shard_map/ppermute | solution.py:586
  166.0 17.2 %collective-permute-start.25 = (bf16[256,512]{1,0:T(8,128)(2,1)S(1)}, bf16[256,512]{1,0:T(8,128)(2,1)S(1)}, u32[]{:S(2)}, u32[]{:S(2)}) collective-permute-start(bf16[256,512]{1,0:T(8,128)(2,1)S(1)} %get-tuple-element.150), channel_id=1, source_target_pairs={{0,1},{1,0},{2,3},{3,2},{4,5},{5,4},{6,7},{7,6},{8,10},{9,11},{10,... | collective-permute-start | bytes 786440 | tf_op jit(solution)/shard_map/ppermute | solution.py:586
  166.8 9.1 %collective-permute-start.17 = (bf16[96,512]{1,0:T(8,128)(2,1)S(1)}, bf16[96,512]{1,0:T(8,128)(2,1)S(1)}, u32[]{:S(2)}, u32[]{:S(2)}) collective-permute-start(bf16[96,512]{1,0:T(8,128)(2,1)S(1)} %pad_maximum_fusion.6), channel_id=1, source_target_pairs={{0,4},{1,5},{2,6},{3,7},{4,0},{5,1},{6,2},{7,3},{8,12},{9,13},{10,... | collective-permute-start | bytes 294920 | tf_op jit(solution)/shard_map/ppermute | solution.py:586
  172.1 7.6 %collective-permute-start.20 = (bf16[80,512]{1,0:T(8,128)(2,1)S(1)}, bf16[80,512]{1,0:T(8,128)(2,1)S(1)}, u32[]{:S(2)}, u32[]{:S(2)}) collective-permute-start(bf16[80,512]{1,0:T(8,128)(2,1)S(1)} %get-tuple-element.132), channel_id=1, source_target_pairs={{0,4},{1,5},{2,6},{3,7},{4,0},{5,1},{6,2},{7,3},{8,12},{9,13},{10,... | collective-permute-start | bytes 245768 | tf_op jit(solution)/shard_map/ppermute | solution.py:586
  175.9 6.6 %collective-permute-start.19 = (bf16[96,512]{1,0:T(8,128)(2,1)S(1)}, bf16[96,512]{1,0:T(8,128)(2,1)S(1)}, u32[]{:S(2)}, u32[]{:S(2)}) collective-permute-start(bf16[96,512]{1,0:T(8,128)(2,1)S(1)} %pad_maximum_fusion.8), channel_id=1, source_target_pairs={{0,4},{1,5},{2,6},{3,7},{4,0},{5,1},{6,2},{7,3},{8,12},{9,13},{10,... | collective-permute-start | bytes 294920 | tf_op jit(solution)/shard_map/ppermute | solution.py:586
  179.7 5.4 %collective-permute-start.22 = (bf16[160,512]{1,0:T(8,128)(2,1)S(1)}, bf16[160,512]{1,0:T(8,128)(2,1)S(1)}, u32[]{:S(2)}, u32[]{:S(2)}) collective-permute-start(bf16[160,512]{1,0:T(8,128)(2,1)S(1)} %constant_dynamic-update-slice_fusion.19), channel_id=1, source_target_pairs={{0,16},{1,17},{2,18},{3,19},{4,20},{5,21},{6,22},{7,23},{8,24},{9,... | collective-permute-start | bytes 491528 | tf_op jit(solution)/shard_map/ppermute | solution.py:586
  182.6 9.2 %collective-permute-start.21 = (bf16[192,512]{1,0:T(8,128)(2,1)S(1)}, bf16[192,512]{1,0:T(8,128)(2,1)S(1)}, u32[]{:S(2)}, u32[]{:S(2)}) collective-permute-start(bf16[192,512]{1,0:T(8,128)(2,1)S(1)} %pad_maximum_fusion.4), channel_id=1, source_target_pairs={{0,2},{1,3},{2,0},{3,1},{4,6},{5,7},{6,4},{7,5},{8,10},{9,11},{10,... | collective-permute-start | bytes 589832 | tf_op jit(solution)/shard_map/ppermute | solution.py:586
  183.3 6.5 %collective-permute-start.26 = (bf16[128,512]{1,0:T(8,128)(2,1)S(1)}, bf16[128,512]{1,0:T(8,128)(2,1)S(1)}, u32[]{:S(2)}, u32[]{:S(2)}) collective-permute-start(bf16[128,512]{1,0:T(8,128)(2,1)S(1)} %add_convert_fusion.9), channel_id=1, source_target_pairs={{0,2},{1,3},{2,0},{3,1},{4,6},{5,7},{6,4},{7,5},{8,9},{9,8},{10,11... | collective-permute-start | bytes 393224 | tf_op jit(solution)/shard_map/ppermute | solution.py:586
  185.1 11.9 %collective-permute-start.32 = (bf16[320,512]{1,0:T(8,128)(2,1)S(1)}, bf16[320,512]{1,0:T(8,128)(2,1)S(1)}, u32[]{:S(2)}, u32[]{:S(2)}) collective-permute-start(bf16[320,512]{1,0:T(8,128)(2,1)S(1)} %constant_dynamic-update-slice_fusion.15), channel_id=1, source_target_pairs={{0,2},{1,3},{2,0},{3,1},{4,6},{5,7},{6,4},{7,5},{8,9},{9,8},{10,11... | collective-permute-start | bytes 983048 | tf_op jit(solution)/shard_map/ppermute | solution.py:586
  189.8 5.0 %collective-permute-start.27 = (bf16[128,512]{1,0:T(8,128)(2,1)S(1)}, bf16[128,512]{1,0:T(8,128)(2,1)S(1)}, u32[]{:S(2)}, u32[]{:S(2)}) collective-permute-start(bf16[128,512]{1,0:T(8,128)(2,1)S(1)} %add_convert_fusion.8), channel_id=1, source_target_pairs={{0,16},{1,17},{2,18},{3,19},{4,20},{5,21},{6,22},{7,23},{8,24},{9,... | collective-permute-start | bytes 393224 | tf_op jit(solution)/shard_map/ppermute | solution.py:586
  191.9 11.0 %collective-permute-start.31 = (bf16[256,512]{1,0:T(8,128)(2,1)S(1)}, bf16[256,512]{1,0:T(8,128)(2,1)S(1)}, u32[]{:S(2)}, u32[]{:S(2)}) collective-permute-start(bf16[256,512]{1,0:T(8,128)(2,1)S(1)} %slice_dynamic-update-slice_fusion), channel_id=1, source_target_pairs={{0,1},{1,0},{2,3},{3,2},{4,5},{5,4},{6,7},{7,6},{8,24},{9,25},{10,... | collective-permute-start | bytes 786440 | tf_op jit(solution)/shard_map/ppermute | solution.py:586
  193.0 7.3 %collective-permute-start.23 = (bf16[128,512]{1,0:T(8,128)(2,1)S(1)}, bf16[128,512]{1,0:T(8,128)(2,1)S(1)}, u32[]{:S(2)}, u32[]{:S(2)}) collective-permute-start(bf16[128,512]{1,0:T(8,128)(2,1)S(1)} %slice_dynamic-update-slice_fusion.1), channel_id=1, source_target_pairs={{0,1},{1,0},{2,3},{3,2},{4,5},{5,4},{6,7},{7,6},{8,9},{9,8},{10,11... | collective-permute-start | bytes 393224 | tf_op jit(solution)/shard_map/ppermute | solution.py:926
  194.9 7.4 %collective-permute-start.28 = (bf16[128,512]{1,0:T(8,128)(2,1)S(1)}, bf16[128,512]{1,0:T(8,128)(2,1)S(1)}, u32[]{:S(2)}, u32[]{:S(2)}) collective-permute-start(bf16[128,512]{1,0:T(8,128)(2,1)S(1)} %add_convert_fusion.7), channel_id=1, source_target_pairs={{0,4},{1,5},{2,6},{3,7},{4,0},{5,1},{6,2},{7,3},{8,12},{9,13},{10,... | collective-permute-start | bytes 393224 | tf_op jit(solution)/shard_map/ppermute | solution.py:586
  197.0 16.7 %collective-permute-start.35 = (bf16[640,512]{1,0:T(8,128)(2,1)S(1)}, bf16[640,512]{1,0:T(8,128)(2,1)S(1)}, u32[]{:S(2)}, u32[]{:S(2)}) collective-permute-start(bf16[640,512]{1,0:T(8,128)(2,1)S(1)} %constant_dynamic-update-slice_fusion.4), channel_id=1, source_target_pairs={{0,1},{1,0},{2,3},{3,2},{4,5},{5,4},{6,7},{7,6},{8,10},{9,11},{10,... | collective-permute-start | bytes 1966088 | tf_op jit(solution)/shard_map/ppermute | solution.py:586
  202.4 6.1 %collective-permute-start.29 = (bf16[128,512]{1,0:T(8,128)(2,1)S(1)}, bf16[128,512]{1,0:T(8,128)(2,1)S(1)}, u32[]{:S(2)}, u32[]{:S(2)}) collective-permute-start(bf16[128,512]{1,0:T(8,128)(2,1)S(1)} %get-tuple-element.128), channel_id=1, source_target_pairs={{0,2},{1,3},{2,0},{3,1},{4,6},{5,7},{6,4},{7,5},{8,9},{9,8},{10,11... | collective-permute-start | bytes 393224 | tf_op jit(solution)/shard_map/ppermute | solution.py:586
  202.9 13.9 %collective-permute-start.34 = (bf16[512,512]{1,0:T(8,128)(2,1)S(1)}, bf16[512,512]{1,0:T(8,128)(2,1)S(1)}, u32[]{:S(2)}, u32[]{:S(2)}) collective-permute-start(bf16[512,512]{1,0:T(8,128)(2,1)S(1)} %constant_dynamic-update-slice_fusion.3), channel_id=1, source_target_pairs={{0,16},{1,17},{2,18},{3,19},{4,20},{5,21},{6,22},{7,23},{8,9},{9,8... | collective-permute-start | bytes 1572872 | tf_op jit(solution)/shard_map/ppermute | solution.py:586
  208.5 8.0 %collective-permute-start.30 = (bf16[256,512]{1,0:T(8,128)(2,1)S(1)}, bf16[256,512]{1,0:T(8,128)(2,1)S(1)}, u32[]{:S(2)}, u32[]{:S(2)}) collective-permute-start(bf16[256,512]{1,0:T(8,128)(2,1)S(1)} %constant_dynamic-update-slice_fusion.8), channel_id=1, source_target_pairs={{0,1},{1,0},{2,3},{3,2},{4,5},{5,4},{6,7},{7,6},{8,10},{9,11},{10,... | collective-permute-start | bytes 786440 | tf_op jit(solution)/shard_map/ppermute | solution.py:586
  213.8 10.4 %collective-permute-start.36 = (bf16[1280,512]{1,0:T(8,128)(2,1)S(1)}, bf16[1280,512]{1,0:T(8,128)(2,1)}, u32[]{:S(2)}, u32[]{:S(2)}) collective-permute-start(bf16[1280,512]{1,0:T(8,128)(2,1)S(1)} %constant_dynamic-update-slice_fusion.21), channel_id=1, source_target_pairs={{0,8},{1,9},{2,10},{3,11},{4,12},{5,13},{6,14},{7,15},{8,0},{9,1},... | collective-permute-start | bytes 3932168 | tf_op jit(solution)/shard_map/ppermute | solution.py:586
  216.6 2.0 collective-permute-start.33
  216.8 10.5 %collective-permute-start.37 = (bf16[1024,512]{1,0:T(8,128)(2,1)S(1)}, bf16[1024,512]{1,0:T(8,128)(2,1)}, u32[]{:S(2)}, u32[]{:S(2)}) collective-permute-start(bf16[1024,512]{1,0:T(8,128)(2,1)S(1)} %constant_dynamic-update-slice_fusion.24), channel_id=1, source_target_pairs={{0,8},{1,9},{2,10},{3,11},{4,12},{5,13},{6,14},{7,15},{8,0},{9,1},... | collective-permute-start | bytes 3145736 | tf_op jit(solution)/shard_map/ppermute | solution.py:586
  218.6 1.0 copy-start

commit v4 on v3

--- a/solution.py
+++ b/solution.py
@@ -94,8 +94,8 @@
 
 
 def table_kernel(
-    embed, gain, shift, weight, cot, frontier_weight,
-    normed_out, table_out, key_out, value_out, stack_out,
+    embed, gain, shift, weight,
+    normed_out, table_out, key_out, value_out,
 ):
     rows = embed[...].astype(F32)
     centered = rows - jnp.mean(rows, -1, keepdims=True)
@@ -109,14 +109,11 @@
     table_out[:, model_width:] = table[:, model_width:].astype(BF16)
     key_out[...] = table[:, model_width : 2 * model_width].T.astype(BF16)
     value_out[...] = table[:, 2 * model_width :].T.astype(BF16)
-    rim_high, rim_low = split_two(
-        jnp.where(iota((STACK - NB, model_width), 0) == 0, frontier_weight[...], 0.0)
-    )
-    for item in range(cot.shape[0]):
-        high, low = split_two(cot[item])
-        for at, (block, rim) in enumerate(((high, rim_high), (high, rim_high), (low, rim_low))):
-            stack_out[item, at * STACK : at * STACK + NB] = block
-            stack_out[item, at * STACK + NB : (at + 1) * STACK] = rim
+
+
+def stacked_cot(cot, frontier_weight):
+    rim = jnp.where(iota((STACK - NB, cot.shape[1]), 0) == 0, frontier_weight, 0.0)
+    return split_two(jnp.concatenate([cot, rim], 0))
 
 
 def take_turns(*parts):
@@ -129,7 +126,7 @@
 
 def forward_kernel(
     place, lengths, ids_row, table, value_table, embed, out_weight, gain, shift,
-    up_weight, up_bias, down_weight, down_bias, cot_stack,
+    up_weight, up_bias, down_weight, down_bias, cot, frontier_weight,
     attended_out, log_out, middle_out, normed_out, act_out, slope_out, high_out, low_out,
     inner_out, frontier_out, running_out,
     bias, query_keys, value_columns, triangle, held_hot, held_attended,
@@ -212,8 +209,9 @@
         high, low = split_two(hidden)
         high_out[0] = high
         low_out[0] = low
-        products = dot_last(cot_stack[0, STACK:, :], high)
-        inner = products[:STACK] + products[STACK:] + dot_last(cot_stack[0, :STACK, :], low)
+        cot_high, cot_low = stacked_cot(cot[0], frontier_weight[...])
+        products = dot_last(jnp.concatenate([cot_high, cot_low], 0), high)
+        inner = products[:STACK] + products[STACK:] + dot_last(cot_high, low)
         inner_out[0] = inner[:NB]
         frontier = 1.0 / (1.0 + jnp.exp(-inner[NB : NB + 1]))
         frontier_out[0] = frontier
@@ -236,13 +234,12 @@
         take_turns(feed())
 
 
-def assignment(place, lengths, counts, before, total, running):
-    item = pl.program_id(0)
+def assignment(place, lengths, counts, before, total, running, item, held=0):
     span = running.shape[2]
     slot = place[0] + iota((1, span), 1)
     inside = slot < lengths[item]
     count = counts[item].astype(F32)
-    position = count * (running[0] + before[item]) / total[item]
+    position = count * (running[held] + before[item]) / total[item]
     block_at = iota((NB, span), 0)
     distance = position - (block_at.astype(F32) + 0.5)
     kept = inside & (block_at < counts[item])
@@ -251,20 +248,26 @@
 
 
 def stats_kernel(place, lengths, counts, before, total, running, inner, stats_out):
-    position, assign, pull, _, _ = assignment(place, lengths, counts, before, total, running)
-    pull_inner = pull * inner[0]
     lane = iota((NB, 128), 1)
-    stats = jnp.zeros((NB, 128), F32)
-    terms = (
-        assign, assign * inner[0], pull, pull_inner, pull * position, pull_inner * position,
-    )
-    for at, cells in enumerate(terms):
-        stats = jnp.where(lane == at, jnp.sum(cells, 1, keepdims=True), stats)
-    stats_out[0] = stats.T[:8]
+    for item in range(inner.shape[0]):
+        position, assign, pull, _, _ = assignment(
+            place, lengths, counts, before, total, running, item, item
+        )
+        products = inner[item]
+        pull_inner = pull * products
+        stats = jnp.zeros((NB, 128), F32)
+        terms = (
+            assign, assign * products, pull, pull_inner, pull * position, pull_inner * position,
+        )
+        for at, cells in enumerate(terms):
+            stats = jnp.where(lane == at, jnp.sum(cells, 1, keepdims=True), stats)
+        stats_out[item] = stats.T[:8]
 
 
 def numer_kernel(place, lengths, counts, before, total, running, high, low, numer_out):
-    _, assign, _, _, _ = assignment(place, lengths, counts, before, total, running)
+    _, assign, _, _, _ = assignment(
+        place, lengths, counts, before, total, running, pl.program_id(0)
+    )
     assign_high, assign_low = split_two(assign)
     numer_out[0] = (
         dot(assign_high, high[0]) + dot(assign_low, high[0]) + dot(assign_high, low[0])
@@ -278,7 +281,7 @@
     item = pl.program_id(0)
     span = running.shape[2]
     position, assign, pull, inside, count = assignment(
-        place, lengths, counts, before, total, running
+        place, lengths, counts, before, total, running, item
     )
     whole_columns = whole_stats[0].T
     after_columns = after_stats[0].T
@@ -316,7 +319,7 @@
 
 def back_kernel(
     place, lengths, counts, before, total, running, frontier, inner, whole_stats, after_stats,
-    cot_stack, ids_row, act, slope, high, low, middle, normed, attended, gain, down_weight,
+    cot, frontier_weight, ids_row, act, slope, high, low, middle, normed, attended, gain, down_weight,
     up_weight, out_weight,
     down_sent, down_kept, up_sent, up_kept, attended_out, embed_out, rows_out,
     triangle, down_total, up_total,
@@ -335,7 +338,11 @@
         place, lengths, counts, before, total, running, frontier, inner, whole_stats,
         after_stats, triangle,
     )
-    d_hidden = dot_first(jnp.concatenate([left_high, left_low, left_high], 0), cot_stack[0])
+    cot_high, cot_low = stacked_cot(cot[0], frontier_weight[...])
+    d_hidden = dot_first(
+        jnp.concatenate([left_high, left_low, left_high], 0),
+        jnp.concatenate([cot_high, cot_high, cot_low], 0),
+    )
     d_low = d_hidden.astype(BF16)
     cuts = [
         slice(begin, begin + model_width) for begin in range(0, hidden_width, model_width)
@@ -380,13 +387,10 @@
     def _():
         write_halves(place, down_total, down_sent, down_kept)
         write_halves(place, up_total, up_sent, up_kept)
-        rows = up_kept.shape[0]
-        high, low = split_two(rows_out[...])
-        up_sent[rows:] = jnp.concatenate([high, low], 0)
 
 
 def attend_back_kernel(
-    place, ids_row, table, key_table, d_attended, logs, rows_in,
+    place, ids_row, table, key_table, d_attended, logs, rows_in, vectors,
     *outs_and_scratch,
 ):
     *outs, rows_total, bias, table_rows, key_columns, d_queries, d_keys, d_values, (
@@ -454,17 +458,64 @@
     @pl.when(item == pl.num_programs(0) - 1)
     def _():
         rows_total[vocab : 2 * vocab] += queries_total[...].T
-        if len(outs) == 2:
-            write_halves(place, rows_total, *outs)
-        else:
-            outs[0][...] = rows_total[...]
+        write_halves(place, rows_total, *outs)
+        vectors_high, vectors_low = split_two(vectors[...])
+        outs[0][outs[1].shape[0] :] = jnp.concatenate([vectors_high, vectors_low], 0)
 
 
 def finish_kernel(
-    embed, normed, gain, weight, sums,
-    embed_out, weight_out, gain_out, shift_out,
+    place, embed, normed, gain, weight, numer, stats, *refs,
 ):
+    far = refs[:6]
+    embed_out, gain_out, shift_out, pooled_out, down_out, up_out, out_out, weight_out = refs[6:14]
+    near = refs[14:20]
+    down_held, up_held, out_held, weight_held, arrived, left = refs[20:]
     vocab, model_width = embed.shape
+    moves = [
+        pltpu.make_async_copy(source, target, arrived.at[at])
+        for at, (source, target) in enumerate(zip(far, near))
+    ]
+    sent = []
+
+    def send(source, target):
+        move = pltpu.make_async_copy(source, target, left.at[len(sent)])
+        move.start()
+        sent.append(move)
+
+    def sides(at):
+        moves[2 * at].wait()
+        moves[2 * at + 1].wait()
+        mine, came = near[2 * at][...], near[2 * at + 1][...]
+        return [jnp.where(place[3] == core, mine, came) for core in (0, 1)]
+
+    for move in moves:
+        move.start()
+    for core, side in enumerate(sides(0)):
+        half = side.shape[0]
+        for begin in range(0, half, half // 2):
+            own = slice(core * half + begin, core * half + begin + half // 2)
+            down_held[own] = side[begin : begin + half // 2].astype(F32)
+            send(down_held.at[own], down_out.at[own])
+    for core, side in enumerate(sides(1)):
+        half = side.shape[0]
+        step = model_width // 2
+        for begin in range(0, half, step):
+            lane, row = divmod(core * half + begin, model_width)
+            cells = side[begin : begin + step].astype(F32)
+            lanes = slice(lane * model_width, (lane + 1) * model_width)
+            if lane * model_width < up_held.shape[1]:
+                up_held[row : row + step, lanes] = cells
+                if row:
+                    send(up_held.at[:, lanes], up_out.at[:, lanes])
+            else:
+                out_held[row : row + step] = cells
+                if row:
+                    send(out_held, out_out)
+    for item in range(stats.shape[0]):
+        own = slice(item * NB, (item + 1) * NB)
+        inverse = 1.0 / (stats[item].T[:, 0:1] + 1.0)
+        pooled_out[item] = numer[own].astype(F32) * inverse
+    sums = jnp.concatenate(sides(2), 0)
     rows = embed[...].astype(F32)
     centered = rows - jnp.mean(rows, -1, keepdims=True)
     scale = lax.rsqrt(jnp.mean(centered * centered, -1, keepdims=True) + eps)
@@ -473,7 +524,8 @@
     for at in range(3):
         lanes = slice(at * model_width, (at + 1) * model_width)
         part = sums[(at + 1) * vocab : (at + 2) * vocab]
-        weight_out[:, lanes] = dot_first(normed[...], part)
+        weight_held[:, lanes] = dot_first(normed[...], part)
+        send(weight_held.at[:, lanes], weight_out.at[:, lanes])
         back = dot_last(part, weight[:, lanes])
         d_normed = back if d_normed is None else d_normed + back
     gain_out[...] = jnp.sum(d_normed * unit, 0, keepdims=True)
@@ -484,6 +536,8 @@
         - jnp.mean(pushed, -1, keepdims=True)
         - unit * jnp.mean(pushed * unit, -1, keepdims=True)
     )
+    for move in sent:
+        move.wait()
 
 
 def whole(shape):
@@ -626,8 +680,8 @@
             moved = [self.cells]
         else:
             moved = [self.sent]
-            if self.vectors is not None and step > 0:
-                moved += split_two_outside(self.vectors)
+        if self.vectors is not None and kind == "sum" and step > 0:
+            moved += split_two_outside(self.vectors)
         if self.rider is not None and self.exchange.shared(step):
             if kind == "sum":
                 away, self.rider = halves(self.rider, self.exchange.side(step))
@@ -646,12 +700,12 @@
             rows = self.cells.shape[0]
             if self.rider is not None and self.exchange.shared(step):
                 self.rider = joined(self.rider.astype(BF16), came[rows:], side)
-            self.cells = joined(self.cells, came[:rows], side)
+            if step == 0:
+                self.last = came
+            else:
+                self.cells = joined(self.cells, came[:rows], side)
             return
-        if step >= self.stop:
-            self.cells = (self.cells.astype(F32) + came.astype(F32)).astype(BF16)
-            return
-        half = self.kept.shape[0]
+        half = self.cells.shape[0] if step >= self.stop else self.kept.shape[0]
         if self.vectors is not None:
             rows = self.vectors.shape[0]
             high, low = split_two_outside(self.vectors)
@@ -659,6 +713,9 @@
                 came[half : half + rows].astype(F32)
                 + came[half + rows : half + 2 * rows].astype(F32)
             )
+        if step >= self.stop:
+            self.cells = (self.cells.astype(F32) + came[:half].astype(F32)).astype(BF16)
+            return
         if self.rider is not None and self.exchange.shared(step):
             self.rider = self.rider + came[half : half + self.rider.shape[0]].astype(F32)
         if step + 1 == self.stop:
@@ -717,23 +774,20 @@
     ids_row = ids_wide[:, None, :]
     ids_own = byte_ids[:, None, :]
 
-    normed_one, table, key_table, value_table, cot_stack = call(
+    normed_one, table, key_table, value_table = call(
         table_kernel,
         1,
         [whole((vocab, model_width)), whole((1, model_width)), whole((1, model_width)),
-         whole((model_width, 3 * model_width)), whole((items, NB, model_width)),
-         whole((1, model_width))],
+         whole((model_width, 3 * model_width))],
         [
             total_out((vocab, model_width), BF16),
             total_out((vocab, 3 * model_width), BF16),
             total_out((model_width, vocab), BF16),
             total_out((model_width, vocab), BF16),
-            total_out((items, 3 * STACK, model_width), BF16),
         ],
         [],
         6 * vocab * model_width * model_width,
-        (byte_embed, norm1_gain[None], norm1_shift[None], qkv_weight, pooled_cot,
-         frontier_weight[None]),
+        (byte_embed, norm1_gain[None], norm1_shift[None], qkv_weight),
     )
 
     first = (seq_place == 0).astype(jnp.int32)
@@ -773,7 +827,7 @@
                 (hidden_width, model_width), (1, model_width),
             )
         ]
-        + [item_behind((3 * STACK, model_width))],
+        + [item_behind((NB, model_width)), whole((1, model_width))],
         [
             (item_ahead(square), (items,) + square, BF16),
             (item_ahead(logs_shape), (items,) + logs_shape, F32),
@@ -797,7 +851,7 @@
         (
             place, item_lengths, ids_row, table, value_table, byte_embed, out_weight,
             norm2_gain[None], norm2_shift[None], up_weight, up_bias[None], down_weight,
-            down_bias[None], cot_stack,
+            down_bias[None], pooled_cot, frontier_weight[None],
         ),
     )
 
@@ -807,9 +861,9 @@
 
     (stats,) = call(
         stats_kernel,
-        items,
-        numbers_specs + [per_item(blocks)],
-        [item_out(items, (8, NB), F32)],
+        1,
+        [scalars()] * 5 + [whole((items,) + row), whole((items,) + blocks)],
+        [total_out((items, 8, NB))],
         [],
         tokens * NB,
         numbers + (inner,),
@@ -841,7 +895,7 @@
             near_came.append(lax.ppermute(away, "seq", pairs))
     back_specs = numbers_specs + [
         per_item(row), per_item(blocks), per_item((8, NB)), per_item((8, NB)),
-        per_item((3 * STACK, model_width)),
+        per_item((NB, model_width)), whole((1, model_width)),
     ]
     (
         down_sent, down_kept, up_sent, up_kept, d_attended, d_embed_direct, rows,
@@ -854,7 +908,7 @@
         + [whole((1, model_width)), whole((hidden_width, model_width)),
            whole((model_width, hidden_width)), whole((model_width, model_width))],
         halves_out(hidden_width, model_width)
-        + halves_out(hidden_width + model_width, model_width, 16)
+        + halves_out(hidden_width + model_width, model_width)
         + [
             item_out(items, square, BF16),
             total_out((vocab, model_width)),
@@ -867,13 +921,13 @@
         ],
         6 * tokens * hidden_width * model_width,
         numbers
-        + (frontier, inner, stats_whole, stats_after, cot_stack, ids_own, act, slope,
+        + (frontier, inner, stats_whole, stats_after, pooled_cot, frontier_weight[None], ids_own, act, slope,
            hidden_high, hidden_low, middle, normed_two, attended, norm2_gain[None],
            down_weight, up_weight, out_weight),
     )
 
     down = Chain(down_exchange, down_sent, down_kept)
-    up = Chain(Exchange(False), up_sent, up_kept, rows)
+    up = Chain(Exchange(False), up_sent, up_kept)
     down.run(1)
     up.run(1)
     down.sent, up.sent, d_attended, near_came = lax.optimization_barrier(
@@ -887,8 +941,8 @@
         items,
         [scalars(), per_item((1, wide)), whole((vocab, 3 * model_width)),
          whole((model_width, vocab)), per_item(square), per_item((tiles * H // 2, 2 * TILE)),
-         whole((vocab, model_width))],
-        halves_out(4 * vocab, model_width),
+         whole((vocab, model_width)), whole((8, model_width))],
+        halves_out(4 * vocab, model_width, 16),
         [
             pltpu.VMEM((4 * vocab, model_width), F32),
             pltpu.VMEM((3, SPAN_KEYS, 2 * TILE), F32),
@@ -900,13 +954,19 @@
             pltpu.VMEM((model_width, vocab), F32),
         ],
         10 * tokens * SPAN_KEYS * model_width,
-        (place, ids_row, table, key_table, d_attended, logs, d_embed_direct),
+        (place, ids_row, table, key_table, d_attended, logs, d_embed_direct, rows),
     )
 
     rows_sent, down.came, up.came = lax.optimization_barrier((rows_sent, down.came, up.came))
-    table_rows = Chain(Exchange(False), rows_sent, rows_kept, stop=exchange_steps - 2)
-    chains = (up, down, table_rows)
-    while any(chain.at < len(chain.plan) for chain in chains):
+    table_rows = Chain(Exchange(False), rows_sent, rows_kept, rows, stop=exchange_steps - 2)
+    numer = None
+    ready = max(
+        step for step in range(1, exchange_steps) if not down_exchange.shared(step)
+    )
+    turn = 0
+    while any(chain.at < len(chain.plan) for chain in (up, down, table_rows)):
+        chains = (table_rows, up, down) if turn < 1 else (up, down, table_rows)
+        turn += 1
         ahead = None
         for chain in chains:
             if chain.at == len(chain.plan):
@@ -915,39 +975,45 @@
                 chain.start()
             if ahead is not None:
                 chain.came, _ = lax.optimization_barrier((chain.came, ahead))
+            if numer is None and down.plan[down.at] == ("gather", ready):
+                numer = down.rider
+                for side, pairs in reversed(near[1:]):
+                    numer = joined(numer, lax.ppermute(numer, "seq", pairs), side)
+                numer_came = lax.ppermute(numer, "seq", near[0][1])
+            if chain is table_rows and chain.plan[chain.at] == ("gather", 1):
+                chain.came, numer_came = lax.optimization_barrier((chain.came, numer_came))
+                numer = joined(numer, numer_came, near[0][0])
             chain.finish()
             ahead = chain.sent if chain.cells is None else chain.cells
-    d_rows = table_rows.cells
-    d_weights = up.cells.astype(F32)
-    d_down = down.cells.astype(F32)
-    rows = up.vectors
-    numer = down.rider
-    for side, pairs in reversed(near):
-        numer = joined(numer, lax.ppermute(numer, "seq", pairs), side)
-    inverse = 1.0 / (stats_whole[:, 0] + 1.0)
-    pooled = numer.astype(F32).reshape(items, NB, model_width) * inverse[:, :, None]
-    d_up = jnp.concatenate(
-        [
-            d_weights[begin : begin + model_width]
-            for begin in range(0, hidden_width, model_width)
-        ],
-        1,
-    )
-    d_out = d_weights[hidden_width:]
-    d_embed, d_qkv, d_gain_one, d_shift_one = call(
+    rows = table_rows.vectors
+    arrived = [
+        cells for chain in (down, up, table_rows) for cells in (chain.cells, chain.last)
+    ]
+    grads = (
+        (hidden_width, model_width), (model_width, hidden_width), (model_width, model_width),
+        (model_width, 3 * model_width),
+    )
+    anywhere = pl.BlockSpec(memory_space=pl.ANY)
+    d_embed, d_gain_one, d_shift_one, pooled, d_down, d_up, d_out, d_qkv = call(
         finish_kernel,
         1,
-        [whole((vocab, model_width)), whole((vocab, model_width)), whole((1, model_width)),
-         whole((model_width, 3 * model_width)), whole((4 * vocab, model_width))],
+        [scalars(), whole((vocab, model_width)), whole((vocab, model_width)),
+         whole((1, model_width)), whole((model_width, 3 * model_width)),
+         whole((items * NB, model_width)), whole((items, 8, NB))]
+        + [anywhere] * 6,
         [
             total_out((vocab, model_width)),
-            total_out((model_width, 3 * model_width)),
             total_out((1, model_width)),
             total_out((1, model_width)),
-        ],
-        [],
+            total_out((items, NB, model_width)),
+        ]
+        + [(anywhere, shape, F32) for shape in grads],
+        [pltpu.VMEM(cells.shape, BF16) for cells in arrived]
+        + [pltpu.VMEM(shape, F32) for shape in grads]
+        + [pltpu.SemaphoreType.DMA((6,)), pltpu.SemaphoreType.DMA((12,))],
         8 * vocab * model_width * model_width,
-        (byte_embed, normed_one, norm1_gain[None], qkv_weight, d_rows),
+        (place, byte_embed, normed_one, norm1_gain[None], qkv_weight, numer, stats_whole,
+         *arrived),
     )
     return (
         pooled,

time: 234 us -> 232 us (level)
  other arithmetic: 13.9 us -> 7.91 us
  local copies, waits for them, and re-layouts: 14.3 us -> 11.4 us
  waiting for transfers between devices: 47.6 us -> 50.1 us
    ppermute x28, waiting for transfers between devices: 38.9 us -> 42.8 us  [swap(): return lax.ppermute(cells, ('dp', 'seq'), pairs)]
    unnamed x30 -> x36, local copies, waits for them, and re-layouts: 2.14 us -> 4.95 us
    dynamic_update_slice x16 -> x13, local copies, waits for them, and re-layouts: 3.06 us -> 0.25 us  [joined(): return lax.dynamic_update_slice_in_dim(cells, came, (1 - side) * half, 0)]
    ppermute x28, starting transfers between devices: 29.5 us -> 32.1 us  [swap(): return lax.ppermute(cells, ('dp', 'seq'), pairs)]
    convert_element_type x2 -> x1, other arithmetic: 2.64 us -> 0.03 us  [finish(): self.cells = (self.cells.astype(F32) + came[:half].astype(F32)).astype(BF16)]
    concatenate x1 -> x0, other arithmetic: 2.39 us -> none  [local(): jnp.concatenate([d_weights[begin:begin + model_width] for begin in range(...]
  transfers between devices with their start and end apart: 38 -> 38, of which waited for: 22 -> 23; matrix products, arithmetic and copies ran while one was open for 6% -> 4% of each run, Pallas kernels for 14% -> 12%
where the time goes in v4:
time: 232 us
  Pallas kernels  107 us (46%)
  starting transfers between devices  53.7 us (23%)
  waiting for transfers between devices  50.1 us (22%)
  local copies, waits for them, and re-layouts  11.4 us (5%)
  other arithmetic  7.91 us (3%)
    pallas_call x7, Pallas kernels, call(): pl.pallas_call(kernel, grid=(items,), in_specs=in_specs, out_specs=[spec...  107 us
    ppermute x28, waiting for transfers between devices, swap(): return lax.ppermute(cells, ('dp', 'seq'), pairs)  42.8 us
    ppermute x28, starting transfers between devices, swap(): return lax.ppermute(cells, ('dp', 'seq'), pairs)  32.1 us
    ppermute x6, starting transfers between devices, scan_over(): other = lax.ppermute(cells, axis, [(at, at ^ bit) for at in range(count)])  13.8 us
    ppermute x6, waiting for transfers between devices, scan_over(): other = lax.ppermute(cells, axis, [(at, at ^ bit) for at in range(count)])  7.14 us
    unnamed x36, local copies, waits for them, and re-layouts  4.95 us
    ppermute x1, starting transfers between devices, local(): lax.ppermute(byte_ids[:, span - WIN:], 'seq', [(at, at + 1) for at in ends])  4.86 us
  transfers between devices with their start and end apart: 38, of which 23 were waited for; matrix products, arithmetic and copies ran while one was open for 4% of the time, Pallas kernels for 12%

profile of v4, /device:TPU:0, one launch (start us, length us, event | category | flops | bytes accessed | tf_op | source)
XLA Modules:
  0.0 231.7 jit_solution(8155178860364319251)
XLA Ops:
  0.7 0.8 fusion.8
  1.5 4.9 %collective-permute-start = (s32[4,64]{1,0:T(4,128)S(1)}, s32[4,64]{1,0:T(4,128)S(1)}, u32[]{:S(2)}, u32[]{:S(2)}) collective-permute-start(s32[4,64]{1,0:T(4,128)S(1)} %get-tuple-element.173), channel_id=1, source_target_pairs={{0,1},{1,2},{2,3},{3,4},{4,5},{5,6},{6,7},{8,9},{9,10},{10,11},{11... | collective-permute-start | bytes 3080 | tf_op jit(solution)/shard_map/ppermute | solution.py:768
  6.3 1.3 collective-permute-start.1
  8.3 3.4 %shard_map.255 = (bf16[256,512]{1,0:T(8,128)(2,1)}, bf16[256,1536]{1,0:T(8,128)(2,1)}, bf16[512,256]{1,0:T(8,128)(2,1)}, bf16[512,256]{1,0:T(8,128)(2,1)}) custom-call(bf16[256,512]{1,0:T(8,128)(2,1)} %embed.5, f32[1,512]{1,0:T(1,128)} %bitcast.28, f32[1,512]{1,0:T(1,128)} %bitcast.33, bf16[512,1536]{1,0:T(8,128)(2,1)} %weight.3), custom_call_target="tpu_custom_call" | custom-call | flops 1 | tf_op jit(solution)/shard_map/pallas_call | solution.py:562
  12.5 32.3 %shard_map.256 = (bf16[4,512,512]{2,1,0:T(8,128)(2,1)}, f32[4,16,256]{2,1,0:T(8,128)}, f32[4,512,512]{2,1,0:T(8,128)}, bf16[4,512,512]{2,1,0:T(8,128)(2,1)}, bf1...) custom-call(s32[4]{0:T(128)} %pad_add_fusion.1.place, ...), custom_call_target="tpu_custom_call" | custom-call | flops 1 | tf_op jit(solution)/shard_map/pallas_call | solution.py:562
  44.8 0.8 slice_reduce_fusion
  45.7 2.5 %collective-permute-start.2 = (f32[4]{0:T(128)S(1)}, f32[4]{0:T(128)S(1)}, u32[]{:S(2)}, u32[]{:S(2)}) collective-permute-start(f32[4]{0:T(128)S(1)} %slice_reduce_fusion), channel_id=1, source_target_pairs={{0,1},{1,0},{2,3},{3,2},{4,5},{5,4},{6,7},{7,6},{8,9},{9,8},{10,11... | collective-permute-start | bytes 56 | tf_op jit(solution)/shard_map/ppermute | solution.py:597
  48.2 1.5 collective-permute-done.2
  49.7 3.0 %collective-permute-start.3 = (f32[4]{0:T(128)S(1)}, f32[4]{0:T(128)S(1)}, u32[]{:S(2)}, u32[]{:S(2)}) collective-permute-start(f32[4]{0:T(128)S(1)} %add.269), channel_id=1, source_target_pairs={{0,2},{1,3},{2,0},{3,1},{4,6},{5,7},{6,4},{7,5},{8,10},{9,11},{10,... | collective-permute-start | bytes 56 | tf_op jit(solution)/shard_map/ppermute | solution.py:597
  52.7 1.5 collective-permute-done.3
  54.2 3.0 %collective-permute-start.4 = (f32[4]{0:T(128)S(1)}, f32[4]{0:T(128)S(1)}, u32[]{:S(2)}, u32[]{:S(2)}) collective-permute-start(f32[4]{0:T(128)S(1)} %add.271), channel_id=1, source_target_pairs={{0,4},{1,5},{2,6},{3,7},{4,0},{5,1},{6,2},{7,3},{8,12},{9,13},{10,... | collective-permute-start | bytes 56 | tf_op jit(solution)/shard_map/ppermute | solution.py:597
  57.3 1.5 collective-permute-done.4
  59.3 2.2 shard_map.257
  61.6 0.9 collective-permute-start.5
  62.5 4.6 %shard_map.258 = f32[4,64,512]{2,1,0:T(8,128)} custom-call(s32[4]{0:T(128)} %pad_add_fusion.1.place, s32[4]{0:T(128)} %lengths.7, s32[4]{0:T(128)} %counts.5, f32[4]{0:T(128)} %get-tuple-element.176.before, f32[4]{0:T(128)} %get-tuple-element.175.total, f32[4,1,512]{2,1,0:T(1,128)} %get-tuple-element.78.running, ...), custom_call_target="tpu_custom_call" | custom-call | flops 1 | tf_op jit(solution)/shard_map/pallas_call | solution.py:562
  67.1 1.7 collective-permute-start.6
  69.4 1.5 collective-permute-done.6
  70.9 2.6 %collective-permute-start.7 = (f32[4,8,64]{2,1,0:T(8,128)S(1)}, f32[4,8,64]{2,1,0:T(8,128)S(1)}, u32[]{:S(2)}, u32[]{:S(2)}) collective-permute-start(f32[4,8,64]{2,1,0:T(8,128)S(1)} %add.276), channel_id=1, source_target_pairs={{0,4},{1,5},{2,6},{3,7},{4,0},{5,1},{6,2},{7,3},{8,12},{9,13},{10,... | collective-permute-start | bytes 24584 | tf_op jit(solution)/shard_map/ppermute | solution.py:597
  73.6 1.0 dynamic-slice_convert_fusion
  74.5 1.0 collective-permute-done.7
  76.2 35.0 %shard_map.259 = (bf16[1024,512]{1,0:T(8,128)(2,1)}, bf16[1024,512]{1,0:T(8,128)(2,1)}, bf16[1280,512]{1,0:T(8,128)(2,1)}, bf16[1280,512]{1,0:T(8,128)(2,1)}, bf...) custom-call(s32[4]{0:T(128)} %pad_add_fusion.1.place, s32[4]{0:T(128)} %lengths.7, s32[4]{0:T(128)} %counts.5, ...), custom_call_target="tpu_custom_call" | custom-call | flops 1 | tf_op jit(solution)/shard_map/pallas_call | solution.py:562
  111.7 1.1 collective-permute-start.10
  112.8 3.1 %collective-permute-done.8 = bf16[1024,512]{1,0:T(8,128)(2,1)S(1)} collective-permute-done((bf16[1024,512]{1,0:T(8,128)(2,1)}, bf16[1024,512]{1,0:T(8,128)(2,1)S(1)}, u32[]{:S(2)}, u32[]{:S(2)}) %collective-permute-start.8) | collective-permute-done | bytes 1048608 | tf_op jit(solution)/shard_map/ppermute | solution.py:640
  116.0 1.6 convert_add_fusion.1
  117.6 1.0 copy-done.6
  118.6 1.6 convert_add_fusion
  120.3 1.2 collective-permute-start.12
  121.5 1.5 collective-permute-start.11
  123.0 20.7 %shard_map.260 = (bf16[528,512]{1,0:T(8,128)(2,1)}, bf16[512,512]{1,0:T(8,128)(2,1)}) custom-call(s32[4]{0:T(128)} %pad_add_fusion.1.place, s32[4,1,640]{2,1,0:T(1,128)} %broadcast_in_dim.63.ids_row, bf16[256,1536]{1,0:T(8,128)(2,1)} %get-tuple-element.76.table, bf16[512,256]{1,0:T(8,128)(2,1)} %get-tuple-element.98.key_table, ...), custom_call_target="tpu_custom_call" | custom-call | flops 1 | tf_op jit(solution)/shard_map/pallas_call | solution.py:562
  143.6 0.8 copy-done.11
  144.4 1.0 convert_add_fusion.7
  145.4 1.3 collective-permute-done.13
  146.7 1.1 slice.124
  148.2 2.0 collective-permute-start.15
  150.3 0.7 collective-permute-start.14
  151.0 0.7 reduce-precision_convert_fusion.3
  151.8 1.5 collective-permute-start.24
  153.2 3.7 %collective-permute-done.15 = bf16[320,512]{1,0:T(8,128)(2,1)S(1)} collective-permute-done((bf16[320,512]{1,0:T(8,128)(2,1)S(1)}, bf16[320,512]{1,0:T(8,128)(2,1)S(1)}, u32[]{:S(2)}, u32[]{:S(2)}) %collective-permute-start.15) | collective-permute-done | bytes 327712 | tf_op jit(solution)/shard_map/ppermute | solution.py:640
  157.4 2.9 %collective-permute-done.24 = bf16[272,512]{1,0:T(8,128)(2,1)S(1)} collective-permute-done((bf16[272,512]{1,0:T(8,128)(2,1)S(1)}, bf16[272,512]{1,0:T(8,128)(2,1)S(1)}, u32[]{:S(2)}, u32[]{:S(2)}) %collective-permute-start.24) | collective-permute-done | bytes 278560 | tf_op jit(solution)/shard_map/ppermute | solution.py:640
  160.3 1.4 collective-permute-start.17
  161.8 1.2 collective-permute-start.16
  163.0 1.0 collective-permute-start.25
  164.0 1.7 collective-permute-done.17
  165.7 3.0 %collective-permute-start.19 = (bf16[80,512]{1,0:T(8,128)(2,1)S(1)}, bf16[80,512]{1,0:T(8,128)(2,1)S(1)}, u32[]{:S(2)}, u32[]{:S(2)}) collective-permute-start(bf16[80,512]{1,0:T(8,128)(2,1)S(1)} %add_convert_fusion.12), channel_id=1, source_target_pairs={{0,4},{1,5},{2,6},{3,7},{4,0},{5,1},{6,2},{7,3},{8,12},{9,13},{10,... | collective-permute-start | bytes 245768 | tf_op jit(solution)/shard_map/ppermute | solution.py:640
  168.8 1.2 collective-permute-done.25
  170.1 0.7 collective-permute-start.26
  170.8 3.4 %collective-permute-start.18 = (bf16[96,512]{1,0:T(8,128)(2,1)S(1)}, bf16[96,512]{1,0:T(8,128)(2,1)S(1)}, u32[]{:S(2)}, u32[]{:S(2)}) collective-permute-start(bf16[96,512]{1,0:T(8,128)(2,1)S(1)} %pad_maximum_fusion.6), channel_id=1, source_target_pairs={{0,4},{1,5},{2,6},{3,7},{4,0},{5,1},{6,2},{7,3},{8,12},{9,13},{10,... | collective-permute-start | bytes 294920 | tf_op jit(solution)/shard_map/ppermute | solution.py:640
  174.7 2.4 %collective-permute-done.18 = bf16[96,512]{1,0:T(8,128)(2,1)S(1)} collective-permute-done((bf16[96,512]{1,0:T(8,128)(2,1)S(1)}, bf16[96,512]{1,0:T(8,128)(2,1)S(1)}, u32[]{:S(2)}, u32[]{:S(2)}) %collective-permute-start.18) | collective-permute-done | bytes 98336 | tf_op jit(solution)/shard_map/ppermute | solution.py:640
  177.2 3.0 %collective-permute-start.20 = (bf16[96,512]{1,0:T(8,128)(2,1)S(1)}, bf16[96,512]{1,0:T(8,128)(2,1)S(1)}, u32[]{:S(2)}, u32[]{:S(2)}) collective-permute-start(bf16[96,512]{1,0:T(8,128)(2,1)S(1)} %pad_maximum_fusion.7), channel_id=1, source_target_pairs={{0,4},{1,5},{2,6},{3,7},{4,0},{5,1},{6,2},{7,3},{8,12},{9,13},{10,... | collective-permute-start | bytes 294920 | tf_op jit(solution)/shard_map/ppermute | solution.py:640
  180.2 3.9 %collective-permute-done.21 = bf16[80,512]{1,0:T(8,128)(2,1)S(1)} collective-permute-done((bf16[80,512]{1,0:T(8,128)(2,1)S(1)}, bf16[80,512]{1,0:T(8,128)(2,1)S(1)}, u32[]{:S(2)}, u32[]{:S(2)}) %collective-permute-start.21) | collective-permute-done | bytes 81952 | tf_op jit(solution)/shard_map/ppermute | solution.py:640
  184.1 1.3 collective-permute-start.23
  186.1 3.8 %collective-permute-start.22 = (bf16[192,512]{1,0:T(8,128)(2,1)S(1)}, bf16[192,512]{1,0:T(8,128)(2,1)S(1)}, u32[]{:S(2)}, u32[]{:S(2)}) collective-permute-start(bf16[192,512]{1,0:T(8,128)(2,1)S(1)} %pad_maximum_fusion.2), channel_id=1, source_target_pairs={{0,2},{1,3},{2,0},{3,1},{4,6},{5,7},{6,4},{7,5},{8,10},{9,11},{10,... | collective-permute-start | bytes 589832 | tf_op jit(solution)/shard_map/ppermute | solution.py:640
  190.0 3.4 %collective-permute-done.27 = bf16[144,512]{1,0:T(8,128)(2,1)S(1)} collective-permute-done((bf16[144,512]{1,0:T(8,128)(2,1)S(1)}, bf16[144,512]{1,0:T(8,128)(2,1)S(1)}, u32[]{:S(2)}, u32[]{:S(2)}) %collective-permute-start.27) | collective-permute-done | bytes 147488 | tf_op jit(solution)/shard_map/ppermute | solution.py:640
  194.1 0.8 collective-permute-start.30
  195.1 1.6 collective-permute-start.28
  196.7 7.4 %collective-permute-done.31 = bf16[320,512]{1,0:T(8,128)(2,1)S(1)} collective-permute-done((bf16[320,512]{1,0:T(8,128)(2,1)S(1)}, bf16[320,512]{1,0:T(8,128)(2,1)S(1)}, u32[]{:S(2)}, u32[]{:S(2)}) %collective-permute-start.31) | collective-permute-done | bytes 327712 | tf_op jit(solution)/shard_map/ppermute | solution.py:640
  204.1 0.7 collective-permute-start.34
  204.9 1.0 collective-permute-start.33
  206.9 1.2 collective-permute-start.29
  208.2 6.5 %collective-permute-done.34 = bf16[640,512]{1,0:T(8,128)(2,1)S(1)} collective-permute-done((bf16[640,512]{1,0:T(8,128)(2,1)S(1)}, bf16[640,512]{1,0:T(8,128)(2,1)S(1)}, u32[]{:S(2)}, u32[]{:S(2)}) %collective-permute-start.34) | collective-permute-done | bytes 655392 | tf_op jit(solution)/shard_map/ppermute | solution.py:640
  215.1 0.8 copy-done
  216.0 3.0 %collective-permute-done.29 = bf16[256,512]{1,0:T(8,128)(2,1)S(1)} collective-permute-done((bf16[256,512]{1,0:T(8,128)(2,1)S(1)}, bf16[256,512]{1,0:T(8,128)(2,1)S(1)}, u32[]{:S(2)}, u32[]{:S(2)}) %collective-permute-start.29) | collective-permute-done | bytes 262176 | tf_op jit(solution)/shard_map/ppermute | solution.py:640
  219.1 0.7 copy.29
  222.6 8.9 %shard_map.261 = (f32[256,512]{1,0:T(8,128)}, f32[1,512]{1,0:T(1,128)}, f32[1,512]{1,0:T(1,128)}, f32[4,64,512]{2,1,0:T(8,128)}, f32[2048,512]{1,0:T(8,128)}, /*...) custom-call(s32[4]{0:T(128)} %pad_add_fusion.1.place, bf16[256,512]{1,0:T(8,128)(2,1)} %embed.5, ...), custom_call_target="tpu_custom_call" | custom-call | flops 1 | tf_op jit(solution)/shard_map/pallas_call | solution.py:562
  (140 shorter events, 11.6 us)
Async XLA Ops:
  0.6 11.2 %copy-start.16 = (s32[4,512]{1,0:T(4,128)S(1)}, s32[4,512]{1,0:T(4,128)}, u32[]{:S(2)}) copy-start(s32[4,512]{1,0:T(4,128)} %param.16) | copy-start | bytes 24580
  1.5 10.2 %collective-permute-start = (s32[4,64]{1,0:T(4,128)S(1)}, s32[4,64]{1,0:T(4,128)S(1)}, u32[]{:S(2)}, u32[]{:S(2)}) collective-permute-start(s32[4,64]{1,0:T(4,128)S(1)} %get-tuple-element.173), channel_id=1, source_target_pairs={{0,1},{1,2},{2,3},{3,4},{4,5},{5,6},{6,7},{8,9},{9,10},{10,11},{11... | collective-permute-start | bytes 3080 | tf_op jit(solution)/shard_map/ppermute | solution.py:768
  6.3 5.5 %collective-permute-start.1 = (s32[4,64]{1,0:T(4,128)S(1)}, s32[4,64]{1,0:T(4,128)S(1)}, u32[]{:S(2)}, u32[]{:S(2)}) collective-permute-start(s32[4,64]{1,0:T(4,128)S(1)} %get-tuple-element.174), channel_id=1, source_target_pairs={{1,0},{2,1},{3,2},{4,3},{5,4},{6,5},{7,6},{9,8},{10,9},{11,10},{12... | collective-permute-start | bytes 3080 | tf_op jit(solution)/shard_map/ppermute | solution.py:770
  45.7 4.0 %collective-permute-start.2 = (f32[4]{0:T(128)S(1)}, f32[4]{0:T(128)S(1)}, u32[]{:S(2)}, u32[]{:S(2)}) collective-permute-start(f32[4]{0:T(128)S(1)} %slice_reduce_fusion), channel_id=1, source_target_pairs={{0,1},{1,0},{2,3},{3,2},{4,5},{5,4},{6,7},{7,6},{8,9},{9,8},{10,11... | collective-permute-start | bytes 56 | tf_op jit(solution)/shard_map/ppermute | solution.py:597
  49.7 4.5 %collective-permute-start.3 = (f32[4]{0:T(128)S(1)}, f32[4]{0:T(128)S(1)}, u32[]{:S(2)}, u32[]{:S(2)}) collective-permute-start(f32[4]{0:T(128)S(1)} %add.269), channel_id=1, source_target_pairs={{0,2},{1,3},{2,0},{3,1},{4,6},{5,7},{6,4},{7,5},{8,10},{9,11},{10,... | collective-permute-start | bytes 56 | tf_op jit(solution)/shard_map/ppermute | solution.py:597
  54.2 4.6 %collective-permute-start.4 = (f32[4]{0:T(128)S(1)}, f32[4]{0:T(128)S(1)}, u32[]{:S(2)}, u32[]{:S(2)}) collective-permute-start(f32[4]{0:T(128)S(1)} %add.271), channel_id=1, source_target_pairs={{0,4},{1,5},{2,6},{3,7},{4,0},{5,1},{6,2},{7,3},{8,12},{9,13},{10,... | collective-permute-start | bytes 56 | tf_op jit(solution)/shard_map/ppermute | solution.py:597
  61.6 5.6 %collective-permute-start.5 = (f32[4,8,64]{2,1,0:T(8,128)}, f32[4,8,64]{2,1,0:T(8,128)S(1)}, u32[]{:S(2)}, u32[]{:S(2)}) collective-permute-start(f32[4,8,64]{2,1,0:T(8,128)} %shard_map.257), channel_id=1, source_target_pairs={{0,1},{1,0},{2,3},{3,2},{4,5},{5,4},{6,7},{7,6},{8,9},{9,8},{10,11... | collective-permute-start | bytes 24584 | tf_op jit(solution)/shard_map/ppermute | solution.py:597
  62.5 4.6 %copy-start.15 = (f32[4,8,64]{2,1,0:T(8,128)S(1)}, f32[4,8,64]{2,1,0:T(8,128)}, u32[]{:S(2)}) copy-start(f32[4,8,64]{2,1,0:T(8,128)} %shard_map.257) | copy-start | bytes 24580
  67.1 3.8 %collective-permute-start.6 = (f32[4,8,64]{2,1,0:T(8,128)S(1)}, f32[4,8,64]{2,1,0:T(8,128)S(1)}, u32[]{:S(2)}, u32[]{:S(2)}) collective-permute-start(f32[4,8,64]{2,1,0:T(8,128)S(1)} %add.274), channel_id=1, source_target_pairs={{0,2},{1,3},{2,0},{3,1},{4,6},{5,7},{6,4},{7,5},{8,10},{9,11},{10,... | collective-permute-start | bytes 24584 | tf_op jit(solution)/shard_map/ppermute | solution.py:597
  70.9 4.6 %collective-permute-start.7 = (f32[4,8,64]{2,1,0:T(8,128)S(1)}, f32[4,8,64]{2,1,0:T(8,128)S(1)}, u32[]{:S(2)}, u32[]{:S(2)}) collective-permute-start(f32[4,8,64]{2,1,0:T(8,128)S(1)} %add.276), channel_id=1, source_target_pairs={{0,4},{1,5},{2,6},{3,7},{4,0},{5,1},{6,2},{7,3},{8,12},{9,13},{10,... | collective-permute-start | bytes 24584 | tf_op jit(solution)/shard_map/ppermute | solution.py:597
  111.2 6.4 %collective-permute-start.9 = (bf16[1280,512]{1,0:T(8,128)(2,1)}, bf16[1280,512]{1,0:T(8,128)(2,1)S(1)}, u32[]{:S(2)}, u32[]{:S(2)}) collective-permute-start(bf16[1280,512]{1,0:T(8,128)(2,1)} %get-tuple-element.94), channel_id=1, source_target_pairs={{0,8},{1,9},{2,10},{3,11},{4,12},{5,13},{6,14},{7,15},{8,0},{9,1},... | collective-permute-start | bytes 3932168 | tf_op jit(solution)/shard_map/ppermute | solution.py:640
  111.2 4.7 %collective-permute-start.8 = (bf16[1024,512]{1,0:T(8,128)(2,1)}, bf16[1024,512]{1,0:T(8,128)(2,1)S(1)}, u32[]{:S(2)}, u32[]{:S(2)}) collective-permute-start(bf16[1024,512]{1,0:T(8,128)(2,1)} %get-tuple-element.92), channel_id=1, source_target_pairs={{0,8},{1,9},{2,10},{3,11},{4,12},{5,13},{6,14},{7,15},{8,0},{9,1},... | collective-permute-start | bytes 3145736 | tf_op jit(solution)/shard_map/ppermute | solution.py:640
  111.7 8.5 %collective-permute-start.10 = (bf16[128,512]{1,0:T(8,128)(2,1)S(1)}, bf16[128,512]{1,0:T(8,128)(2,1)S(1)}, u32[]{:S(2)}, u32[]{:S(2)}) collective-permute-start(bf16[128,512]{1,0:T(8,128)(2,1)S(1)} %dynamic-slice_convert_fusion), channel_id=1, source_target_pairs={{0,1},{1,0},{2,3},{3,2},{4,5},{5,4},{6,7},{7,6},{8,9},{9,8},{10,11... | collective-permute-start | bytes 393224 | tf_op jit(solution)/shard_map/ppermute | solution.py:895
  116.0 2.6 %copy-start.4 = (bf16[1280,512]{1,0:T(8,128)(2,1)S(1)}, bf16[1280,512]{1,0:T(8,128)(2,1)}, u32[]{:S(2)}) copy-start(bf16[1280,512]{1,0:T(8,128)(2,1)} %get-tuple-element.93) | copy-start | bytes 3932164
  117.6 1.1 copy-start.6
  120.3 24.1 %copy-start.13 = (bf16[128,512]{1,0:T(8,128)(2,1)}, bf16[128,512]{1,0:T(8,128)(2,1)S(1)}, u32[]{:S(2)}) copy-start(bf16[128,512]{1,0:T(8,128)(2,1)S(1)} %collective-permute-done.10) | copy-start | bytes 393220
  120.3 23.3 %collective-permute-start.12 = (bf16[640,512]{1,0:T(8,128)(2,1)S(1)}, bf16[640,512]{1,0:T(8,128)(2,1)S(1)}, u32[]{:S(2)}, u32[]{:S(2)}) collective-permute-start(bf16[640,512]{1,0:T(8,128)(2,1)S(1)} %get-tuple-element.105), channel_id=1, source_target_pairs={{0,1},{1,0},{2,3},{3,2},{4,5},{5,4},{6,7},{7,6},{8,10},{9,11},{10,... | collective-permute-start | bytes 1966088 | tf_op jit(solution)/shard_map/ppermute | solution.py:640
  121.5 22.2 %collective-permute-start.11 = (bf16[512,512]{1,0:T(8,128)(2,1)S(1)}, bf16[512,512]{1,0:T(8,128)(2,1)S(1)}, u32[]{:S(2)}, u32[]{:S(2)}) collective-permute-start(bf16[512,512]{1,0:T(8,128)(2,1)S(1)} %get-tuple-element.104), channel_id=1, source_target_pairs={{0,16},{1,17},{2,18},{3,19},{4,20},{5,21},{6,22},{7,23},{8,9},{9,8... | collective-permute-start | bytes 1572872 | tf_op jit(solution)/shard_map/ppermute | solution.py:640
  123.0 21.5 %copy-start.3 = (f32[4,64,512]{2,1,0:T(8,128)S(1)}, f32[4,64,512]{2,1,0:T(8,128)}, u32[]{:S(2)}) copy-start(f32[4,64,512]{2,1,0:T(8,128)} %shard_map.258) | copy-start | bytes 1572868
  143.6 0.8 copy-start.11
  144.4 2.3 collective-permute-start.13
  144.4 3.3 %copy-start.9 = (bf16[512,512]{1,0:T(8,128)(2,1)S(1)}, bf16[512,512]{1,0:T(8,128)(2,1)}, u32[]{:S(2)}) copy-start(bf16[512,512]{1,0:T(8,128)(2,1)} %get-tuple-element.108) | copy-start | bytes 1572868
  147.9 2.2 copy-start.12
  148.2 2.8 %copy-start.14 = (f32[8,512]{1,0:T(8,128)S(1)}, f32[8,512]{1,0:T(8,128)}, u32[]{:S(2)}) copy-start(f32[8,512]{1,0:T(8,128)} %get-tuple-element.102.vectors) | copy-start | bytes 49156
  148.2 8.8 %collective-permute-start.15 = (bf16[320,512]{1,0:T(8,128)(2,1)S(1)}, bf16[320,512]{1,0:T(8,128)(2,1)S(1)}, u32[]{:S(2)}, u32[]{:S(2)}) collective-permute-start(bf16[320,512]{1,0:T(8,128)(2,1)S(1)} %get-tuple-element.150), channel_id=1, source_target_pairs={{0,2},{1,3},{2,0},{3,1},{4,6},{5,7},{6,4},{7,5},{8,9},{9,8},{10,11... | collective-permute-start | bytes 983048 | tf_op jit(solution)/shard_map/ppermute | solution.py:640
  150.3 7.0 %collective-permute-start.14 = (bf16[256,512]{1,0:T(8,128)(2,1)S(1)}, bf16[256,512]{1,0:T(8,128)(2,1)S(1)}, u32[]{:S(2)}, u32[]{:S(2)}) collective-permute-start(bf16[256,512]{1,0:T(8,128)(2,1)S(1)} %get-tuple-element.151), channel_id=1, source_target_pairs={{0,1},{1,0},{2,3},{3,2},{4,5},{5,4},{6,7},{7,6},{8,24},{9,25},{10,... | collective-permute-start | bytes 786440 | tf_op jit(solution)/shard_map/ppermute | solution.py:640
  151.8 8.5 %collective-permute-start.24 = (bf16[272,512]{1,0:T(8,128)(2,1)S(1)}, bf16[272,512]{1,0:T(8,128)(2,1)S(1)}, u32[]{:S(2)}, u32[]{:S(2)}) collective-permute-start(bf16[272,512]{1,0:T(8,128)(2,1)S(1)} %pad_maximum_fusion), channel_id=1, source_target_pairs={{0,1},{1,0},{2,3},{3,2},{4,5},{5,4},{6,7},{7,6},{8,10},{9,11},{10,... | collective-permute-start | bytes 835592 | tf_op jit(solution)/shard_map/ppermute | solution.py:640
  160.3 5.4 %collective-permute-start.17 = (bf16[160,512]{1,0:T(8,128)(2,1)S(1)}, bf16[160,512]{1,0:T(8,128)(2,1)S(1)}, u32[]{:S(2)}, u32[]{:S(2)}) collective-permute-start(bf16[160,512]{1,0:T(8,128)(2,1)S(1)} %get-tuple-element.156), channel_id=1, source_target_pairs={{0,16},{1,17},{2,18},{3,19},{4,20},{5,21},{6,22},{7,23},{8,24},{9,... | collective-permute-start | bytes 491528 | tf_op jit(solution)/shard_map/ppermute | solution.py:640
  161.8 7.0 %collective-permute-start.16 = (bf16[192,512]{1,0:T(8,128)(2,1)S(1)}, bf16[192,512]{1,0:T(8,128)(2,1)S(1)}, u32[]{:S(2)}, u32[]{:S(2)}) collective-permute-start(bf16[192,512]{1,0:T(8,128)(2,1)S(1)} %pad_maximum_fusion.1), channel_id=1, source_target_pairs={{0,2},{1,3},{2,0},{3,1},{4,6},{5,7},{6,4},{7,5},{8,10},{9,11},{10,... | collective-permute-start | bytes 589832 | tf_op jit(solution)/shard_map/ppermute | solution.py:640
  163.0 7.0 %collective-permute-start.25 = (bf16[144,512]{1,0:T(8,128)(2,1)S(1)}, bf16[144,512]{1,0:T(8,128)(2,1)S(1)}, u32[]{:S(2)}, u32[]{:S(2)}) collective-permute-start(bf16[144,512]{1,0:T(8,128)(2,1)S(1)} %pad_maximum_fusion.3), channel_id=1, source_target_pairs={{0,2},{1,3},{2,0},{3,1},{4,6},{5,7},{6,4},{7,5},{8,9},{9,8},{10,11... | collective-permute-start | bytes 442376 | tf_op jit(solution)/shard_map/ppermute | solution.py:640
  165.7 8.5 %collective-permute-start.19 = (bf16[80,512]{1,0:T(8,128)(2,1)S(1)}, bf16[80,512]{1,0:T(8,128)(2,1)S(1)}, u32[]{:S(2)}, u32[]{:S(2)}) collective-permute-start(bf16[80,512]{1,0:T(8,128)(2,1)S(1)} %add_convert_fusion.12), channel_id=1, source_target_pairs={{0,4},{1,5},{2,6},{3,7},{4,0},{5,1},{6,2},{7,3},{8,12},{9,13},{10,... | collective-permute-start | bytes 245768 | tf_op jit(solution)/shard_map/ppermute | solution.py:640
  170.1 15.4 %collective-permute-start.26 = (bf16[144,512]{1,0:T(8,128)(2,1)S(1)}, bf16[144,512]{1,0:T(8,128)(2,1)S(1)}, u32[]{:S(2)}, u32[]{:S(2)}) collective-permute-start(bf16[144,512]{1,0:T(8,128)(2,1)S(1)} %pad_maximum_fusion.4), channel_id=1, source_target_pairs={{0,16},{1,17},{2,18},{3,19},{4,20},{5,21},{6,22},{7,23},{8,24},{9,... | collective-permute-start | bytes 442376 | tf_op jit(solution)/shard_map/ppermute | solution.py:640
  170.8 6.3 %collective-permute-start.18 = (bf16[96,512]{1,0:T(8,128)(2,1)S(1)}, bf16[96,512]{1,0:T(8,128)(2,1)S(1)}, u32[]{:S(2)}, u32[]{:S(2)}) collective-permute-start(bf16[96,512]{1,0:T(8,128)(2,1)S(1)} %pad_maximum_fusion.6), channel_id=1, source_target_pairs={{0,4},{1,5},{2,6},{3,7},{4,0},{5,1},{6,2},{7,3},{8,12},{9,13},{10,... | collective-permute-start | bytes 294920 | tf_op jit(solution)/shard_map/ppermute | solution.py:640
  174.3 9.8 %collective-permute-start.21 = (bf16[80,512]{1,0:T(8,128)(2,1)S(1)}, bf16[80,512]{1,0:T(8,128)(2,1)S(1)}, u32[]{:S(2)}, u32[]{:S(2)}) collective-permute-start(bf16[80,512]{1,0:T(8,128)(2,1)S(1)} %get-tuple-element.142), channel_id=1, source_target_pairs={{0,4},{1,5},{2,6},{3,7},{4,0},{5,1},{6,2},{7,3},{8,12},{9,13},{10,... | collective-permute-start | bytes 245768 | tf_op jit(solution)/shard_map/ppermute | solution.py:640
  177.2 8.8 %collective-permute-start.20 = (bf16[96,512]{1,0:T(8,128)(2,1)S(1)}, bf16[96,512]{1,0:T(8,128)(2,1)S(1)}, u32[]{:S(2)}, u32[]{:S(2)}) collective-permute-start(bf16[96,512]{1,0:T(8,128)(2,1)S(1)} %pad_maximum_fusion.7), channel_id=1, source_target_pairs={{0,4},{1,5},{2,6},{3,7},{4,0},{5,1},{6,2},{7,3},{8,12},{9,13},{10,... | collective-permute-start | bytes 294920 | tf_op jit(solution)/shard_map/ppermute | solution.py:640
  184.1 9.3 %collective-permute-start.23 = (bf16[160,512]{1,0:T(8,128)(2,1)S(1)}, bf16[160,512]{1,0:T(8,128)(2,1)S(1)}, u32[]{:S(2)}, u32[]{:S(2)}) collective-permute-start(bf16[160,512]{1,0:T(8,128)(2,1)S(1)} %constant_dynamic-update-slice_fusion.9), channel_id=1, source_target_pairs={{0,16},{1,17},{2,18},{3,19},{4,20},{5,21},{6,22},{7,23},{8,24},{9,... | collective-permute-start | bytes 491528 | tf_op jit(solution)/shard_map/ppermute | solution.py:640
  185.6 7.8 %collective-permute-start.27 = (bf16[144,512]{1,0:T(8,128)(2,1)S(1)}, bf16[144,512]{1,0:T(8,128)(2,1)S(1)}, u32[]{:S(2)}, u32[]{:S(2)}) collective-permute-start(bf16[144,512]{1,0:T(8,128)(2,1)S(1)} %pad_maximum_fusion.5), channel_id=1, source_target_pairs={{0,4},{1,5},{2,6},{3,7},{4,0},{5,1},{6,2},{7,3},{8,12},{9,13},{10,... | collective-permute-start | bytes 442376 | tf_op jit(solution)/shard_map/ppermute | solution.py:640
  186.1 8.0 %collective-permute-start.22 = (bf16[192,512]{1,0:T(8,128)(2,1)S(1)}, bf16[192,512]{1,0:T(8,128)(2,1)S(1)}, u32[]{:S(2)}, u32[]{:S(2)}) collective-permute-start(bf16[192,512]{1,0:T(8,128)(2,1)S(1)} %pad_maximum_fusion.2), channel_id=1, source_target_pairs={{0,2},{1,3},{2,0},{3,1},{4,6},{5,7},{6,4},{7,5},{8,10},{9,11},{10,... | collective-permute-start | bytes 589832 | tf_op jit(solution)/shard_map/ppermute | solution.py:640
  193.4 10.7 %collective-permute-start.31 = (bf16[320,512]{1,0:T(8,128)(2,1)S(1)}, bf16[320,512]{1,0:T(8,128)(2,1)S(1)}, u32[]{:S(2)}, u32[]{:S(2)}) collective-permute-start(bf16[320,512]{1,0:T(8,128)(2,1)S(1)} %constant_dynamic-update-slice_fusion.5), channel_id=1, source_target_pairs={{0,2},{1,3},{2,0},{3,1},{4,6},{5,7},{6,4},{7,5},{8,9},{9,8},{10,11... | collective-permute-start | bytes 983048 | tf_op jit(solution)/shard_map/ppermute | solution.py:640
  194.1 10.7 %collective-permute-start.30 = (bf16[256,512]{1,0:T(8,128)(2,1)S(1)}, bf16[256,512]{1,0:T(8,128)(2,1)S(1)}, u32[]{:S(2)}, u32[]{:S(2)}) collective-permute-start(bf16[256,512]{1,0:T(8,128)(2,1)S(1)} %slice_dynamic-update-slice_fusion), channel_id=1, source_target_pairs={{0,1},{1,0},{2,3},{3,2},{4,5},{5,4},{6,7},{7,6},{8,24},{9,25},{10,... | collective-permute-start | bytes 786440 | tf_op jit(solution)/shard_map/ppermute | solution.py:640
  195.1 11.8 %collective-permute-start.28 = (bf16[128,512]{1,0:T(8,128)(2,1)S(1)}, bf16[128,512]{1,0:T(8,128)(2,1)S(1)}, u32[]{:S(2)}, u32[]{:S(2)}) collective-permute-start(bf16[128,512]{1,0:T(8,128)(2,1)S(1)} %get-tuple-element.138), channel_id=1, source_target_pairs={{0,2},{1,3},{2,0},{3,1},{4,6},{5,7},{6,4},{7,5},{8,9},{9,8},{10,11... | collective-permute-start | bytes 393224 | tf_op jit(solution)/shard_map/ppermute | solution.py:640
  204.1 10.7 %collective-permute-start.34 = (bf16[640,512]{1,0:T(8,128)(2,1)S(1)}, bf16[640,512]{1,0:T(8,128)(2,1)S(1)}, u32[]{:S(2)}, u32[]{:S(2)}) collective-permute-start(bf16[640,512]{1,0:T(8,128)(2,1)S(1)} %constant_dynamic-update-slice_fusion.17), channel_id=1, source_target_pairs={{0,1},{1,0},{2,3},{3,2},{4,5},{5,4},{6,7},{7,6},{8,10},{9,11},{10,... | collective-permute-start | bytes 1966088 | tf_op jit(solution)/shard_map/ppermute | solution.py:640
  204.9 10.1 %collective-permute-start.33 = (bf16[512,512]{1,0:T(8,128)(2,1)S(1)}, bf16[512,512]{1,0:T(8,128)(2,1)S(1)}, u32[]{:S(2)}, u32[]{:S(2)}) collective-permute-start(bf16[512,512]{1,0:T(8,128)(2,1)S(1)} %constant_dynamic-update-slice_fusion.14), channel_id=1, source_target_pairs={{0,16},{1,17},{2,18},{3,19},{4,20},{5,21},{6,22},{7,23},{8,9},{9,8... | collective-permute-start | bytes 1572872 | tf_op jit(solution)/shard_map/ppermute | solution.py:640
  205.9 13.1 %collective-permute-start.32 = (bf16[128,512]{1,0:T(8,128)(2,1)S(1)}, bf16[128,512]{1,0:T(8,128)(2,1)S(1)}, u32[]{:S(2)}, u32[]{:S(2)}) collective-permute-start(bf16[128,512]{1,0:T(8,128)(2,1)S(1)} %slice_dynamic-update-slice_fusion.1), channel_id=1, source_target_pairs={{0,1},{1,0},{2,3},{3,2},{4,5},{5,4},{6,7},{7,6},{8,9},{9,8},{10,11... | collective-permute-start | bytes 393224 | tf_op jit(solution)/shard_map/ppermute | solution.py:982
  206.9 12.1 %collective-permute-start.29 = (bf16[256,512]{1,0:T(8,128)(2,1)S(1)}, bf16[256,512]{1,0:T(8,128)(2,1)S(1)}, u32[]{:S(2)}, u32[]{:S(2)}) collective-permute-start(bf16[256,512]{1,0:T(8,128)(2,1)S(1)} %constant_dynamic-update-slice_fusion.11), channel_id=1, source_target_pairs={{0,1},{1,0},{2,3},{3,2},{4,5},{5,4},{6,7},{7,6},{8,10},{9,11},{10,... | collective-permute-start | bytes 786440 | tf_op jit(solution)/shard_map/ppermute | solution.py:640
  214.8 1.1 copy-start
  214.8 6.2 %collective-permute-start.36 = (bf16[1280,512]{1,0:T(8,128)(2,1)S(1)}, bf16[1280,512]{1,0:T(8,128)(2,1)S(1)}, u32[]{:S(2)}, u32[]{:S(2)}) collective-permute-start(bf16[1280,512]{1,0:T(8,128)(2,1)S(1)} %constant_dynamic-update-slice_fusion.16.refs_2_), channel_id=1, source_target_pairs={{0,8},{1,9},{2,10},{3,11},{4,12},{5,13},{6,14},{7,15},{8,0},{9,1},... | collective-permute-start | bytes 3932168 | tf_op jit(solution)/shard_map/ppermute | solution.py:640
  215.9 5.1 %copy-start.1 = (bf16[1024,512]{1,0:T(8,128)(2,1)}, bf16[1024,512]{1,0:T(8,128)(2,1)S(1)}, u32[]{:S(2)}) copy-start(bf16[1024,512]{1,0:T(8,128)(2,1)S(1)} %constant_dynamic-update-slice_fusion.21.refs_0_) | copy-start | bytes 3145732
  215.9 5.1 %collective-permute-start.35 = (bf16[1024,512]{1,0:T(8,128)(2,1)S(1)}, bf16[1024,512]{1,0:T(8,128)(2,1)S(1)}, u32[]{:S(2)}, u32[]{:S(2)}) collective-permute-start(bf16[1024,512]{1,0:T(8,128)(2,1)S(1)} %constant_dynamic-update-slice_fusion.21.refs_0_), channel_id=1, source_target_pairs={{0,8},{1,9},{2,10},{3,11},{4,12},{5,13},{6,14},{7,15},{8,0},{9,1},... | collective-permute-start | bytes 3145736 | tf_op jit(solution)/shard_map/ppermute | solution.py:640
  219.0 2.0 copy-start.2
  219.0 2.0 collective-permute-start.37
  220.5 0.7 copy-start.8
  221.0 0.8 copy-start.10
  221.0 1.2 copy-start.7
  221.0 1.6 copy-start.5

commit v5 on v4

--- a/solution.py
+++ b/solution.py
@@ -264,14 +264,12 @@
         stats_out[item] = stats.T[:8]
 
 
-def numer_kernel(place, lengths, counts, before, total, running, high, low, numer_out):
+def numer_kernel(place, lengths, counts, before, total, running, high, numer_out):
     _, assign, _, _, _ = assignment(
         place, lengths, counts, before, total, running, pl.program_id(0)
     )
     assign_high, assign_low = split_two(assign)
-    numer_out[0] = (
-        dot(assign_high, high[0]) + dot(assign_low, high[0]) + dot(assign_high, low[0])
-    )
+    numer_out[0] = dot(assign_high, high[0]) + dot(assign_low, high[0])
 
 
 def hidden_gradient(
@@ -871,11 +869,11 @@
     (numer,) = call(
         numer_kernel,
         items,
-        numbers_specs + [per_item(square), per_item(square)],
+        numbers_specs + [per_item(square)],
         [item_out(items, (NB, model_width), F32)],
         [],
         6 * tokens * NB * model_width,
-        numbers + (hidden_high, hidden_low),
+        numbers + (hidden_high,),
     )
     _, stats_whole, stats_after, numer = scan_over("seq", stats, seq_place, numer)
 

time: 232 us -> 232 us (level)
  no operation moved by 1% of the time
where the time goes in v5:
time: 232 us; the launch traced here: 231 us
  Pallas kernels  107 us (46%)
  starting transfers between devices  53.8 us (23%)
  waiting for transfers between devices  50 us (22%)
  local copies, waits for them, and re-layouts  11.4 us (5%)
  other arithmetic  7.91 us (3%)
    pallas_call x7, Pallas kernels, call(): pl.pallas_call(kernel, grid=(items,), in_specs=in_specs, out_specs=[spec...  107 us
    ppermute x28, waiting for transfers between devices, swap(): return lax.ppermute(cells, ('dp', 'seq'), pairs)  42.7 us
    ppermute x28, starting transfers between devices, swap(): return lax.ppermute(cells, ('dp', 'seq'), pairs)  32.2 us
    ppermute x6, starting transfers between devices, scan_over(): other = lax.ppermute(cells, axis, [(at, at ^ bit) for at in range(count)])  13.8 us
    ppermute x6, waiting for transfers between devices, scan_over(): other = lax.ppermute(cells, axis, [(at, at ^ bit) for at in range(count)])  7.13 us
    unnamed x36, local copies, waits for them, and re-layouts  4.95 us
    ppermute x1, starting transfers between devices, local(): lax.ppermute(byte_ids[:, span - WIN:], 'seq', [(at, at + 1) for at in ends])  4.86 us
  transfers between devices with their start and end apart: 38, of which 23 were waited for; matrix products, arithmetic and copies ran while one was open for 4% of the time, Pallas kernels for 12%

profile of v5, /device:TPU:0, one launch (start us, length us, event | category | flops | bytes accessed | tf_op | source)
XLA Modules:
  0.0 231.2 jit_solution(15716191911710664577)
XLA Ops:
  0.7 0.8 fusion.8
  1.5 4.9 %collective-permute-start = (s32[4,64]{1,0:T(4,128)S(1)}, s32[4,64]{1,0:T(4,128)S(1)}, u32[]{:S(2)}, u32[]{:S(2)}) collective-permute-start(s32[4,64]{1,0:T(4,128)S(1)} %get-tuple-element.173), channel_id=1, source_target_pairs={{0,1},{1,2},{2,3},{3,4},{4,5},{5,6},{6,7},{8,9},{9,10},{10,11},{11... | collective-permute-start | bytes 3080 | tf_op jit(solution)/shard_map/ppermute | solution.py:766
  6.3 1.3 collective-permute-start.1
  8.3 3.4 %shard_map.255 = (bf16[256,512]{1,0:T(8,128)(2,1)}, bf16[256,1536]{1,0:T(8,128)(2,1)}, bf16[512,256]{1,0:T(8,128)(2,1)}, bf16[512,256]{1,0:T(8,128)(2,1)}) custom-call(bf16[256,512]{1,0:T(8,128)(2,1)} %embed.5, f32[1,512]{1,0:T(1,128)} %bitcast.28, f32[1,512]{1,0:T(1,128)} %bitcast.33, bf16[512,1536]{1,0:T(8,128)(2,1)} %weight.3), custom_call_target="tpu_custom_call" | custom-call | flops 1 | tf_op jit(solution)/shard_map/pallas_call | solution.py:560
  12.5 32.3 %shard_map.256 = (bf16[4,512,512]{2,1,0:T(8,128)(2,1)}, f32[4,16,256]{2,1,0:T(8,128)}, f32[4,512,512]{2,1,0:T(8,128)}, bf16[4,512,512]{2,1,0:T(8,128)(2,1)}, bf1...) custom-call(s32[4]{0:T(128)} %pad_add_fusion.1.place, ...), custom_call_target="tpu_custom_call" | custom-call | flops 1 | tf_op jit(solution)/shard_map/pallas_call | solution.py:560
  44.8 0.8 slice_reduce_fusion
  45.7 2.5 %collective-permute-start.2 = (f32[4]{0:T(128)S(1)}, f32[4]{0:T(128)S(1)}, u32[]{:S(2)}, u32[]{:S(2)}) collective-permute-start(f32[4]{0:T(128)S(1)} %slice_reduce_fusion), channel_id=1, source_target_pairs={{0,1},{1,0},{2,3},{3,2},{4,5},{5,4},{6,7},{7,6},{8,9},{9,8},{10,11... | collective-permute-start | bytes 56 | tf_op jit(solution)/shard_map/ppermute | solution.py:595
  48.2 1.5 collective-permute-done.2
  49.7 3.0 %collective-permute-start.3 = (f32[4]{0:T(128)S(1)}, f32[4]{0:T(128)S(1)}, u32[]{:S(2)}, u32[]{:S(2)}) collective-permute-start(f32[4]{0:T(128)S(1)} %add.269), channel_id=1, source_target_pairs={{0,2},{1,3},{2,0},{3,1},{4,6},{5,7},{6,4},{7,5},{8,10},{9,11},{10,... | collective-permute-start | bytes 56 | tf_op jit(solution)/shard_map/ppermute | solution.py:595
  52.7 1.5 collective-permute-done.3
  54.2 3.0 %collective-permute-start.4 = (f32[4]{0:T(128)S(1)}, f32[4]{0:T(128)S(1)}, u32[]{:S(2)}, u32[]{:S(2)}) collective-permute-start(f32[4]{0:T(128)S(1)} %add.271), channel_id=1, source_target_pairs={{0,4},{1,5},{2,6},{3,7},{4,0},{5,1},{6,2},{7,3},{8,12},{9,13},{10,... | collective-permute-start | bytes 56 | tf_op jit(solution)/shard_map/ppermute | solution.py:595
  57.3 1.5 collective-permute-done.4
  59.3 2.2 shard_map.257
  61.6 0.9 collective-permute-start.5
  62.5 4.1 %shard_map.258 = f32[4,64,512]{2,1,0:T(8,128)} custom-call(s32[4]{0:T(128)} %pad_add_fusion.1.place, s32[4]{0:T(128)} %lengths.7, s32[4]{0:T(128)} %counts.5, f32[4]{0:T(128)} %get-tuple-element.176.before, f32[4]{0:T(128)} %get-tuple-element.175.total, f32[4,1,512]{2,1,0:T(1,128)} %get-tuple-element.78.running, bf16[4,512,512]{2,1,0:T(8,128)(2,1)} %get-tuple-element.80.high), custom_call_target="tpu_custom_call" | custom-call | flops 1 | tf_op jit(solution)/shard_map/pallas_call | solution.py:560
  66.6 1.7 collective-permute-start.6
  68.9 1.5 collective-permute-done.6
  70.4 2.6 %collective-permute-start.7 = (f32[4,8,64]{2,1,0:T(8,128)S(1)}, f32[4,8,64]{2,1,0:T(8,128)S(1)}, u32[]{:S(2)}, u32[]{:S(2)}) collective-permute-start(f32[4,8,64]{2,1,0:T(8,128)S(1)} %add.276), channel_id=1, source_target_pairs={{0,4},{1,5},{2,6},{3,7},{4,0},{5,1},{6,2},{7,3},{8,12},{9,13},{10,... | collective-permute-start | bytes 24584 | tf_op jit(solution)/shard_map/ppermute | solution.py:595
  73.0 1.0 dynamic-slice_convert_fusion
  74.0 1.0 collective-permute-done.7
  75.7 35.0 %shard_map.259 = (bf16[1024,512]{1,0:T(8,128)(2,1)}, bf16[1024,512]{1,0:T(8,128)(2,1)}, bf16[1280,512]{1,0:T(8,128)(2,1)}, bf16[1280,512]{1,0:T(8,128)(2,1)}, bf...) custom-call(s32[4]{0:T(128)} %pad_add_fusion.1.place, s32[4]{0:T(128)} %lengths.7, s32[4]{0:T(128)} %counts.5, ...), custom_call_target="tpu_custom_call" | custom-call | flops 1 | tf_op jit(solution)/shard_map/pallas_call | solution.py:560
  111.2 1.1 collective-permute-start.10
  112.3 3.1 %collective-permute-done.8 = bf16[1024,512]{1,0:T(8,128)(2,1)S(1)} collective-permute-done((bf16[1024,512]{1,0:T(8,128)(2,1)}, bf16[1024,512]{1,0:T(8,128)(2,1)S(1)}, u32[]{:S(2)}, u32[]{:S(2)}) %collective-permute-start.8) | collective-permute-done | bytes 1048608 | tf_op jit(solution)/shard_map/ppermute | solution.py:638
  115.5 1.6 convert_add_fusion.1
  117.0 1.0 copy-done.6
  118.1 1.6 convert_add_fusion
  119.8 1.2 collective-permute-start.12
  120.9 1.5 collective-permute-start.11
  122.4 20.7 %shard_map.260 = (bf16[528,512]{1,0:T(8,128)(2,1)}, bf16[512,512]{1,0:T(8,128)(2,1)}) custom-call(s32[4]{0:T(128)} %pad_add_fusion.1.place, s32[4,1,640]{2,1,0:T(1,128)} %broadcast_in_dim.63.ids_row, bf16[256,1536]{1,0:T(8,128)(2,1)} %get-tuple-element.76.table, bf16[512,256]{1,0:T(8,128)(2,1)} %get-tuple-element.98.key_table, ...), custom_call_target="tpu_custom_call" | custom-call | flops 1 | tf_op jit(solution)/shard_map/pallas_call | solution.py:560
  143.1 0.8 copy-done.11
  143.9 1.0 convert_add_fusion.7
  144.9 1.3 collective-permute-done.13
  146.2 1.1 slice.124
  147.6 2.0 collective-permute-start.15
  149.8 0.7 collective-permute-start.14
  150.5 0.7 reduce-precision_convert_fusion.3
  151.2 1.5 collective-permute-start.24
  152.7 3.8 %collective-permute-done.15 = bf16[320,512]{1,0:T(8,128)(2,1)S(1)} collective-permute-done((bf16[320,512]{1,0:T(8,128)(2,1)S(1)}, bf16[320,512]{1,0:T(8,128)(2,1)S(1)}, u32[]{:S(2)}, u32[]{:S(2)}) %collective-permute-start.15) | collective-permute-done | bytes 327712 | tf_op jit(solution)/shard_map/ppermute | solution.py:638
  156.8 2.9 %collective-permute-done.24 = bf16[272,512]{1,0:T(8,128)(2,1)S(1)} collective-permute-done((bf16[272,512]{1,0:T(8,128)(2,1)S(1)}, bf16[272,512]{1,0:T(8,128)(2,1)S(1)}, u32[]{:S(2)}, u32[]{:S(2)}) %collective-permute-start.24) | collective-permute-done | bytes 278560 | tf_op jit(solution)/shard_map/ppermute | solution.py:638
  159.8 1.4 collective-permute-start.17
  161.2 1.2 collective-permute-start.16
  162.5 1.0 collective-permute-start.25
  163.4 1.7 collective-permute-done.17
  165.2 3.0 %collective-permute-start.19 = (bf16[80,512]{1,0:T(8,128)(2,1)S(1)}, bf16[80,512]{1,0:T(8,128)(2,1)S(1)}, u32[]{:S(2)}, u32[]{:S(2)}) collective-permute-start(bf16[80,512]{1,0:T(8,128)(2,1)S(1)} %add_convert_fusion.12), channel_id=1, source_target_pairs={{0,4},{1,5},{2,6},{3,7},{4,0},{5,1},{6,2},{7,3},{8,12},{9,13},{10,... | collective-permute-start | bytes 245768 | tf_op jit(solution)/shard_map/ppermute | solution.py:638
  168.2 1.2 collective-permute-done.25
  169.5 0.7 collective-permute-start.26
  170.3 3.4 %collective-permute-start.18 = (bf16[96,512]{1,0:T(8,128)(2,1)S(1)}, bf16[96,512]{1,0:T(8,128)(2,1)S(1)}, u32[]{:S(2)}, u32[]{:S(2)}) collective-permute-start(bf16[96,512]{1,0:T(8,128)(2,1)S(1)} %pad_maximum_fusion.6), channel_id=1, source_target_pairs={{0,4},{1,5},{2,6},{3,7},{4,0},{5,1},{6,2},{7,3},{8,12},{9,13},{10,... | collective-permute-start | bytes 294920 | tf_op jit(solution)/shard_map/ppermute | solution.py:638
  174.2 2.4 %collective-permute-done.18 = bf16[96,512]{1,0:T(8,128)(2,1)S(1)} collective-permute-done((bf16[96,512]{1,0:T(8,128)(2,1)S(1)}, bf16[96,512]{1,0:T(8,128)(2,1)S(1)}, u32[]{:S(2)}, u32[]{:S(2)}) %collective-permute-start.18) | collective-permute-done | bytes 98336 | tf_op jit(solution)/shard_map/ppermute | solution.py:638
  176.7 3.0 %collective-permute-start.20 = (bf16[96,512]{1,0:T(8,128)(2,1)S(1)}, bf16[96,512]{1,0:T(8,128)(2,1)S(1)}, u32[]{:S(2)}, u32[]{:S(2)}) collective-permute-start(bf16[96,512]{1,0:T(8,128)(2,1)S(1)} %pad_maximum_fusion.7), channel_id=1, source_target_pairs={{0,4},{1,5},{2,6},{3,7},{4,0},{5,1},{6,2},{7,3},{8,12},{9,13},{10,... | collective-permute-start | bytes 294920 | tf_op jit(solution)/shard_map/ppermute | solution.py:638
  179.7 3.9 %collective-permute-done.21 = bf16[80,512]{1,0:T(8,128)(2,1)S(1)} collective-permute-done((bf16[80,512]{1,0:T(8,128)(2,1)S(1)}, bf16[80,512]{1,0:T(8,128)(2,1)S(1)}, u32[]{:S(2)}, u32[]{:S(2)}) %collective-permute-start.21) | collective-permute-done | bytes 81952 | tf_op jit(solution)/shard_map/ppermute | solution.py:638
  183.6 1.3 collective-permute-start.23
  185.6 3.8 %collective-permute-start.22 = (bf16[192,512]{1,0:T(8,128)(2,1)S(1)}, bf16[192,512]{1,0:T(8,128)(2,1)S(1)}, u32[]{:S(2)}, u32[]{:S(2)}) collective-permute-start(bf16[192,512]{1,0:T(8,128)(2,1)S(1)} %pad_maximum_fusion.2), channel_id=1, source_target_pairs={{0,2},{1,3},{2,0},{3,1},{4,6},{5,7},{6,4},{7,5},{8,10},{9,11},{10,... | collective-permute-start | bytes 589832 | tf_op jit(solution)/shard_map/ppermute | solution.py:638
  189.5 3.4 %collective-permute-done.27 = bf16[144,512]{1,0:T(8,128)(2,1)S(1)} collective-permute-done((bf16[144,512]{1,0:T(8,128)(2,1)S(1)}, bf16[144,512]{1,0:T(8,128)(2,1)S(1)}, u32[]{:S(2)}, u32[]{:S(2)}) %collective-permute-start.27) | collective-permute-done | bytes 147488 | tf_op jit(solution)/shard_map/ppermute | solution.py:638
  193.6 0.9 collective-permute-start.30
  194.6 1.6 collective-permute-start.28
  196.2 7.4 %collective-permute-done.31 = bf16[320,512]{1,0:T(8,128)(2,1)S(1)} collective-permute-done((bf16[320,512]{1,0:T(8,128)(2,1)S(1)}, bf16[320,512]{1,0:T(8,128)(2,1)S(1)}, u32[]{:S(2)}, u32[]{:S(2)}) %collective-permute-start.31) | collective-permute-done | bytes 327712 | tf_op jit(solution)/shard_map/ppermute | solution.py:638
  203.6 0.7 collective-permute-start.34
  204.4 1.0 collective-permute-start.33
  206.4 1.2 collective-permute-start.29
  207.7 6.5 %collective-permute-done.34 = bf16[640,512]{1,0:T(8,128)(2,1)S(1)} collective-permute-done((bf16[640,512]{1,0:T(8,128)(2,1)S(1)}, bf16[640,512]{1,0:T(8,128)(2,1)S(1)}, u32[]{:S(2)}, u32[]{:S(2)}) %collective-permute-start.34) | collective-permute-done | bytes 655392 | tf_op jit(solution)/shard_map/ppermute | solution.py:638
  214.6 0.8 copy-done
  215.5 3.0 %collective-permute-done.29 = bf16[256,512]{1,0:T(8,128)(2,1)S(1)} collective-permute-done((bf16[256,512]{1,0:T(8,128)(2,1)S(1)}, bf16[256,512]{1,0:T(8,128)(2,1)S(1)}, u32[]{:S(2)}, u32[]{:S(2)}) %collective-permute-start.29) | collective-permute-done | bytes 262176 | tf_op jit(solution)/shard_map/ppermute | solution.py:638
  218.6 0.7 copy.29
  222.1 8.9 %shard_map.261 = (f32[256,512]{1,0:T(8,128)}, f32[1,512]{1,0:T(1,128)}, f32[1,512]{1,0:T(1,128)}, f32[4,64,512]{2,1,0:T(8,128)}, f32[2048,512]{1,0:T(8,128)}, /*...) custom-call(s32[4]{0:T(128)} %pad_add_fusion.1.place, bf16[256,512]{1,0:T(8,128)(2,1)} %embed.5, ...), custom_call_target="tpu_custom_call" | custom-call | flops 1 | tf_op jit(solution)/shard_map/pallas_call | solution.py:560
  (140 shorter events, 11.6 us)
Async XLA Ops:
  0.6 11.2 %copy-start.16 = (s32[4,512]{1,0:T(4,128)S(1)}, s32[4,512]{1,0:T(4,128)}, u32[]{:S(2)}) copy-start(s32[4,512]{1,0:T(4,128)} %param.16) | copy-start | bytes 24580
  1.5 10.2 %collective-permute-start = (s32[4,64]{1,0:T(4,128)S(1)}, s32[4,64]{1,0:T(4,128)S(1)}, u32[]{:S(2)}, u32[]{:S(2)}) collective-permute-start(s32[4,64]{1,0:T(4,128)S(1)} %get-tuple-element.173), channel_id=1, source_target_pairs={{0,1},{1,2},{2,3},{3,4},{4,5},{5,6},{6,7},{8,9},{9,10},{10,11},{11... | collective-permute-start | bytes 3080 | tf_op jit(solution)/shard_map/ppermute | solution.py:766
  6.3 5.5 %collective-permute-start.1 = (s32[4,64]{1,0:T(4,128)S(1)}, s32[4,64]{1,0:T(4,128)S(1)}, u32[]{:S(2)}, u32[]{:S(2)}) collective-permute-start(s32[4,64]{1,0:T(4,128)S(1)} %get-tuple-element.174), channel_id=1, source_target_pairs={{1,0},{2,1},{3,2},{4,3},{5,4},{6,5},{7,6},{9,8},{10,9},{11,10},{12... | collective-permute-start | bytes 3080 | tf_op jit(solution)/shard_map/ppermute | solution.py:768
  45.7 4.0 %collective-permute-start.2 = (f32[4]{0:T(128)S(1)}, f32[4]{0:T(128)S(1)}, u32[]{:S(2)}, u32[]{:S(2)}) collective-permute-start(f32[4]{0:T(128)S(1)} %slice_reduce_fusion), channel_id=1, source_target_pairs={{0,1},{1,0},{2,3},{3,2},{4,5},{5,4},{6,7},{7,6},{8,9},{9,8},{10,11... | collective-permute-start | bytes 56 | tf_op jit(solution)/shard_map/ppermute | solution.py:595
  49.7 4.5 %collective-permute-start.3 = (f32[4]{0:T(128)S(1)}, f32[4]{0:T(128)S(1)}, u32[]{:S(2)}, u32[]{:S(2)}) collective-permute-start(f32[4]{0:T(128)S(1)} %add.269), channel_id=1, source_target_pairs={{0,2},{1,3},{2,0},{3,1},{4,6},{5,7},{6,4},{7,5},{8,10},{9,11},{10,... | collective-permute-start | bytes 56 | tf_op jit(solution)/shard_map/ppermute | solution.py:595
  54.2 4.6 %collective-permute-start.4 = (f32[4]{0:T(128)S(1)}, f32[4]{0:T(128)S(1)}, u32[]{:S(2)}, u32[]{:S(2)}) collective-permute-start(f32[4]{0:T(128)S(1)} %add.271), channel_id=1, source_target_pairs={{0,4},{1,5},{2,6},{3,7},{4,0},{5,1},{6,2},{7,3},{8,12},{9,13},{10,... | collective-permute-start | bytes 56 | tf_op jit(solution)/shard_map/ppermute | solution.py:595
  61.6 5.0 %collective-permute-start.5 = (f32[4,8,64]{2,1,0:T(8,128)}, f32[4,8,64]{2,1,0:T(8,128)S(1)}, u32[]{:S(2)}, u32[]{:S(2)}) collective-permute-start(f32[4,8,64]{2,1,0:T(8,128)} %shard_map.257), channel_id=1, source_target_pairs={{0,1},{1,0},{2,3},{3,2},{4,5},{5,4},{6,7},{7,6},{8,9},{9,8},{10,11... | collective-permute-start | bytes 24584 | tf_op jit(solution)/shard_map/ppermute | solution.py:595
  62.5 4.1 %copy-start.15 = (f32[4,8,64]{2,1,0:T(8,128)S(1)}, f32[4,8,64]{2,1,0:T(8,128)}, u32[]{:S(2)}) copy-start(f32[4,8,64]{2,1,0:T(8,128)} %shard_map.257) | copy-start | bytes 24580
  66.6 3.8 %collective-permute-start.6 = (f32[4,8,64]{2,1,0:T(8,128)S(1)}, f32[4,8,64]{2,1,0:T(8,128)S(1)}, u32[]{:S(2)}, u32[]{:S(2)}) collective-permute-start(f32[4,8,64]{2,1,0:T(8,128)S(1)} %add.274), channel_id=1, source_target_pairs={{0,2},{1,3},{2,0},{3,1},{4,6},{5,7},{6,4},{7,5},{8,10},{9,11},{10,... | collective-permute-start | bytes 24584 | tf_op jit(solution)/shard_map/ppermute | solution.py:595
  70.4 4.6 %collective-permute-start.7 = (f32[4,8,64]{2,1,0:T(8,128)S(1)}, f32[4,8,64]{2,1,0:T(8,128)S(1)}, u32[]{:S(2)}, u32[]{:S(2)}) collective-permute-start(f32[4,8,64]{2,1,0:T(8,128)S(1)} %add.276), channel_id=1, source_target_pairs={{0,4},{1,5},{2,6},{3,7},{4,0},{5,1},{6,2},{7,3},{8,12},{9,13},{10,... | collective-permute-start | bytes 24584 | tf_op jit(solution)/shard_map/ppermute | solution.py:595
  110.6 6.4 %collective-permute-start.9 = (bf16[1280,512]{1,0:T(8,128)(2,1)}, bf16[1280,512]{1,0:T(8,128)(2,1)S(1)}, u32[]{:S(2)}, u32[]{:S(2)}) collective-permute-start(bf16[1280,512]{1,0:T(8,128)(2,1)} %get-tuple-element.94), channel_id=1, source_target_pairs={{0,8},{1,9},{2,10},{3,11},{4,12},{5,13},{6,14},{7,15},{8,0},{9,1},... | collective-permute-start | bytes 3932168 | tf_op jit(solution)/shard_map/ppermute | solution.py:638
  110.7 4.7 %collective-permute-start.8 = (bf16[1024,512]{1,0:T(8,128)(2,1)}, bf16[1024,512]{1,0:T(8,128)(2,1)S(1)}, u32[]{:S(2)}, u32[]{:S(2)}) collective-permute-start(bf16[1024,512]{1,0:T(8,128)(2,1)} %get-tuple-element.92), channel_id=1, source_target_pairs={{0,8},{1,9},{2,10},{3,11},{4,12},{5,13},{6,14},{7,15},{8,0},{9,1},... | collective-permute-start | bytes 3145736 | tf_op jit(solution)/shard_map/ppermute | solution.py:638
  111.2 8.5 %collective-permute-start.10 = (bf16[128,512]{1,0:T(8,128)(2,1)S(1)}, bf16[128,512]{1,0:T(8,128)(2,1)S(1)}, u32[]{:S(2)}, u32[]{:S(2)}) collective-permute-start(bf16[128,512]{1,0:T(8,128)(2,1)S(1)} %dynamic-slice_convert_fusion), channel_id=1, source_target_pairs={{0,1},{1,0},{2,3},{3,2},{4,5},{5,4},{6,7},{7,6},{8,9},{9,8},{10,11... | collective-permute-start | bytes 393224 | tf_op jit(solution)/shard_map/ppermute | solution.py:893
  115.4 2.6 %copy-start.4 = (bf16[1280,512]{1,0:T(8,128)(2,1)S(1)}, bf16[1280,512]{1,0:T(8,128)(2,1)}, u32[]{:S(2)}) copy-start(bf16[1280,512]{1,0:T(8,128)(2,1)} %get-tuple-element.93) | copy-start | bytes 3932164
  117.0 1.1 copy-start.6
  119.8 24.1 %copy-start.13 = (bf16[128,512]{1,0:T(8,128)(2,1)}, bf16[128,512]{1,0:T(8,128)(2,1)S(1)}, u32[]{:S(2)}) copy-start(bf16[128,512]{1,0:T(8,128)(2,1)S(1)} %collective-permute-done.10) | copy-start | bytes 393220
  119.8 23.3 %collective-permute-start.12 = (bf16[640,512]{1,0:T(8,128)(2,1)S(1)}, bf16[640,512]{1,0:T(8,128)(2,1)S(1)}, u32[]{:S(2)}, u32[]{:S(2)}) collective-permute-start(bf16[640,512]{1,0:T(8,128)(2,1)S(1)} %get-tuple-element.105), channel_id=1, source_target_pairs={{0,1},{1,0},{2,3},{3,2},{4,5},{5,4},{6,7},{7,6},{8,10},{9,11},{10,... | collective-permute-start | bytes 1966088 | tf_op jit(solution)/shard_map/ppermute | solution.py:638
  120.9 22.2 %collective-permute-start.11 = (bf16[512,512]{1,0:T(8,128)(2,1)S(1)}, bf16[512,512]{1,0:T(8,128)(2,1)S(1)}, u32[]{:S(2)}, u32[]{:S(2)}) collective-permute-start(bf16[512,512]{1,0:T(8,128)(2,1)S(1)} %get-tuple-element.104), channel_id=1, source_target_pairs={{0,16},{1,17},{2,18},{3,19},{4,20},{5,21},{6,22},{7,23},{8,9},{9,8... | collective-permute-start | bytes 1572872 | tf_op jit(solution)/shard_map/ppermute | solution.py:638
  122.4 21.5 %copy-start.3 = (f32[4,64,512]{2,1,0:T(8,128)S(1)}, f32[4,64,512]{2,1,0:T(8,128)}, u32[]{:S(2)}) copy-start(f32[4,64,512]{2,1,0:T(8,128)} %shard_map.258) | copy-start | bytes 1572868
  143.1 0.8 copy-start.11
  143.9 2.3 collective-permute-start.13
  143.9 3.3 %copy-start.9 = (bf16[512,512]{1,0:T(8,128)(2,1)S(1)}, bf16[512,512]{1,0:T(8,128)(2,1)}, u32[]{:S(2)}) copy-start(bf16[512,512]{1,0:T(8,128)(2,1)} %get-tuple-element.108) | copy-start | bytes 1572868
  147.4 2.2 copy-start.12
  147.6 2.8 %copy-start.14 = (f32[8,512]{1,0:T(8,128)S(1)}, f32[8,512]{1,0:T(8,128)}, u32[]{:S(2)}) copy-start(f32[8,512]{1,0:T(8,128)} %get-tuple-element.102.vectors) | copy-start | bytes 49156
  147.6 8.8 %collective-permute-start.15 = (bf16[320,512]{1,0:T(8,128)(2,1)S(1)}, bf16[320,512]{1,0:T(8,128)(2,1)S(1)}, u32[]{:S(2)}, u32[]{:S(2)}) collective-permute-start(bf16[320,512]{1,0:T(8,128)(2,1)S(1)} %get-tuple-element.150), channel_id=1, source_target_pairs={{0,2},{1,3},{2,0},{3,1},{4,6},{5,7},{6,4},{7,5},{8,9},{9,8},{10,11... | collective-permute-start | bytes 983048 | tf_op jit(solution)/shard_map/ppermute | solution.py:638
  149.8 7.0 %collective-permute-start.14 = (bf16[256,512]{1,0:T(8,128)(2,1)S(1)}, bf16[256,512]{1,0:T(8,128)(2,1)S(1)}, u32[]{:S(2)}, u32[]{:S(2)}) collective-permute-start(bf16[256,512]{1,0:T(8,128)(2,1)S(1)} %get-tuple-element.151), channel_id=1, source_target_pairs={{0,1},{1,0},{2,3},{3,2},{4,5},{5,4},{6,7},{7,6},{8,24},{9,25},{10,... | collective-permute-start | bytes 786440 | tf_op jit(solution)/shard_map/ppermute | solution.py:638
  151.2 8.5 %collective-permute-start.24 = (bf16[272,512]{1,0:T(8,128)(2,1)S(1)}, bf16[272,512]{1,0:T(8,128)(2,1)S(1)}, u32[]{:S(2)}, u32[]{:S(2)}) collective-permute-start(bf16[272,512]{1,0:T(8,128)(2,1)S(1)} %pad_maximum_fusion), channel_id=1, source_target_pairs={{0,1},{1,0},{2,3},{3,2},{4,5},{5,4},{6,7},{7,6},{8,10},{9,11},{10,... | collective-permute-start | bytes 835592 | tf_op jit(solution)/shard_map/ppermute | solution.py:638
  159.8 5.4 %collective-permute-start.17 = (bf16[160,512]{1,0:T(8,128)(2,1)S(1)}, bf16[160,512]{1,0:T(8,128)(2,1)S(1)}, u32[]{:S(2)}, u32[]{:S(2)}) collective-permute-start(bf16[160,512]{1,0:T(8,128)(2,1)S(1)} %get-tuple-element.156), channel_id=1, source_target_pairs={{0,16},{1,17},{2,18},{3,19},{4,20},{5,21},{6,22},{7,23},{8,24},{9,... | collective-permute-start | bytes 491528 | tf_op jit(solution)/shard_map/ppermute | solution.py:638
  161.2 7.0 %collective-permute-start.16 = (bf16[192,512]{1,0:T(8,128)(2,1)S(1)}, bf16[192,512]{1,0:T(8,128)(2,1)S(1)}, u32[]{:S(2)}, u32[]{:S(2)}) collective-permute-start(bf16[192,512]{1,0:T(8,128)(2,1)S(1)} %pad_maximum_fusion.1), channel_id=1, source_target_pairs={{0,2},{1,3},{2,0},{3,1},{4,6},{5,7},{6,4},{7,5},{8,10},{9,11},{10,... | collective-permute-start | bytes 589832 | tf_op jit(solution)/shard_map/ppermute | solution.py:638
  162.5 7.0 %collective-permute-start.25 = (bf16[144,512]{1,0:T(8,128)(2,1)S(1)}, bf16[144,512]{1,0:T(8,128)(2,1)S(1)}, u32[]{:S(2)}, u32[]{:S(2)}) collective-permute-start(bf16[144,512]{1,0:T(8,128)(2,1)S(1)} %pad_maximum_fusion.3), channel_id=1, source_target_pairs={{0,2},{1,3},{2,0},{3,1},{4,6},{5,7},{6,4},{7,5},{8,9},{9,8},{10,11... | collective-permute-start | bytes 442376 | tf_op jit(solution)/shard_map/ppermute | solution.py:638
  165.2 8.5 %collective-permute-start.19 = (bf16[80,512]{1,0:T(8,128)(2,1)S(1)}, bf16[80,512]{1,0:T(8,128)(2,1)S(1)}, u32[]{:S(2)}, u32[]{:S(2)}) collective-permute-start(bf16[80,512]{1,0:T(8,128)(2,1)S(1)} %add_convert_fusion.12), channel_id=1, source_target_pairs={{0,4},{1,5},{2,6},{3,7},{4,0},{5,1},{6,2},{7,3},{8,12},{9,13},{10,... | collective-permute-start | bytes 245768 | tf_op jit(solution)/shard_map/ppermute | solution.py:638
  169.5 15.4 %collective-permute-start.26 = (bf16[144,512]{1,0:T(8,128)(2,1)S(1)}, bf16[144,512]{1,0:T(8,128)(2,1)S(1)}, u32[]{:S(2)}, u32[]{:S(2)}) collective-permute-start(bf16[144,512]{1,0:T(8,128)(2,1)S(1)} %pad_maximum_fusion.4), channel_id=1, source_target_pairs={{0,16},{1,17},{2,18},{3,19},{4,20},{5,21},{6,22},{7,23},{8,24},{9,... | collective-permute-start | bytes 442376 | tf_op jit(solution)/shard_map/ppermute | solution.py:638
  170.3 6.3 %collective-permute-start.18 = (bf16[96,512]{1,0:T(8,128)(2,1)S(1)}, bf16[96,512]{1,0:T(8,128)(2,1)S(1)}, u32[]{:S(2)}, u32[]{:S(2)}) collective-permute-start(bf16[96,512]{1,0:T(8,128)(2,1)S(1)} %pad_maximum_fusion.6), channel_id=1, source_target_pairs={{0,4},{1,5},{2,6},{3,7},{4,0},{5,1},{6,2},{7,3},{8,12},{9,13},{10,... | collective-permute-start | bytes 294920 | tf_op jit(solution)/shard_map/ppermute | solution.py:638
  173.8 9.8 %collective-permute-start.21 = (bf16[80,512]{1,0:T(8,128)(2,1)S(1)}, bf16[80,512]{1,0:T(8,128)(2,1)S(1)}, u32[]{:S(2)}, u32[]{:S(2)}) collective-permute-start(bf16[80,512]{1,0:T(8,128)(2,1)S(1)} %get-tuple-element.142), channel_id=1, source_target_pairs={{0,4},{1,5},{2,6},{3,7},{4,0},{5,1},{6,2},{7,3},{8,12},{9,13},{10,... | collective-permute-start | bytes 245768 | tf_op jit(solution)/shard_map/ppermute | solution.py:638
  176.7 8.8 %collective-permute-start.20 = (bf16[96,512]{1,0:T(8,128)(2,1)S(1)}, bf16[96,512]{1,0:T(8,128)(2,1)S(1)}, u32[]{:S(2)}, u32[]{:S(2)}) collective-permute-start(bf16[96,512]{1,0:T(8,128)(2,1)S(1)} %pad_maximum_fusion.7), channel_id=1, source_target_pairs={{0,4},{1,5},{2,6},{3,7},{4,0},{5,1},{6,2},{7,3},{8,12},{9,13},{10,... | collective-permute-start | bytes 294920 | tf_op jit(solution)/shard_map/ppermute | solution.py:638
  183.6 9.3 %collective-permute-start.23 = (bf16[160,512]{1,0:T(8,128)(2,1)S(1)}, bf16[160,512]{1,0:T(8,128)(2,1)S(1)}, u32[]{:S(2)}, u32[]{:S(2)}) collective-permute-start(bf16[160,512]{1,0:T(8,128)(2,1)S(1)} %constant_dynamic-update-slice_fusion.9), channel_id=1, source_target_pairs={{0,16},{1,17},{2,18},{3,19},{4,20},{5,21},{6,22},{7,23},{8,24},{9,... | collective-permute-start | bytes 491528 | tf_op jit(solution)/shard_map/ppermute | solution.py:638
  185.0 7.8 %collective-permute-start.27 = (bf16[144,512]{1,0:T(8,128)(2,1)S(1)}, bf16[144,512]{1,0:T(8,128)(2,1)S(1)}, u32[]{:S(2)}, u32[]{:S(2)}) collective-permute-start(bf16[144,512]{1,0:T(8,128)(2,1)S(1)} %pad_maximum_fusion.5), channel_id=1, source_target_pairs={{0,4},{1,5},{2,6},{3,7},{4,0},{5,1},{6,2},{7,3},{8,12},{9,13},{10,... | collective-permute-start | bytes 442376 | tf_op jit(solution)/shard_map/ppermute | solution.py:638
  185.6 8.0 %collective-permute-start.22 = (bf16[192,512]{1,0:T(8,128)(2,1)S(1)}, bf16[192,512]{1,0:T(8,128)(2,1)S(1)}, u32[]{:S(2)}, u32[]{:S(2)}) collective-permute-start(bf16[192,512]{1,0:T(8,128)(2,1)S(1)} %pad_maximum_fusion.2), channel_id=1, source_target_pairs={{0,2},{1,3},{2,0},{3,1},{4,6},{5,7},{6,4},{7,5},{8,10},{9,11},{10,... | collective-permute-start | bytes 589832 | tf_op jit(solution)/shard_map/ppermute | solution.py:638
  192.9 10.7 %collective-permute-start.31 = (bf16[320,512]{1,0:T(8,128)(2,1)S(1)}, bf16[320,512]{1,0:T(8,128)(2,1)S(1)}, u32[]{:S(2)}, u32[]{:S(2)}) collective-permute-start(bf16[320,512]{1,0:T(8,128)(2,1)S(1)} %constant_dynamic-update-slice_fusion.5), channel_id=1, source_target_pairs={{0,2},{1,3},{2,0},{3,1},{4,6},{5,7},{6,4},{7,5},{8,9},{9,8},{10,11... | collective-permute-start | bytes 983048 | tf_op jit(solution)/shard_map/ppermute | solution.py:638
  193.6 10.8 %collective-permute-start.30 = (bf16[256,512]{1,0:T(8,128)(2,1)S(1)}, bf16[256,512]{1,0:T(8,128)(2,1)S(1)}, u32[]{:S(2)}, u32[]{:S(2)}) collective-permute-start(bf16[256,512]{1,0:T(8,128)(2,1)S(1)} %slice_dynamic-update-slice_fusion), channel_id=1, source_target_pairs={{0,1},{1,0},{2,3},{3,2},{4,5},{5,4},{6,7},{7,6},{8,24},{9,25},{10,... | collective-permute-start | bytes 786440 | tf_op jit(solution)/shard_map/ppermute | solution.py:638
  194.6 11.8 %collective-permute-start.28 = (bf16[128,512]{1,0:T(8,128)(2,1)S(1)}, bf16[128,512]{1,0:T(8,128)(2,1)S(1)}, u32[]{:S(2)}, u32[]{:S(2)}) collective-permute-start(bf16[128,512]{1,0:T(8,128)(2,1)S(1)} %get-tuple-element.138), channel_id=1, source_target_pairs={{0,2},{1,3},{2,0},{3,1},{4,6},{5,7},{6,4},{7,5},{8,9},{9,8},{10,11... | collective-permute-start | bytes 393224 | tf_op jit(solution)/shard_map/ppermute | solution.py:638
  203.6 10.7 %collective-permute-start.34 = (bf16[640,512]{1,0:T(8,128)(2,1)S(1)}, bf16[640,512]{1,0:T(8,128)(2,1)S(1)}, u32[]{:S(2)}, u32[]{:S(2)}) collective-permute-start(bf16[640,512]{1,0:T(8,128)(2,1)S(1)} %constant_dynamic-update-slice_fusion.17), channel_id=1, source_target_pairs={{0,1},{1,0},{2,3},{3,2},{4,5},{5,4},{6,7},{7,6},{8,10},{9,11},{10,... | collective-permute-start | bytes 1966088 | tf_op jit(solution)/shard_map/ppermute | solution.py:638
  204.4 10.1 %collective-permute-start.33 = (bf16[512,512]{1,0:T(8,128)(2,1)S(1)}, bf16[512,512]{1,0:T(8,128)(2,1)S(1)}, u32[]{:S(2)}, u32[]{:S(2)}) collective-permute-start(bf16[512,512]{1,0:T(8,128)(2,1)S(1)} %constant_dynamic-update-slice_fusion.14), channel_id=1, source_target_pairs={{0,16},{1,17},{2,18},{3,19},{4,20},{5,21},{6,22},{7,23},{8,9},{9,8... | collective-permute-start | bytes 1572872 | tf_op jit(solution)/shard_map/ppermute | solution.py:638
  205.4 13.1 %collective-permute-start.32 = (bf16[128,512]{1,0:T(8,128)(2,1)S(1)}, bf16[128,512]{1,0:T(8,128)(2,1)S(1)}, u32[]{:S(2)}, u32[]{:S(2)}) collective-permute-start(bf16[128,512]{1,0:T(8,128)(2,1)S(1)} %slice_dynamic-update-slice_fusion.1), channel_id=1, source_target_pairs={{0,1},{1,0},{2,3},{3,2},{4,5},{5,4},{6,7},{7,6},{8,9},{9,8},{10,11... | collective-permute-start | bytes 393224 | tf_op jit(solution)/shard_map/ppermute | solution.py:980
  206.4 12.1 %collective-permute-start.29 = (bf16[256,512]{1,0:T(8,128)(2,1)S(1)}, bf16[256,512]{1,0:T(8,128)(2,1)S(1)}, u32[]{:S(2)}, u32[]{:S(2)}) collective-permute-start(bf16[256,512]{1,0:T(8,128)(2,1)S(1)} %constant_dynamic-update-slice_fusion.11), channel_id=1, source_target_pairs={{0,1},{1,0},{2,3},{3,2},{4,5},{5,4},{6,7},{7,6},{8,10},{9,11},{10,... | collective-permute-start | bytes 786440 | tf_op jit(solution)/shard_map/ppermute | solution.py:638
  214.3 1.1 copy-start
  214.3 6.2 %collective-permute-start.36 = (bf16[1280,512]{1,0:T(8,128)(2,1)S(1)}, bf16[1280,512]{1,0:T(8,128)(2,1)S(1)}, u32[]{:S(2)}, u32[]{:S(2)}) collective-permute-start(bf16[1280,512]{1,0:T(8,128)(2,1)S(1)} %constant_dynamic-update-slice_fusion.16.refs_2_), channel_id=1, source_target_pairs={{0,8},{1,9},{2,10},{3,11},{4,12},{5,13},{6,14},{7,15},{8,0},{9,1},... | collective-permute-start | bytes 3932168 | tf_op jit(solution)/shard_map/ppermute | solution.py:638
  215.4 5.1 %copy-start.1 = (bf16[1024,512]{1,0:T(8,128)(2,1)}, bf16[1024,512]{1,0:T(8,128)(2,1)S(1)}, u32[]{:S(2)}) copy-start(bf16[1024,512]{1,0:T(8,128)(2,1)S(1)} %constant_dynamic-update-slice_fusion.21.refs_0_) | copy-start | bytes 3145732
  215.4 5.1 %collective-permute-start.35 = (bf16[1024,512]{1,0:T(8,128)(2,1)S(1)}, bf16[1024,512]{1,0:T(8,128)(2,1)S(1)}, u32[]{:S(2)}, u32[]{:S(2)}) collective-permute-start(bf16[1024,512]{1,0:T(8,128)(2,1)S(1)} %constant_dynamic-update-slice_fusion.21.refs_0_), channel_id=1, source_target_pairs={{0,8},{1,9},{2,10},{3,11},{4,12},{5,13},{6,14},{7,15},{8,0},{9,1},... | collective-permute-start | bytes 3145736 | tf_op jit(solution)/shard_map/ppermute | solution.py:638
  218.5 2.0 copy-start.2
  218.5 2.0 collective-permute-start.37
  219.9 0.7 copy-start.8
  220.5 0.8 copy-start.10
  220.5 1.2 copy-start.7
  220.5 1.6 copy-start.5
